TPU v7x, 32 devices: a whole 2x2x4 slice. The times are simulated.
32 devices in a mesh: segment: 4 (over y, x), seq: 8 (over z, core).
Axes of the slice: x: 2, y: 2, z: 4, core: 2. Of those that a mesh axis runs over, the one named last changes fastest.
Arguments:
- held: bfloat16 [4, 1024, 1024], P('segment', 'seq'), may hold values from -6 to 6
- log_decay: float32 [4, 1024, 8], P('segment', 'seq'), may hold values from -2 to 0, as said below
- route_ids: int32 [4, 8, 1], P('segment'), may hold values from 0 to 7; in each aligned block of 8 rows (0 to 7, 8 to 15, ..., all dimensions but the last counted through in order) at most 2 rows name the same one
- norm_gain: float32 [4, 1024], P('segment'), may hold values from 0.1 to 1.9
- qkv_weight: bfloat16 [4, 1024, 3072], P('segment'), may hold values from -0.1875 to 0.1875
- beta_weight: bfloat16 [4, 1024, 8], P('segment'), may hold values from -0.1875 to 0.1875
- out_gain: float32 [4, 128], P('segment'), may hold values from 0.1 to 1.9
- out_weight: bfloat16 [4, 1024, 1024], P('segment'), may hold values from -0.1875 to 0.1875
- ffn_gain: float32 [4, 1024], P('segment'), may hold values from 0.1 to 1.9
- gate_weight: bfloat16 [4, 8, 1024, 4096], P('segment', 'seq'), may hold values from -0.1875 to 0.1875
- up_weight: bfloat16 [4, 8, 1024, 4096], P('segment', 'seq'), may hold values from -0.1875 to 0.1875
- down_weight: bfloat16 [4, 8, 4096, 1024], P('segment', 'seq'), may hold values from -0.09375 to 0.09375
Outputs:
- next_held: bfloat16 [4, 1024, 1024], P('segment', 'seq')
Inputs may be any that keep to these rules, and one draw needn't show every extreme that they name: `log_decay`: every entry is negative. `route_ids`: within each aligned group of 8 consecutive blocks of a section no machine type is named more than 2 times, and in some group of every draw one type is named exactly 2 times.
All inputs are finite; a program needn't handle non-finite values.
Results may differ from a plain program's by a relative error of at most 0.018.
Values may be sent and summed in bfloat16 or wider, within the bound.
No kernel may reach another device: no remote copies, remote signals or barrier semaphores. Data moves between devices by JAX's collectives and lax.ppermute only.
A program may use at most 192 MiB of HBM per device.

v0:
```python
from functools import partial

import jax
import jax.numpy as jnp
from jax import lax
from jax.sharding import PartitionSpec as P

EXPERTS = 8
BLOCK = 128


def swapped(block, axis, distance):
    count = lax.axis_size(axis)
    route = []
    for low in range(count):
        high = low | 1 << distance
        if high != low and high < count:
            route += [(low, high), (high, low)]
    return lax.ppermute(block, axis, route)


def carried_in(shard, axis, join, neutral):
    place = lax.axis_index(axis)
    gathered = jax.tree.map(
        lambda a, kind: lax.all_gather(a.astype(kind), axis),
        shard,
        jax.tree.map(lambda a: jnp.bfloat16 if a.dtype == jnp.float32 else a.dtype, shard),
    )
    state = jax.tree.map(lambda a, e: jnp.zeros_like(a) + jnp.asarray(e, a.dtype), shard, neutral)

    def one(hop, state):
        return join(
            state,
            jax.tree.map(
                lambda a, own: lax.dynamic_index_in_dim(a, hop, 0, False).astype(own.dtype),
                gathered,
                shard,
            ),
        )

    return lax.fori_loop(0, place, one, state)


def from_behind(shard, axis, by):
    peers = lax.axis_size(axis)
    return lax.ppermute(shard, axis, [(i, (i + by) % peers) for i in range(peers)])


def rms(values, gain):
    return values * lax.rsqrt(jnp.mean(values * values, axis=-1, keepdims=True) + 1e-06) * gain


def unit_lower_solve(strict_part, rhs):
    ein = partial(jnp.einsum, precision=lax.Precision.HIGHEST)
    length = strict_part.shape[-1]
    raised = -strict_part
    running = jnp.eye(length, dtype=jnp.float32) + raised
    for _ in range((length - 1).bit_length() - 1):
        raised = ein("hij,hjk->hik", raised, raised)
        running = running + ein("hij,hjk->hik", running, raised)
    return ein("hij,hjk->hik", running, rhs)


def span_terms(lookup_vectors, values, beta, logd):
    ein = partial(jnp.einsum, precision=lax.Precision.HIGHEST)
    length = lookup_vectors.shape[1]
    dim_k = lookup_vectors.shape[2]
    cumul = jnp.cumsum(logd, axis=-1)
    posit = jnp.arange(length)
    strict = posit[:, None] > posit[None, :]
    differ = cumul[:, :, None] - cumul[:, None, :]
    ratio = jnp.where(strict, jnp.exp(jnp.where(strict, differ, 0.0)), 0.0)
    inner = ein("htd,hsd->hts", lookup_vectors, lookup_vectors)
    strict_part = beta[:, :, None] * ratio * inner
    growth = jnp.exp(cumul)
    rhs = jnp.concatenate(
        [(beta * growth)[:, :, None] * lookup_vectors, beta[:, :, None] * values], axis=-1
    )
    solved = unit_lower_solve(strict_part, rhs)
    w_part = solved[..., :dim_k]
    u_part = solved[..., dim_k:]
    tail = jnp.exp(cumul[:, -1:] - cumul)
    scaled = tail[:, :, None] * lookup_vectors
    trans_a = growth[:, -1][:, None, None] * jnp.eye(dim_k, dtype=jnp.float32) - ein(
        "hck,hcj->hkj", w_part, scaled
    )
    trans_b = ein("hcv,hck->hvk", u_part, scaled)
    return (cumul, w_part, u_part, trans_a, trans_b)


def span_output(queries, lookup_vectors, cumul, w_part, u_part, state):
    ein = partial(jnp.einsum, precision=lax.Precision.HIGHEST)
    length = lookup_vectors.shape[1]
    posit = jnp.arange(length)
    incl = posit[:, None] >= posit[None, :]
    differ = cumul[:, :, None] - cumul[:, None, :]
    ratio = jnp.where(incl, jnp.exp(jnp.where(incl, differ, 0.0)), 0.0)
    update = u_part - ein("hck,hvk->hcv", w_part, state)
    scores = ein("htd,hsd->hts", queries, lookup_vectors) * ratio
    return jnp.exp(cumul)[:, :, None] * ein("hck,hvk->hcv", queries, state) + ein(
        "hts,hsv->htv", scores, update
    )


def compose(earlier, later):
    ein = partial(jnp.einsum, precision=lax.Precision.HIGHEST)
    return (
        ein("hij,hjk->hik", earlier[0], later[0]),
        ein("hvk,hkj->hvj", earlier[1], later[0]) + later[1],
    )


def group_gather(piece, place):
    for bit in range(EXPERTS.bit_length() - 1):
        other = swapped(piece, "seq", bit)
        upper = place >> bit & 1
        piece = jnp.where(
            upper == 1,
            jnp.concatenate([other, piece], axis=0),
            jnp.concatenate([piece, other], axis=0),
        )
    return piece


def slice_gather(piece, place, low_bits, high_bits):
    for bit in range(high_bits):
        other = swapped(piece, "seq", low_bits + bit)
        upper = place >> low_bits + bit & 1
        piece = jnp.where(
            upper == 1,
            jnp.concatenate([other, piece], axis=0),
            jnp.concatenate([piece, other], axis=0),
        )
    return piece


def per_device(
    held,
    log_decay,
    route_ids,
    norm_gain,
    qkv_weight,
    beta_weight,
    out_gain,
    out_weight,
    ffn_gain,
    gate_weight,
    up_weight,
    down_weight,
):
    x_rows = held[0]
    steps_dev = x_rows.shape[0]
    width = x_rows.shape[1]
    heads = log_decay.shape[2]
    head_dim = width // heads
    xf = x_rows.astype(jnp.float32)
    xn = rms(xf, norm_gain[0]).astype(jnp.bfloat16)
    qkv = (
        jnp.dot(xn, qkv_weight[0], preferred_element_type=jnp.float32)
        .astype(jnp.bfloat16)
        .astype(jnp.float32)
    )
    queries = qkv[:, :width].reshape(steps_dev, heads, head_dim)
    lookup_vectors = qkv[:, width : 2 * width].reshape(steps_dev, heads, head_dim)
    values = qkv[:, 2 * width :].reshape(steps_dev, heads, head_dim)
    queries = queries * lax.rsqrt(jnp.sum(queries * queries, axis=-1, keepdims=True) + 1e-06)
    lookup_vectors = lookup_vectors * lax.rsqrt(
        jnp.sum(lookup_vectors * lookup_vectors, axis=-1, keepdims=True) + 1e-06
    )
    beta = jax.nn.sigmoid(jnp.dot(xn, beta_weight[0], preferred_element_type=jnp.float32))
    spans = steps_dev // BLOCK

    def arrange(arr):
        return arr.reshape(spans, BLOCK, heads, head_dim).transpose(0, 2, 1, 3)

    q_c = arrange(queries)
    k_c = arrange(lookup_vectors)
    v_c = arrange(values)
    b_c = beta.reshape(spans, BLOCK, heads).transpose(0, 2, 1)
    l_c = log_decay[0].reshape(spans, BLOCK, heads).transpose(0, 2, 1)
    terms = span_terms(k_c[0], v_c[0], b_c[0], l_c[0])
    total_pair = (terms[3], terms[4])
    identity = (
        jnp.broadcast_to(jnp.eye(head_dim, dtype=jnp.float32), (heads, head_dim, head_dim)),
        jnp.zeros((heads, head_dim, head_dim), jnp.float32),
    )
    prefix = carried_in(total_pair, "seq", compose, identity)
    state = prefix[1]
    cumul, w_part, u_part, trans_a, trans_b = terms
    results = [span_output(q_c[0], k_c[0], cumul, w_part, u_part, state)]
    mixed = jnp.stack(results, axis=0).transpose(0, 2, 1, 3).reshape(steps_dev, heads, head_dim)
    normed = rms(mixed, out_gain[0]).astype(jnp.bfloat16).reshape(steps_dev, width)
    hidden = (xf + jnp.dot(normed, out_weight[0], preferred_element_type=jnp.float32)).astype(
        jnp.bfloat16
    )
    hn = rms(hidden.astype(jnp.float32), ffn_gain[0]).astype(jnp.bfloat16)
    place = lax.axis_index("seq")
    low_bits = EXPERTS.bit_length() - 1
    high_bits = lax.axis_size("seq").bit_length() - 1 - low_bits
    own_kind = place % EXPERTS
    group = place // EXPERTS
    blocks_dev = steps_dev // BLOCK
    group_size = EXPERTS * blocks_dev
    capacity = 2 * blocks_dev
    kinds = route_ids[0, :, 0]
    group_kinds = lax.dynamic_slice_in_dim(kinds, group * group_size, group_size)
    index_g = jnp.arange(group_size)
    same = group_kinds[:, None] == group_kinds[None, :]
    before = index_g[None, :] < index_g[:, None]
    rank_all = jnp.sum((same & before).astype(jnp.int32), axis=1)
    slot_ids = jnp.arange(capacity)
    select = ((group_kinds[None, :] == own_kind) & (rank_all[None, :] == slot_ids[:, None])).astype(
        jnp.bfloat16
    )
    grouped = group_gather(hn.reshape(blocks_dev, BLOCK, width), place)
    picked = jnp.einsum("cb,brd->crd", select, grouped, preferred_element_type=jnp.float32).astype(
        jnp.bfloat16
    )
    spread = slice_gather(picked, place, low_bits, high_bits)
    rows = spread.reshape(-1, width)
    gate = jnp.dot(rows, gate_weight[0, 0], preferred_element_type=jnp.float32)
    up_val = jnp.dot(rows, up_weight[0, 0], preferred_element_type=jnp.float32)
    act = (jax.nn.silu(gate) * up_val).astype(jnp.bfloat16)
    partial_sum = jnp.dot(act, down_weight[0, 0], preferred_element_type=jnp.float32)
    buffer = partial_sum.reshape(-1, capacity * BLOCK, width)
    for bit in reversed(range(high_bits)):
        half = buffer.shape[0] // 2
        lower_half = buffer[:half]
        upper_half = buffer[half:]
        upper = group >> bit & 1
        keep = jnp.where(upper == 1, upper_half, lower_half)
        send = jnp.where(upper == 1, lower_half, upper_half)
        buffer = keep + swapped(send.astype(jnp.bfloat16), "seq", low_bits + bit).astype(send.dtype)
    finished = buffer[0].astype(jnp.bfloat16).reshape(capacity, BLOCK, width)
    returned = group_gather(finished, place)
    mine = own_kind * blocks_dev + jnp.arange(blocks_dev)
    target = jnp.take(group_kinds, mine) * capacity + jnp.take(rank_all, mine)
    choose = (jnp.arange(EXPERTS * capacity)[None, :] == target[:, None]).astype(jnp.bfloat16)
    ffn = (
        jnp.einsum("ib,brd->ird", choose, returned, preferred_element_type=jnp.float32)
        .astype(jnp.bfloat16)
        .reshape(steps_dev, width)
    )
    result = (hidden.astype(jnp.float32) + ffn.astype(jnp.float32)).astype(jnp.bfloat16)
    moved = from_behind(result, "segment", 1)
    return moved[None]


def solution(mesh):
    placed = (
        P("segment", "seq", None),
        P("segment", "seq", None),
        P("segment", None, None),
        P("segment", None),
        P("segment", None, None),
        P("segment", None, None),
        P("segment", None),
        P("segment", None, None),
        P("segment", None),
        P("segment", "seq", None, None),
        P("segment", "seq", None, None),
        P("segment", "seq", None, None),
    )
    return jax.shard_map(
        per_device, mesh=mesh, in_specs=placed, out_specs=P("segment", "seq", None), check_vma=False
    )
```

profile of v0, /device:TPU:0, one launch (start us, length us, event | category | flops | bytes accessed | tf_op | source)
XLA Modules:
  0.0 344.9 jit_solution(16591647072271702418)
XLA Ops:
  6.6 1.2 fusion.61
  9.0 1.2 fusion.105
  10.4 4.0 %fusion.23 = f32[128,3072]{1,0:T(8,128)S(1)} fusion(bf16[1,1024,3072]{2,1,0:T(8,128)(2,1)} %param.18, bf16[1,128,1024]{2,1,0:T(8,128)(2,1)} %param.14, f32[1024]{0:T(1024)} %bitcast.206, f32[128]{0:T(128)S(1)} %add_rsqrt_fusion.4), kind=kOutput, calls=%fused_computation.20 | convolution fusion | flops 806617088 | bytes 8131072 | tf_op jit(solution)/shard_map/dot_general | solution.py:159
  14.4 1.2 multiply_bitcast_fusion.1
  16.0 1.2 copy.127
  17.2 1.4 fusion.41
  26.8 1.2 fusion.56
  29.0 2.0 fusion.45
  31.1 3.1 convolution_convert_fusion
  37.6 2.2 convolution_multiply_fusion
  39.7 23.3 %all-gather.5.cloned.1.call-done = bf16[64,128,128]{2,1,0:T(8,128)(2,1)} async-done(((bf16[8,128,128]{2,1,0:T(8,128)(2,1)}), bf16[64,128,128]{2,1,0:T(8,128)(2,1)}) %all-gather.5.cloned.1.call-update) | async-done | bytes 2097168 | tf_op jit(solution)/shard_map/all_gather | solution.py:25
  63.0 30.2 %all-gather.7.cloned.1.call-done = bf16[64,128,128]{2,1,0:T(8,128)(2,1)} async-done(((bf16[8,128,128]{2,1,0:T(8,128)(2,1)}), bf16[64,128,128]{2,1,0:T(8,128)(2,1)}) %all-gather.7.cloned.1.call-update) | async-done | bytes 2097168 | tf_op jit(solution)/shard_map/all_gather | solution.py:25
  93.3 1.9 convolution_subtract_fusion
  95.2 2.3 convolution_multiply_fusion.1
  97.5 2.1 multiply_reduce_fusion.1
  100.4 2.9 collective-permute-start
  103.3 1.2 collective-permute-done
  104.6 6.8 %collective-permute-start.1 = (bf16[2,128,1024]{2,1,0:T(8,128)(2,1)S(1)}, bf16[2,128,1024]{2,1,0:T(8,128)(2,1)S(1)}, u32[]{:S(2)}, u32[]{:S(2)}) collective-permute-start(bf16[2,128,1024]{2,1,0:T(8,128)(2,1)S(1)} %maximum_select_fusion.5), channel_id=1, source_target_pairs={{0,2},{2,0},{1,3},{3,1},{4,6},{6,4},{5,7},{7,5},{8,10},{10,8},{9,1... | collective-permute-start | bytes 1572872 | tf_op jit(solution)/shard_map/ppermute | solution.py:19
  111.4 12.4 %collective-permute-done.1 = bf16[2,128,1024]{2,1,0:T(8,128)(2,1)S(1)} collective-permute-done((bf16[2,128,1024]{2,1,0:T(8,128)(2,1)S(1)}, bf16[2,128,1024]{2,1,0:T(8,128)(2,1)S(1)}, u32[]{:S(2)}, u32[]{:S(2)}) %collective-permute-start.1) | collective-permute-done | bytes 524320 | tf_op jit(solution)/shard_map/ppermute | solution.py:19
  124.0 11.6 %collective-permute-start.2 = (bf16[4,128,1024]{2,1,0:T(8,128)(2,1)S(1)}, bf16[4,128,1024]{2,1,0:T(8,128)(2,1)}, u32[]{:S(2)}, u32[]{:S(2)}) collective-permute-start(bf16[4,128,1024]{2,1,0:T(8,128)(2,1)S(1)} %maximum_select_fusion.3), channel_id=1, source_target_pairs={{0,4},{4,0},{1,5},{5,1},{2,6},{6,2},{3,7},{7,3},{8,12},{12,8},{9,1... | collective-permute-start | bytes 3145736 | tf_op jit(solution)/shard_map/ppermute | solution.py:19
  135.9 45.5 %collective-permute-done.2 = bf16[4,128,1024]{2,1,0:T(8,128)(2,1)} collective-permute-done((bf16[4,128,1024]{2,1,0:T(8,128)(2,1)S(1)}, bf16[4,128,1024]{2,1,0:T(8,128)(2,1)}, u32[]{:S(2)}, u32[]{:S(2)}) %collective-permute-start.2) | collective-permute-done | bytes 1048608 | tf_op jit(solution)/shard_map/ppermute | solution.py:19
  181.4 2.6 maximum_select_fusion.1
  183.9 1.4 fusion.32
  185.5 7.7 %fusion.8 = f32[256,4096]{1,0:T(8,128)} fusion(bf16[256,1024]{1,0:T(8,128)(2,1)S(1)} %bitcast.202, bf16[1,1,1024,4096]{3,2,1,0:T(8,128)(2,1)} %param.23), kind=kOutput, calls=%fused_computation.10 | convolution fusion | flops 2147483648 | bytes 13107200 | tf_op jit(solution)/shard_map/dot_general | solution.py:221
  193.1 11.9 %fusion.35 = bf16[256,1024]{1,0:T(8,128)(2,1)S(1)} fusion(bf16[1,1,4096,1024]{3,2,1,0:T(8,128)(2,1)} %param.25, bf16[256,1024]{1,0:T(8,128)(2,1)S(1)} %bitcast.203, bf16[1,1,1024,4096]{3,2,1,0:T(8,128)(2,1)} %param.24, f32[256,4096]{1,0:T(8,128)} %fusion.8), kind=kOutput, calls=%fused_computation.34 | convolution fusion | flops 4301520896 | bytes 22020096 | tf_op jit(solution)/shard_map/dot_general | solution.py:224
  205.1 1.9 collective-permute-done.3
  208.0 24.6 %collective-permute-done.4 = bf16[4,128,1024]{2,1,0:T(8,128)(2,1)S(1)} collective-permute-done((bf16[4,128,1024]{2,1,0:T(8,128)(2,1)S(1)}, bf16[4,128,1024]{2,1,0:T(8,128)(2,1)S(1)}, u32[]{:S(2)}, u32[]{:S(2)}) %collective-permute-start.4) | collective-permute-done | bytes 1048608 | tf_op jit(solution)/shard_map/ppermute | solution.py:19
  233.0 2.4 collective-permute-start.5
  237.9 87.8 %collective-permute-done.5 = bf16[8,128,1024]{2,1,0:T(8,128)(2,1)S(1)} collective-permute-done((bf16[8,128,1024]{2,1,0:T(8,128)(2,1)S(1)}, bf16[8,128,1024]{2,1,0:T(8,128)(2,1)S(1)}, u32[]{:S(2)}, u32[]{:S(2)}) %collective-permute-start.5) | collective-permute-done | bytes 2097184 | tf_op jit(solution)/shard_map/ppermute | solution.py:19
  326.4 2.5 fusion.18
  329.1 1.5 collective-permute-start.6
  330.6 6.8 %collective-permute-done.6 = bf16[128,1024]{1,0:T(8,128)(2,1)S(1)} collective-permute-done((bf16[128,1024]{1,0:T(8,128)(2,1)S(1)}, bf16[128,1024]{1,0:T(8,128)(2,1)S(1)}, u32[]{:S(2)}, u32[]{:S(2)}) %collective-permute-start.6) | collective-permute-done | bytes 262176 | tf_op jit(solution)/shard_map/ppermute | solution.py:46
  (73 shorter events, 19.9 us)
Async XLA Ops:
  6.5 93.1 %copy-start = (bf16[1,1024,1024]{2,1,0:T(8,128)(2,1)S(1)}, bf16[1,1024,1024]{2,1,0:T(8,128)(2,1)}, u32[]{:S(2)}) copy-start(bf16[1,1024,1024]{2,1,0:T(8,128)(2,1)} %param.21) | copy-start | bytes 6291460
  6.5 56.5 %all-gather.5.cloned.1.call-start = ((), (), s32[]{:S(2)}) async-start(), calls=%async_computation | async-start | bytes 2359296 | tf_op jit(solution)/shard_map/all_gather | solution.py:25
  28.0 1.0 copy-start.2
  31.0 62.2 %all-gather.7.cloned.1.call-start = ((), (), s32[]{:S(2)}) async-start(), calls=%async_computation.1 | async-start | bytes 2359296 | tf_op jit(solution)/shard_map/all_gather | solution.py:25
  36.7 0.8 copy-start.3
  93.3 6.3 %copy-start.7 = (f32[1,128]{1,0:T(1,128)S(1)}, f32[1,128]{1,0:T(1,128)}, u32[]{:S(2)}) copy-start(f32[1,128]{1,0:T(1,128)} %param.20) | copy-start | bytes 1540
  93.3 6.4 %copy-start.5 = (bf16[1,128,1024]{2,1,0:T(8,128)(2,1)S(1)}, bf16[1,128,1024]{2,1,0:T(8,128)(2,1)}, u32[]{:S(2)}) copy-start(bf16[1,128,1024]{2,1,0:T(8,128)(2,1)} %param.14) | copy-start | bytes 786436
  95.2 5.1 %copy-start.6 = (f32[1,1024]{1,0:T(1,128)S(1)}, f32[1,1024]{1,0:T(1,128)}, u32[]{:S(2)}) copy-start(f32[1,1024]{1,0:T(1,128)} %param.22) | copy-start | bytes 12292
  99.5 36.2 %copy-start.8 = (s32[1,8,1]{1,2,0:T(1,128)S(1)}, s32[1,8,1]{1,2,0:T(1,128)}, u32[]{:S(2)}) copy-start(s32[1,8,1]{1,2,0:T(1,128)} %param.16) | copy-start | bytes 100
  100.4 4.1 %collective-permute-start = (bf16[1,128,1024]{2,1,0:T(8,128)(2,1)S(1)}, bf16[1,128,1024]{2,1,0:T(8,128)(2,1)S(1)}, u32[]{:S(2)}, u32[]{:S(2)}) collective-permute-start(bf16[1,128,1024]{2,1,0:T(8,128)(2,1)S(1)} %fusion.77), channel_id=1, source_target_pairs={{0,1},{1,0},{2,3},{3,2},{4,5},{5,4},{6,7},{7,6},{8,9},{9,8},{10,11... | collective-permute-start | bytes 786440 | tf_op jit(solution)/shard_map/ppermute | solution.py:19
  104.6 19.3 %collective-permute-start.1 = (bf16[2,128,1024]{2,1,0:T(8,128)(2,1)S(1)}, bf16[2,128,1024]{2,1,0:T(8,128)(2,1)S(1)}, u32[]{:S(2)}, u32[]{:S(2)}) collective-permute-start(bf16[2,128,1024]{2,1,0:T(8,128)(2,1)S(1)} %maximum_select_fusion.5), channel_id=1, source_target_pairs={{0,2},{2,0},{1,3},{3,1},{4,6},{6,4},{5,7},{7,5},{8,10},{10,8},{9,1... | collective-permute-start | bytes 1572872 | tf_op jit(solution)/shard_map/ppermute | solution.py:19
  124.0 11.8 %copy-start.4 = (bf16[4,128,1024]{2,1,0:T(8,128)(2,1)}, bf16[4,128,1024]{2,1,0:T(8,128)(2,1)S(1)}, u32[]{:S(2)}) copy-start(bf16[4,128,1024]{2,1,0:T(8,128)(2,1)S(1)} %maximum_select_fusion.3) | copy-start | bytes 3145732
  124.0 57.3 %collective-permute-start.2 = (bf16[4,128,1024]{2,1,0:T(8,128)(2,1)S(1)}, bf16[4,128,1024]{2,1,0:T(8,128)(2,1)}, u32[]{:S(2)}, u32[]{:S(2)}) collective-permute-start(bf16[4,128,1024]{2,1,0:T(8,128)(2,1)S(1)} %maximum_select_fusion.3), channel_id=1, source_target_pairs={{0,4},{4,0},{1,5},{5,1},{2,6},{6,2},{3,7},{7,3},{8,12},{12,8},{9,1... | collective-permute-start | bytes 3145736 | tf_op jit(solution)/shard_map/ppermute | solution.py:19
  205.0 2.0 collective-permute-start.3
  207.4 25.3 %collective-permute-start.4 = (bf16[4,128,1024]{2,1,0:T(8,128)(2,1)S(1)}, bf16[4,128,1024]{2,1,0:T(8,128)(2,1)S(1)}, u32[]{:S(2)}, u32[]{:S(2)}) collective-permute-start(bf16[4,128,1024]{2,1,0:T(8,128)(2,1)S(1)} %maximum_select_fusion.4), channel_id=1, source_target_pairs={{0,2},{2,0},{1,3},{3,1},{4,6},{6,4},{5,7},{7,5},{8,10},{10,8},{9,1... | collective-permute-start | bytes 3145736 | tf_op jit(solution)/shard_map/ppermute | solution.py:19
  233.0 92.8 %collective-permute-start.5 = (bf16[8,128,1024]{2,1,0:T(8,128)(2,1)S(1)}, bf16[8,128,1024]{2,1,0:T(8,128)(2,1)S(1)}, u32[]{:S(2)}, u32[]{:S(2)}) collective-permute-start(bf16[8,128,1024]{2,1,0:T(8,128)(2,1)S(1)} %maximum_select_fusion.2), channel_id=1, source_target_pairs={{0,4},{4,0},{1,5},{5,1},{2,6},{6,2},{3,7},{7,3},{8,12},{12,8},{9,1... | collective-permute-start | bytes 6291464 | tf_op jit(solution)/shard_map/ppermute | solution.py:19
  325.7 12.3 %copy-start.1 = (bf16[1,1024,1024]{2,1,0:T(8,128)(2,1)S(1)}, bf16[1,1024,1024]{2,1,0:T(8,128)(2,1)}, u32[]{:S(2)}) copy-start(bf16[1,1024,1024]{2,1,0:T(8,128)(2,1)} %param.21) | copy-start | bytes 6291460
  329.1 8.3 %collective-permute-start.6 = (bf16[128,1024]{1,0:T(8,128)(2,1)S(1)}, bf16[128,1024]{1,0:T(8,128)(2,1)S(1)}, u32[]{:S(2)}, u32[]{:S(2)}) collective-permute-start(bf16[128,1024]{1,0:T(8,128)(2,1)S(1)} %add_convert_fusion), channel_id=1, source_target_pairs={{0,8},{8,16},{16,24},{24,0},{1,9},{9,17},{17,25},{25,1},{2,10},{10... | collective-permute-start | bytes 786440 | tf_op jit(solution)/shard_map/ppermute | solution.py:46
Sparse Core Ops, SparseCore 0:
  31.2 31.7 all-gather.4
  64.6 28.5 all-gather.6
where the time goes:
time: 346 us; the launch traced here: 345 us
  waiting for transfers between devices  234 us (68%)
  matrix products  52.9 us (15%)
  starting transfers between devices  26.1 us (8%)
  between operations  15.1 us (4%)
  other arithmetic  9.1 us (3%)
  local copies, waits for them, and re-layouts  7.99 us (2%)
    ppermute x6, waiting for transfers between devices, swapped(): return lax.ppermute(block, axis, route)  173 us
    all_gather x2, waiting for transfers between devices, carried_in(): lax.all_gather(a.astype(kind), axis)  53.5 us
    ppermute x6, starting transfers between devices, swapped(): return lax.ppermute(block, axis, route)  24.6 us
    dot_general x1, matrix products, per_device(): jnp.dot(act, down_weight[0, 0], preferred_element_type=jnp.float32)  11.9 us
    dot_general x1, matrix products, per_device(): gate = jnp.dot(rows, gate_weight[0, 0], preferred_element_type=jnp.float32)  7.65 us
  transfers between devices with their start and end apart: 9, of which 9 were waited for; matrix products, arithmetic and copies ran while one was open for 3% of the time, Pallas kernels for 0%

commit v1 on v0

v1 whole, which is shorter than its diff:
```python
from functools import partial

import jax
import jax.numpy as jnp
from jax import lax
from jax.experimental import pallas as pl
from jax.experimental.pallas import tpu as pltpu
from jax.sharding import PartitionSpec as P

EXPERTS = 8
BLOCK = 128
CHIPS = 4
CORES = 2
CAP = 2
F32 = jnp.float32
BF16 = jnp.bfloat16
VMEM_LIMIT = 56 * 1024 * 1024


def lane_route(count, hop):
    route = []
    for i in range(count):
        base, chip, core = i - i % EXPERTS, i % EXPERTS // CORES, i % CORES
        route.append((i, base + (chip + hop) % CHIPS * CORES + core))
    return route


def pair_route(count):
    return [(i, i ^ 1) for i in range(count)]


def chip_route(count, k):
    return [(i, i ^ (CORES * k)) for i in range(count)]


def home_route(sections, count, k):
    return [
        (s * count + i, (s + 1) % sections * count + (i ^ (CORES * k)))
        for s in range(sections)
        for i in range(count)
    ]


def mm(a, b, dims=((1,), (0,))):
    return lax.dot_general(a, b, (dims, ((), ())), preferred_element_type=F32)


def halves(a):
    high = a.astype(BF16)
    return high, (a - high.astype(F32)).astype(BF16)


def mm3(a, b):
    (ah, al), (bh, bl) = a, b
    return mm(ah, bh) + (mm(ah, bl) + mm(al, bh))


def place_iota():
    row = lax.broadcasted_iota(jnp.int32, (BLOCK, BLOCK), 0)
    col = lax.broadcasted_iota(jnp.int32, (BLOCK, BLOCK), 1)
    return row, col


def lower_inverse(negs):
    row, col = place_iota()
    eye = jnp.where(row == col, 1.0, 0.0).astype(F32)
    small = 16
    near = row // small == col // small
    diag = [jnp.where(near, n, 0.0) for n in negs]
    total = [eye + d for d in diag]
    power = [halves(d) for d in diag]
    for _ in range((small - 1).bit_length() - 1):
        power = [halves(mm3(p, p)) for p in power]
        total = [t + mm3(halves(t), p) for t, p in zip(total, power)]
    size = small
    while size < BLOCK:
        off = (row // (2 * size) == col // (2 * size)) & (row // size != col // size)
        cross = [halves(jnp.where(off, n, 0.0)) for n in negs]
        split = [halves(t) for t in total]
        left = [halves(mm3(t, c)) for t, c in zip(split, cross)]
        total = [t + mm3(m, s) for t, m, s in zip(total, left, split)]
        size *= 2
    return total


def unit(v):
    return v * lax.rsqrt(jnp.sum(v * v, axis=-1, keepdims=True) + 1e-06)


def running_decay(logd_ref, cum_ref):
    row, col = place_iota()
    upto = jnp.where(row <= col, 1.0, 0.0).astype(BF16)
    rest = logd_ref[...]
    total = jnp.zeros_like(rest)
    for _ in range(3):
        part = rest.astype(BF16)
        total = total + mm(part, upto)
        rest = rest - part.astype(F32)
    cum_ref[...] = total


def block_terms(projs, cums):
    row, col = place_iota()
    hd = BLOCK
    q = [unit(p[:, :hd].astype(BF16).astype(F32)) for p in projs]
    k = [unit(p[:, hd : 2 * hd].astype(BF16).astype(F32)) for p in projs]
    v = [p[:, 2 * hd : 3 * hd].astype(BF16).astype(F32) for p in projs]
    beta = [jax.nn.sigmoid(p[:, 3 * hd :]) for p in projs]
    across = [jnp.broadcast_to(c, (BLOCK, BLOCK)) for c in cums]
    down = [jnp.transpose(a) for a in across]
    kb = [a.astype(BF16) for a in k]
    inner = [
        mm(jnp.concatenate([a.astype(BF16), b], axis=0), b, ((1,), (1,))) for a, b in zip(q, kb)
    ]
    ratio = [
        jnp.where(row >= col, jnp.exp(jnp.where(row >= col, d - a, 0.0)), 0.0)
        for d, a in zip(down, across)
    ]
    negs = [
        jnp.where(row > col, -(b * r * i[BLOCK:]), 0.0) for b, r, i in zip(beta, ratio, inner)
    ]
    growth = [jnp.exp(d) for d in down]
    rhs = [
        jnp.concatenate([b * g * a, b * c], axis=1) for b, g, a, c in zip(beta, growth, k, v)
    ]
    inv = lower_inverse(negs)
    solved = [mm3(halves(t), halves(r)).astype(BF16) for t, r in zip(inv, rhs)]
    scores = [(i[:BLOCK] * r).astype(BF16) for i, r in zip(inner, ratio)]
    inside = [mm(s, w) for s, w in zip(scores, solved)]
    last = [d[BLOCK - 1 :, :] for d in down]
    tail = [(jnp.exp(e - d) * a).astype(BF16) for e, d, a in zip(last, down, k)]
    step = [mm(w, t, ((0,), (0,))) for w, t in zip(solved, tail)]
    fade = [jnp.exp(e) for e in last]
    reads = [g * a - i[:, :hd] for g, a, i in zip(growth, q, inside)]
    local = [i[:, hd:] for i in inside]
    return reads, local, step, fade


def arrivals(place):
    chip, core = place // CORES % CHIPS, place % CORES
    return [
        (chip + hop) % CHIPS * CORES + (core if side == 0 else 1 - core)
        for hop in (0, 3, 1, 2)
        for side in (0, 1)
    ]


def terms_kernel(first, count, meta_ref, logd_ref, gain_ref, weight_ref, *refs):
    x_refs = refs[:count]
    reads_ref, local_ref, step_ref, fade_ref, cum_ref, norm_ref = refs[count:]
    running_decay(logd_ref, cum_ref)
    blocks = arrivals(meta_ref[0])[first : first + count]
    gain = gain_ref[...]
    for j in range(count):
        xf = x_refs[j][...].astype(F32)
        scale = lax.rsqrt(jnp.mean(xf * xf, axis=-1, keepdims=True) + 1e-06)
        norm_ref[j * BLOCK : (j + 1) * BLOCK, :] = (xf * scale * gain).astype(BF16)
    for j in range(0, count, 2):
        both = mm(norm_ref[j * BLOCK : (j + 2) * BLOCK, :], weight_ref[...])
        reads, local, step, fade = block_terms(
            [both[:BLOCK], both[BLOCK:]], [cum_ref[pl.ds(blocks[i], 1), :] for i in (j, j + 1)]
        )
        for i in range(2):
            reads_ref[j + i] = reads[i].astype(BF16)
            local_ref[j + i] = local[i]
            step_ref[j + i] = step[i]
            fade_ref[j + i] = jnp.broadcast_to(fade[i], (8, BLOCK))


def terms(first, meta, logd, gain, weight, blocks):
    count = len(blocks)
    width = blocks[0].shape[1]
    vmem = pl.BlockSpec(memory_space=pltpu.VMEM)
    return pl.pallas_call(
        partial(terms_kernel, first, count),
        out_shape=(
            jax.ShapeDtypeStruct((count, BLOCK, BLOCK), BF16),
            jax.ShapeDtypeStruct((count, BLOCK, BLOCK), F32),
            jax.ShapeDtypeStruct((count, 2 * BLOCK, BLOCK), F32),
            jax.ShapeDtypeStruct((count, 8, BLOCK), F32),
        ),
        in_specs=[pl.BlockSpec(memory_space=pltpu.SMEM)] + [vmem] * (3 + count),
        out_specs=(vmem,) * 4,
        scratch_shapes=[
            pltpu.VMEM((EXPERTS, BLOCK), F32),
            pltpu.VMEM((count * BLOCK, width), BF16),
        ],
        compiler_params=pltpu.CompilerParams(vmem_limit_bytes=VMEM_LIMIT),
        cost_estimate=pl.CostEstimate(
            flops=count * 2 * BLOCK * (width * 512 + 60 * BLOCK * BLOCK),
            bytes_accessed=count * 800000 + 2000000,
            transcendentals=count * 60000,
        ),
        name="chunk_terms",
    )(meta, logd, gain, weight, *blocks)


def mix_kernel(early, late, meta_ref, start_ref, gain_ref, *refs):
    first = refs[:4]
    second = refs[4:8]
    outs = refs[8 : 8 + CHIPS]
    reads_scr, local_scr, step_scr, fade_scr, on_scr = refs[8 + CHIPS :]
    place = meta_ref[0]
    blocks = arrivals(place)
    for group, at, count in ((first, 0, early), (second, early, late)):
        for j in range(count):
            spot = blocks[at + j]
            for ref, scr in zip(group, (reads_scr, local_scr, step_scr, fade_scr)):
                scr[spot] = ref[j]
    state = start_ref[...]
    gain = gain_ref[...]
    for b in range(EXPERTS):
        split = halves(state)
        move = step_scr[b]
        mixed = mm(reads_scr[b], split[0], ((1,), (1,))) + local_scr[b]
        scale = lax.rsqrt(jnp.mean(mixed * mixed, axis=-1, keepdims=True) + 1e-06)
        on_scr[b] = (mixed * scale * gain).astype(BF16)
        if b + 1 < EXPERTS:
            erase = mm3(split, halves(move[:BLOCK]))
            state = fade_scr[b][0:1, :] * state - erase + move[BLOCK:]
    chip = place // CORES % CHIPS
    for k in range(CHIPS):
        there = jnp.bitwise_xor(chip, k)
        for side in range(CORES):
            for slot in range(CAP):
                source = meta_ref[1 + (there * CORES + side) * CAP + slot]
                outs[k][side, slot] = on_scr[source]


def mix(meta, start, gain, first, second):
    early, late = first[0].shape[0], second[0].shape[0]
    vmem = pl.BlockSpec(memory_space=pltpu.VMEM)
    sent = jax.ShapeDtypeStruct((CORES, CAP, BLOCK, BLOCK), BF16)
    return pl.pallas_call(
        partial(mix_kernel, early, late),
        out_shape=(sent,) * CHIPS,
        in_specs=[pl.BlockSpec(memory_space=pltpu.SMEM)] + [vmem] * 10,
        out_specs=(vmem,) * CHIPS,
        scratch_shapes=[
            pltpu.VMEM((EXPERTS, BLOCK, BLOCK), BF16),
            pltpu.VMEM((EXPERTS, BLOCK, BLOCK), F32),
            pltpu.VMEM((EXPERTS, 2 * BLOCK, BLOCK), F32),
            pltpu.VMEM((EXPERTS, 8, BLOCK), F32),
            pltpu.VMEM((EXPERTS, BLOCK, BLOCK), BF16),
        ],
        compiler_params=pltpu.CompilerParams(vmem_limit_bytes=VMEM_LIMIT),
        name="state_walk",
    )(meta, start, gain, *first, *second)


def project(meta_ref, gain_ref, out_weight_ref, x_ref, on_refs, on_scr, h_ref, hn_ref):
    place = meta_ref[0]
    chip, core = place // CORES % CHIPS, place % CORES
    for k in range(CHIPS):
        there = jnp.bitwise_xor(chip, k)
        for side in range(CORES):
            head = there * CORES + (core if side == 0 else 1 - core)
            at = pl.ds(pl.multiple_of(head * BLOCK, BLOCK), BLOCK)
            got = on_refs[k * CORES + side]
            for slot in range(CAP):
                on_scr[slot * BLOCK : (slot + 1) * BLOCK, at] = got[core, slot]
    hidden = x_ref[...].astype(F32) + mm(on_scr[...], out_weight_ref[...])
    hidden = hidden.astype(BF16)
    h_ref[...] = hidden
    hf = hidden.astype(F32)
    scale = lax.rsqrt(jnp.mean(hf * hf, axis=-1, keepdims=True) + 1e-06)
    hn_ref[...] = (hf * scale * gain_ref[...]).astype(BF16)


def project_kernel(meta_ref, gain_ref, out_weight_ref, x_ref, *refs):
    on_refs = refs[: CHIPS * CORES]
    h_ref, hn_ref, on_scr = refs[CHIPS * CORES :]
    project(meta_ref, gain_ref, out_weight_ref, x_ref, on_refs, on_scr, h_ref, hn_ref)


def expert_kernel(meta_ref, gain_ref, out_weight_ref, x_ref, gate_ref, up_ref, down_ref, *refs):
    on_refs = refs[: CHIPS * CORES]
    out_ref, on_scr, h_scr, hn_scr, sum_scr = refs[CHIPS * CORES :]
    at = pl.program_id(0)

    @pl.when(at == 0)
    def _():
        project(meta_ref, gain_ref, out_weight_ref, x_ref, on_refs, on_scr, h_scr, hn_scr)
        sum_scr[...] = jnp.zeros_like(sum_scr)

    rows = hn_scr[...]
    gate = mm(rows, gate_ref[0, 0])
    up = mm(rows, up_ref[0, 0])
    act = (gate / (1.0 + jnp.exp(-gate)) * up).astype(BF16)
    sum_scr[...] += mm(act, down_ref[0, 0])

    @pl.when(at == pl.num_programs(0) - 1)
    def _():
        ffn = sum_scr[...].astype(BF16).astype(F32)
        out_ref[...] = (h_scr[...].astype(F32) + ffn).astype(BF16)


def expert(meta, gain, out_weight, x_rows, gate, up, down, ons):
    rows, width = x_rows.shape
    hidden = gate.shape[3]
    tile = min(512, hidden)
    vmem = pl.BlockSpec(memory_space=pltpu.VMEM)
    return pl.pallas_call(
        expert_kernel,
        out_shape=jax.ShapeDtypeStruct((rows, width), BF16),
        grid=(hidden // tile,),
        in_specs=[pl.BlockSpec(memory_space=pltpu.SMEM), vmem, vmem, vmem]
        + [pl.BlockSpec((1, 1, width, tile), lambda i: (0, 0, 0, i))] * 2
        + [pl.BlockSpec((1, 1, tile, width), lambda i: (0, 0, i, 0))]
        + [vmem] * len(ons),
        out_specs=vmem,
        scratch_shapes=[
            pltpu.VMEM((rows, width), BF16),
            pltpu.VMEM((rows, width), BF16),
            pltpu.VMEM((rows, width), BF16),
            pltpu.VMEM((rows, width), F32),
        ],
        compiler_params=pltpu.CompilerParams(vmem_limit_bytes=VMEM_LIMIT),
        name="expert",
    )(meta, gain, out_weight, x_rows, gate, up, down, *ons)


def project_only(meta, gain, out_weight, x_rows, ons):
    rows, width = x_rows.shape
    vmem = pl.BlockSpec(memory_space=pltpu.VMEM)
    return pl.pallas_call(
        project_kernel,
        out_shape=(jax.ShapeDtypeStruct((rows, width), BF16),) * 2,
        in_specs=[pl.BlockSpec(memory_space=pltpu.SMEM)] + [vmem] * (3 + len(ons)),
        out_specs=(vmem, vmem),
        scratch_shapes=[pltpu.VMEM((rows, width), BF16)],
        compiler_params=pltpu.CompilerParams(vmem_limit_bytes=VMEM_LIMIT),
        name="project",
    )(meta, gain, out_weight, x_rows, *ons)


def group_start(place, count, first, second):
    groups = count // EXPERTS
    ein = partial(jnp.einsum, precision=lax.Precision.HIGHEST)
    eye = jnp.eye(BLOCK, dtype=F32)
    step = jnp.concatenate([first[2], second[2]], axis=0)
    fade = jnp.concatenate([first[3], second[3]], axis=0)
    order = jnp.argsort(jnp.stack(arrivals(place)))
    step, fade = jnp.take(step, order, axis=0), jnp.take(fade, order, axis=0)
    moves = fade[:, 0, :][:, None, :] * eye - step[:, :BLOCK]
    adds = step[:, BLOCK:]
    total, added = moves[0], adds[0]
    for b in range(1, EXPERTS):
        total, added = ein("ij,jk->ik", total, moves[b]), ein("vk,kj->vj", added, moves[b]) + adds[b]
    peers = [[g * EXPERTS + e for g in range(groups)] for e in range(EXPERTS)]
    gather = partial(lax.all_gather, axis_name="seq", axis_index_groups=peers)
    totals, addeds = gather(total), gather(added)

    def one(hop, state):
        return ein(
            "vk,kj->vj", state, lax.dynamic_index_in_dim(totals, hop, 0, False)
        ) + lax.dynamic_index_in_dim(addeds, hop, 0, False)

    return lax.fori_loop(0, place // EXPERTS, one, jnp.zeros((BLOCK, BLOCK), F32))


def per_device(
    held,
    log_decay,
    route_ids,
    norm_gain,
    qkv_weight,
    beta_weight,
    out_gain,
    out_weight,
    ffn_gain,
    gate_weight,
    up_weight,
    down_weight,
):
    count = lax.axis_size("seq")
    sections = lax.axis_size("segment")
    groups = count // EXPERTS
    place = lax.axis_index("seq")
    group, inner = place // EXPERTS, place % EXPERTS
    chip, core = inner // CORES, inner % CORES
    width = held.shape[2]
    pair = partial(lax.ppermute, axis_name="seq", perm=pair_route(count))

    def hop(block, by):
        return lax.ppermute(block, "seq", lane_route(count, by))

    own = held[0]
    left = hop(own, 1)
    right = hop(own, -1)
    far = hop(left, 1)
    near = [own, pair(own), left, pair(left), right, pair(right)]
    distant = [far, pair(far)]

    members = [[g * EXPERTS + e for e in range(EXPERTS)] for g in range(groups)]
    decays = lax.all_gather(
        log_decay[0].T, "seq", axis_index_groups=members if groups > 1 else None
    )
    decays = lax.dynamic_index_in_dim(decays, inner, 1, False)

    def head_columns(at):
        return lax.dynamic_slice_in_dim(qkv_weight[0], at * width + inner * BLOCK, BLOCK, 1)

    beta_column = lax.dynamic_slice_in_dim(beta_weight[0], inner, 1, 1)
    weight = jnp.concatenate(
        [head_columns(0), head_columns(1), head_columns(2)]
        + [jnp.broadcast_to(beta_column, (width, BLOCK))],
        axis=1,
    )

    kinds = lax.dynamic_slice_in_dim(route_ids[0, :, 0], group * EXPERTS, EXPERTS)
    index = jnp.arange(EXPERTS)
    same = kinds[:, None] == kinds[None, :]
    rank = jnp.sum((same & (index[None, :] < index[:, None])).astype(jnp.int32), axis=1)
    named = (kinds[None, None, :] == index[:, None, None]) & (
        rank[None, None, :] == jnp.arange(CAP)[None, :, None]
    )
    source = jnp.sum(jnp.where(named, index[None, None, :], 0), axis=2).astype(jnp.int32)
    meta = jnp.concatenate([place.astype(jnp.int32)[None], source.reshape(-1)])

    first = terms(0, meta, decays, norm_gain, weight, near)
    second = terms(6, meta, decays, norm_gain, weight, distant)
    if groups > 1:
        start = group_start(place, count, first, second)
    else:
        start = jnp.zeros((BLOCK, BLOCK), F32)
    sends = mix(meta, start, out_gain, first, second)

    got = [sends[0]] + [lax.ppermute(sends[k], "seq", chip_route(count, k)) for k in range(1, CHIPS)]
    ons = []
    for block in got:
        ons += [block, pair(block)]

    stacked = jnp.stack(near + distant, axis=0)
    wanted = lax.dynamic_index_in_dim(source, inner, 0, False)
    hop_index = jnp.array([0, 4, 6, 2], jnp.int32)
    came = jnp.take(hop_index, (wanted // CORES - chip) % CHIPS) + (wanted % CORES != core)
    x_rows = jnp.take(stacked, came, axis=0).reshape(CAP * BLOCK, width)

    if groups == 1:
        finished = expert(
            meta, ffn_gain, out_weight[0], x_rows, gate_weight, up_weight, down_weight, ons
        )
    else:
        hidden, hn = project_only(meta, ffn_gain, out_weight[0], x_rows, ons)
        peers = [[g * EXPERTS + e for g in range(groups)] for e in range(EXPERTS)]
        rows = lax.all_gather(hn, "seq", axis_index_groups=peers, tiled=True)
        gate = jnp.dot(rows, gate_weight[0, 0], preferred_element_type=F32)
        up = jnp.dot(rows, up_weight[0, 0], preferred_element_type=F32)
        act = (jax.nn.silu(gate) * up).astype(BF16)
        part = jnp.dot(act, down_weight[0, 0], preferred_element_type=F32)
        ffn = lax.psum_scatter(
            part, "seq", scatter_dimension=0, axis_index_groups=peers, tiled=True
        ).astype(BF16)
        finished = (hidden.astype(F32) + ffn.astype(F32)).astype(BF16)

    other = pair(finished)
    fronts = [finished[:BLOCK], finished[BLOCK:], other[:BLOCK], other[BLOCK:]]
    total = None
    for k in range(CHIPS):
        home = jnp.bitwise_xor(inner, CORES * k)
        kind = lax.dynamic_index_in_dim(kinds, home, 0, False)
        slot = lax.dynamic_index_in_dim(rank, home, 0, False)
        which = jnp.where(
            kind // CORES == chip, (kind % CORES != core).astype(jnp.int32) * CAP + slot, -1
        )
        send = jnp.zeros((BLOCK, width), BF16)
        for at, front in enumerate(fronts):
            send = jnp.where(which == at, front, send)
        moved = lax.ppermute(send, ("segment", "seq"), home_route(sections, count, k))
        total = moved if total is None else total + moved
    return total[None]


def solution(mesh):
    placed = (
        P("segment", "seq", None),
        P("segment", "seq", None),
        P("segment", None, None),
        P("segment", None),
        P("segment", None, None),
        P("segment", None, None),
        P("segment", None),
        P("segment", None, None),
        P("segment", None),
        P("segment", "seq", None, None),
        P("segment", "seq", None, None),
        P("segment", "seq", None, None),
    )
    return jax.shard_map(
        per_device, mesh=mesh, in_specs=placed, out_specs=P("segment", "seq", None), check_vma=False
    )
```

time: 346 us -> 147 us (0.42)
  waiting for transfers between devices: 234 us -> 44.7 us
  matrix products: 52.9 us -> 0 us
  Pallas kernels: 0 us -> 37.2 us
  blocking collectives: 0 us -> 16.2 us
  starting transfers between devices: 26.1 us -> 19.2 us
    ppermute x7 -> x19, waiting for transfers between devices: 180 us -> 44.7 us  [the longest x4 26.7 us: per_device(): lax.ppermute(send, ('segment', 'seq'), home_route(sections, count, k))]
    all_gather x2 -> x0, waiting for transfers between devices: 53.5 us -> none  [carried_in(): lax.all_gather(a.astype(kind), axis)]
    dot_general x27 -> x0, matrix products: 52.9 us -> none  [the longest x1 11.9 us: per_device(): jnp.dot(act, down_weight[0, 0], preferred_element_type=jnp.float32)]
    pallas_call x0 -> x4, Pallas kernels: none -> 37.2 us  [the longest x1 17 us: expert(): pl.pallas_call(expert_kernel, out_shape=jax.ShapeDtypeStruct((rows, width...]
    all_gather x0 -> x1, blocking collectives: none -> 16.2 us  [per_device(): lax.all_gather(log_decay[0].T, 'seq', axis_index_groups=members if groups...]
    ppermute x7 -> x19, starting transfers between devices: 26.1 us -> 19.2 us  [the longest x4 7.75 us: per_device(): lax.ppermute(send, ('segment', 'seq'), home_route(sections, count, k))]
  transfers between devices with their start and end apart: 9 -> 19, of which waited for: 9 -> 5; matrix products, arithmetic and copies ran while one was open for 3% -> 8% of each run, Pallas kernels for 0% -> 8%
where the time goes in v1:
time: 147 us; the launch traced here: 146 us
  waiting for transfers between devices  44.7 us (30%)
  Pallas kernels  37.2 us (25%)
  starting transfers between devices  19.2 us (13%)
  blocking collectives  16.2 us (11%)
  between operations  12.9 us (9%)
  local copies, waits for them, and re-layouts  9.5 us (6%)
  other arithmetic  6.36 us (4%)
    ppermute x4, waiting for transfers between devices, per_device(): lax.ppermute(send, ('segment', 'seq'), home_route(sections, count, k))  26.7 us
    pallas_call x1, Pallas kernels, expert(): pl.pallas_call(expert_kernel, out_shape=jax.ShapeDtypeStruct((rows, width...  17 us
    all_gather x1, blocking collectives, per_device(): lax.all_gather(log_decay[0].T, 'seq', axis_index_groups=members if groups...  16.2 us
    pallas_call x2, Pallas kernels, terms(): pl.pallas_call(partial(terms_kernel, first, count), out_shape=(jax.ShapeD...  16.2 us
    ppermute x3, waiting for transfers between devices, hop(): return lax.ppermute(block, 'seq', lane_route(count, by))  9.88 us
    ppermute x3, waiting for transfers between devices, per_device(): lax.ppermute(sends[k], 'seq', chip_route(count, k))  8.11 us
    ppermute x4, starting transfers between devices, per_device(): lax.ppermute(send, ('segment', 'seq'), home_route(sections, count, k))  7.75 us
    ppermute x3, starting transfers between devices, hop(): return lax.ppermute(block, 'seq', lane_route(count, by))  4.75 us
  transfers between devices with their start and end apart: 19, of which 5 were waited for; matrix products, arithmetic and copies ran while one was open for 8% of the time, Pallas kernels for 8%

profile of v1, /device:TPU:0, one launch (start us, length us, event | category | flops | bytes accessed | tf_op | source)
XLA Modules:
  0.0 146.1 jit_solution(17673022335101730963)
XLA Ops:
  0.5 2.6 %collective-permute-start.1 = (bf16[128,1024]{1,0:T(8,128)(2,1)}, bf16[128,1024]{1,0:T(8,128)(2,1)S(1)}, u32[]{:S(2)}, u32[]{:S(2)}) collective-permute-start(bf16[128,1024]{1,0:T(8,128)(2,1)} %bitcast.76), channel_id=1, source_target_pairs={{0,2},{1,3},{2,4},{3,5},{4,6},{5,7},{6,0},{7,1},{8,10},{9,11},{10,... | collective-permute-start | bytes 786440 | tf_op jit(solution)/shard_map/ppermute | solution.py:386
  3.1 2.1 %collective-permute-start.3 = (bf16[128,1024]{1,0:T(8,128)(2,1)}, bf16[128,1024]{1,0:T(8,128)(2,1)S(1)}, u32[]{:S(2)}, u32[]{:S(2)}) collective-permute-start(bf16[128,1024]{1,0:T(8,128)(2,1)} %bitcast.77), channel_id=1, source_target_pairs={{0,6},{1,7},{2,0},{3,1},{4,2},{5,3},{6,4},{7,5},{8,14},{9,15},{10,... | collective-permute-start | bytes 786440 | tf_op jit(solution)/shard_map/ppermute | solution.py:386
  5.2 0.9 convert_reduce_fusion
  6.1 0.7 iota_compare_fusion
  6.8 1.0 constant_dynamic-update-slice_fusion
  8.3 1.3 gather_fusion
  9.7 16.2 %all-gather = f32[64,128]{1,0:T(8,128)S(1)} all-gather(f32[8,128]{1,0:T(8,128)} %bitcast.82), channel_id=2, replica_groups=mesh['segment'=4,'seq'=8] {'seq'}, dimensions={0}, use_global_device_ids=true | all-gather | bytes 36864 | tf_op jit(solution)/shard_map/all_gather | solution.py:396
  25.9 0.6 constant_dynamic-slice_fusion.3
  26.6 1.2 dynamic-slice_bitcast_fusion.2
  28.0 1.1 pad_maximum_fusion.weight_ref
  29.1 0.6 pad_add_fusion.meta_ref
  30.4 9.9 %collective-permute-done.5.refs_0_ = bf16[128,1024]{1,0:T(8,128)(2,1)S(1)} collective-permute-done((bf16[128,1024]{1,0:T(8,128)(2,1)S(1)}, bf16[128,1024]{1,0:T(8,128)(2,1)S(1)}, u32[]{:S(2)}, u32[]{:S(2)}) %collective-permute-start.5) | collective-permute-done | bytes 262176 | tf_op jit(solution)/shard_map/ppermute | solution.py:386
  40.4 0.6 copy-done.8
  41.2 11.1 %chunk_terms.2 = (bf16[6,128,128]{2,1,0:T(8,128)(2,1)}, f32[6,128,128]{2,1,0:T(8,128)}, f32[6,256,128]{2,1,0:T(8,128)}, f32[6,8,128]{2,1,0:T(8,128)}) custom-call(s32[17]{0:T(128)} %pad_add_fusion.meta_ref, f32[8,128]{1,0:T(8,128)} %bitcast.83, f32[1,1024]{1,0:T(1,128)} %gain_ref.5, bf16[1024,512]{1,0:T(8,128)(2,1)} %pad_maximum_fusion.weight_ref, ...), custom_call_target="tpu_custom_call" | custom-call | flops 2315255808 | bytes 6800000 | tf_op jit(solution)/shard_map/chunk_terms/pallas_call | solution.py:174
  52.3 0.7 copy-done.5
  53.0 5.1 %chunk_terms.3 = (bf16[2,128,128]{2,1,0:T(8,128)(2,1)}, f32[2,128,128]{2,1,0:T(8,128)}, f32[2,256,128]{2,1,0:T(8,128)}, f32[2,8,128]{2,1,0:T(8,128)}) custom-call(s32[17]{0:T(128)} %pad_add_fusion.meta_ref, f32[8,128]{1,0:T(8,128)} %bitcast.84, f32[1,1024]{1,0:T(1,128)} %gain_ref.5, bf16[1024,512]{1,0:T(8,128)(2,1)} %pad_maximum_fusion.weight_ref, ...), custom_call_target="tpu_custom_call" | custom-call | flops 771751936 | bytes 3600000 | tf_op jit(solution)/shard_map/chunk_terms/pallas_call | solution.py:174
  58.1 0.6 broadcast_in_dim.60.start_ref
  58.7 4.0 %state_walk.1 = (bf16[2,2,128,128]{3,2,1,0:T(8,128)(2,1)}, bf16[2,2,128,128]{3,2,1,0:T(8,128)(2,1)}, bf16[2,2,128,128]{3,2,1,0:T(8,128)(2,1)}, bf16[2,2,128,128]{3,2,1,0:T(8,128)(2,1)}) custom-call(s32[17]{0:T(128)} %pad_add_fusion.meta_ref, f32[128,128]{1,0:T(8,128)} %broadcast_in_dim.60.start_ref, f32[1,128]{1,0:T(1,128)} %gain_ref.6, ...), custom_call_target="tpu_custom_call" | custom-call | tf_op jit(solution)/shard_map/state_walk/pallas_call | solution.py:234
  63.6 3.9 %collective-permute-start.12 = (bf16[2,2,128,128]{3,2,1,0:T(8,128)(2,1)}, bf16[2,2,128,128]{3,2,1,0:T(8,128)(2,1)S(1)}, u32[]{:S(2)}, u32[]{:S(2)}) collective-permute-start(bf16[2,2,128,128]{3,2,1,0:T(8,128)(2,1)} %get-tuple-element.28), channel_id=1, source_target_pairs={{0,6},{1,7},{2,4},{3,5},{4,2},{5,3},{6,0},{7,1},{8,14},{9,15},{10,... | collective-permute-start | bytes 393224 | tf_op jit(solution)/shard_map/ppermute | solution.py:429
  68.1 2.0 %collective-permute-done.8.refs_2_ = bf16[2,2,128,128]{3,2,1,0:T(8,128)(2,1)S(1)} collective-permute-done((bf16[2,2,128,128]{3,2,1,0:T(8,128)(2,1)}, bf16[2,2,128,128]{3,2,1,0:T(8,128)(2,1)S(1)}, u32[]{:S(2)}, u32[]{:S(2)}) %collective-permute-start.8) | collective-permute-done | bytes 131104 | tf_op jit(solution)/shard_map/ppermute | solution.py:429
  70.2 6.1 %collective-permute-done.10.refs_4_ = bf16[2,2,128,128]{3,2,1,0:T(8,128)(2,1)S(1)} collective-permute-done((bf16[2,2,128,128]{3,2,1,0:T(8,128)(2,1)}, bf16[2,2,128,128]{3,2,1,0:T(8,128)(2,1)S(1)}, u32[]{:S(2)}, u32[]{:S(2)}) %collective-permute-start.10) | collective-permute-done | bytes 131104 | tf_op jit(solution)/shard_map/ppermute | solution.py:429
  76.8 0.9 bitcast_select_fusion.x_ref
  78.5 17.0 %expert.1 = bf16[256,1024]{1,0:T(8,128)(2,1)} custom-call(s32[17]{0:T(128)} %pad_add_fusion.meta_ref, f32[1,1024]{1,0:T(1,128)} %gain_ref.7, bf16[1024,1024]{1,0:T(8,128)(2,1)} %bitcast.74, bf16[256,1024]{1,0:T(8,128)(2,1)} %bitcast_select_fusion.x_ref, bf16[1,1,1024,4096]{3,2,1,0:T(8,128)(2,1)} %gate_ref.1, bf16[1,1,1024,4096]{3,2,1,0:T(8,128)(2,1)} %up_ref.1, ...), custom_call_target="tpu_custom_call" | custom-call | tf_op jit(solution)/shard_map/expert/pallas_call | solution.py:303
  95.8 0.7 constant_dynamic-slice_fusion.2
  98.8 0.7 fusion.8
  109.8 1.1 select_select_fusion.3
  110.9 2.4 %collective-permute-start.18 = (bf16[128,1024]{1,0:T(8,128)(2,1)S(1)}, bf16[128,1024]{1,0:T(8,128)(2,1)S(1)}, u32[]{:S(2)}, u32[]{:S(2)}) collective-permute-start(bf16[128,1024]{1,0:T(8,128)(2,1)S(1)} %get-tuple-element.35), channel_id=1, source_target_pairs={{0,14},{1,15},{2,12},{3,13},{4,10},{5,11},{6,8},{7,9},{8,22},{9,23... | collective-permute-start | bytes 786440 | tf_op jit(solution)/shard_map/ppermute | solution.py:470
  113.4 3.3 %collective-permute-start.17 = (bf16[128,1024]{1,0:T(8,128)(2,1)S(1)}, bf16[128,1024]{1,0:T(8,128)(2,1)S(1)}, u32[]{:S(2)}, u32[]{:S(2)}) collective-permute-start(bf16[128,1024]{1,0:T(8,128)(2,1)S(1)} %get-tuple-element.33), channel_id=1, source_target_pairs={{0,12},{1,13},{2,14},{3,15},{4,8},{5,9},{6,10},{7,11},{8,20},{9,21... | collective-permute-start | bytes 786440 | tf_op jit(solution)/shard_map/ppermute | solution.py:470
  116.7 1.5 %collective-permute-start.15 = (bf16[128,1024]{1,0:T(8,128)(2,1)S(1)}, bf16[128,1024]{1,0:T(8,128)(2,1)S(1)}, u32[]{:S(2)}, u32[]{:S(2)}) collective-permute-start(bf16[128,1024]{1,0:T(8,128)(2,1)S(1)} %get-tuple-element.34), channel_id=1, source_target_pairs={{0,8},{1,9},{2,10},{3,11},{4,12},{5,13},{6,14},{7,15},{8,16},{9,17... | collective-permute-start | bytes 786440 | tf_op jit(solution)/shard_map/ppermute | solution.py:470
  118.7 5.1 %collective-permute-done.18 = bf16[128,1024]{1,0:T(8,128)(2,1)S(1)} collective-permute-done((bf16[128,1024]{1,0:T(8,128)(2,1)S(1)}, bf16[128,1024]{1,0:T(8,128)(2,1)S(1)}, u32[]{:S(2)}, u32[]{:S(2)}) %collective-permute-start.18) | collective-permute-done | bytes 262176 | tf_op jit(solution)/shard_map/ppermute | solution.py:470
  123.8 21.5 %collective-permute-done.17 = bf16[128,1024]{1,0:T(8,128)(2,1)S(1)} collective-permute-done((bf16[128,1024]{1,0:T(8,128)(2,1)S(1)}, bf16[128,1024]{1,0:T(8,128)(2,1)S(1)}, u32[]{:S(2)}, u32[]{:S(2)}) %collective-permute-start.17) | collective-permute-done | bytes 262176 | tf_op jit(solution)/shard_map/ppermute | solution.py:470
  145.4 0.8 add_bitcast_fusion
  (83 shorter events, 6.0 us)
Async XLA Ops:
  0.0 26.5 %copy-start = (bf16[1,1024,8]{1,2,0:T(8,128)(2,1)S(1)}, bf16[1,1024,8]{1,2,0:T(8,128)(2,1)}, u32[]{:S(2)}) copy-start(bf16[1,1024,8]{1,2,0:T(8,128)(2,1)} %param.18) | copy-start | bytes 49156
  0.0 30.3 %collective-permute-start = (bf16[128,1024]{1,0:T(8,128)(2,1)}, bf16[128,1024]{1,0:T(8,128)(2,1)S(1)}, u32[]{:S(2)}, u32[]{:S(2)}) collective-permute-start(bf16[128,1024]{1,0:T(8,128)(2,1)} %bitcast.75), channel_id=1, source_target_pairs={{0,1},{1,0},{2,3},{3,2},{4,5},{5,4},{6,7},{7,6},{8,9},{9,8},{10,11... | collective-permute-start | bytes 786440 | tf_op jit(solution)/shard_map/ppermute | solution.py:392
  0.5 29.3 %collective-permute-start.1 = (bf16[128,1024]{1,0:T(8,128)(2,1)}, bf16[128,1024]{1,0:T(8,128)(2,1)S(1)}, u32[]{:S(2)}, u32[]{:S(2)}) collective-permute-start(bf16[128,1024]{1,0:T(8,128)(2,1)} %bitcast.76), channel_id=1, source_target_pairs={{0,2},{1,3},{2,4},{3,5},{4,6},{5,7},{6,0},{7,1},{8,10},{9,11},{10,... | collective-permute-start | bytes 786440 | tf_op jit(solution)/shard_map/ppermute | solution.py:386
  3.1 27.0 %collective-permute-start.3 = (bf16[128,1024]{1,0:T(8,128)(2,1)}, bf16[128,1024]{1,0:T(8,128)(2,1)S(1)}, u32[]{:S(2)}, u32[]{:S(2)}) collective-permute-start(bf16[128,1024]{1,0:T(8,128)(2,1)} %bitcast.77), channel_id=1, source_target_pairs={{0,6},{1,7},{2,0},{3,1},{4,2},{5,3},{6,4},{7,5},{8,14},{9,15},{10,... | collective-permute-start | bytes 786440 | tf_op jit(solution)/shard_map/ppermute | solution.py:386
  29.7 10.7 %copy-start.3 = (bf16[128,1024]{1,0:T(8,128)(2,1)}, bf16[128,1024]{1,0:T(8,128)(2,1)S(1)}, u32[]{:S(2)}) copy-start(bf16[128,1024]{1,0:T(8,128)(2,1)S(1)} %collective-permute-done.1.refs_2_) | copy-start | bytes 786436
  29.7 10.5 %collective-permute-start.2 = (bf16[128,1024]{1,0:T(8,128)(2,1)S(1)}, bf16[128,1024]{1,0:T(8,128)(2,1)S(1)}, u32[]{:S(2)}, u32[]{:S(2)}) collective-permute-start(bf16[128,1024]{1,0:T(8,128)(2,1)S(1)} %collective-permute-done.1.refs_2_), channel_id=1, source_target_pairs={{0,1},{1,0},{2,3},{3,2},{4,5},{5,4},{6,7},{7,6},{8,9},{9,8},{10,11... | collective-permute-start | bytes 786440 | tf_op jit(solution)/shard_map/ppermute | solution.py:392
  30.1 10.2 %collective-permute-start.5 = (bf16[128,1024]{1,0:T(8,128)(2,1)S(1)}, bf16[128,1024]{1,0:T(8,128)(2,1)S(1)}, u32[]{:S(2)}, u32[]{:S(2)}) collective-permute-start(bf16[128,1024]{1,0:T(8,128)(2,1)S(1)} %collective-permute-done.1.refs_2_), channel_id=1, source_target_pairs={{0,2},{1,3},{2,4},{3,5},{4,6},{5,7},{6,0},{7,1},{8,10},{9,11},{10,... | collective-permute-start | bytes 786440 | tf_op jit(solution)/shard_map/ppermute | solution.py:386
  30.1 10.3 %copy-start.4 = (bf16[128,1024]{1,0:T(8,128)(2,1)}, bf16[128,1024]{1,0:T(8,128)(2,1)S(1)}, u32[]{:S(2)}) copy-start(bf16[128,1024]{1,0:T(8,128)(2,1)S(1)} %collective-permute-done.3.refs_4_) | copy-start | bytes 786436
  30.1 10.3 %collective-permute-start.4 = (bf16[128,1024]{1,0:T(8,128)(2,1)S(1)}, bf16[128,1024]{1,0:T(8,128)(2,1)S(1)}, u32[]{:S(2)}, u32[]{:S(2)}) collective-permute-start(bf16[128,1024]{1,0:T(8,128)(2,1)S(1)} %collective-permute-done.3.refs_4_), channel_id=1, source_target_pairs={{0,1},{1,0},{2,3},{3,2},{4,5},{5,4},{6,7},{7,6},{8,9},{9,8},{10,11... | collective-permute-start | bytes 786440 | tf_op jit(solution)/shard_map/ppermute | solution.py:392
  30.3 10.1 %copy-start.2 = (bf16[128,1024]{1,0:T(8,128)(2,1)}, bf16[128,1024]{1,0:T(8,128)(2,1)S(1)}, u32[]{:S(2)}) copy-start(bf16[128,1024]{1,0:T(8,128)(2,1)S(1)} %collective-permute-done.refs_1_) | copy-start | bytes 786436
  40.3 11.9 %copy-start.7 = (bf16[128,1024]{1,0:T(8,128)(2,1)}, bf16[128,1024]{1,0:T(8,128)(2,1)S(1)}, u32[]{:S(2)}) copy-start(bf16[128,1024]{1,0:T(8,128)(2,1)S(1)} %collective-permute-done.5.refs_0_) | copy-start | bytes 786436
  40.3 12.0 %collective-permute-start.6 = (bf16[128,1024]{1,0:T(8,128)(2,1)S(1)}, bf16[128,1024]{1,0:T(8,128)(2,1)S(1)}, u32[]{:S(2)}, u32[]{:S(2)}) collective-permute-start(bf16[128,1024]{1,0:T(8,128)(2,1)S(1)} %collective-permute-done.5.refs_0_), channel_id=1, source_target_pairs={{0,1},{1,0},{2,3},{3,2},{4,5},{5,4},{6,7},{7,6},{8,9},{9,8},{10,11... | collective-permute-start | bytes 786440 | tf_op jit(solution)/shard_map/ppermute | solution.py:393
  40.3 0.7 copy-start.8
  40.4 0.8 copy-start.9
  58.1 9.5 %copy-start.6 = (bf16[128,1024]{1,0:T(8,128)(2,1)S(1)}, bf16[128,1024]{1,0:T(8,128)(2,1)}, u32[]{:S(2)}) copy-start(bf16[128,1024]{1,0:T(8,128)(2,1)} %copy-done.5) | copy-start | bytes 786436
  62.7 15.0 %collective-permute-start.7 = (bf16[2,2,128,128]{3,2,1,0:T(8,128)(2,1)}, bf16[2,2,128,128]{3,2,1,0:T(8,128)(2,1)S(1)}, u32[]{:S(2)}, u32[]{:S(2)}) collective-permute-start(bf16[2,2,128,128]{3,2,1,0:T(8,128)(2,1)} %get-tuple-element.25.refs_0_), channel_id=1, source_target_pairs={{0,1},{1,0},{2,3},{3,2},{4,5},{5,4},{6,7},{7,6},{8,9},{9,8},{10,11... | collective-permute-start | bytes 393224 | tf_op jit(solution)/shard_map/ppermute | solution.py:432
  63.1 7.0 %collective-permute-start.8 = (bf16[2,2,128,128]{3,2,1,0:T(8,128)(2,1)}, bf16[2,2,128,128]{3,2,1,0:T(8,128)(2,1)S(1)}, u32[]{:S(2)}, u32[]{:S(2)}) collective-permute-start(bf16[2,2,128,128]{3,2,1,0:T(8,128)(2,1)} %get-tuple-element.26), channel_id=1, source_target_pairs={{0,2},{1,3},{2,0},{3,1},{4,6},{5,7},{6,4},{7,5},{8,10},{9,11},{10,... | collective-permute-start | bytes 393224 | tf_op jit(solution)/shard_map/ppermute | solution.py:429
  63.1 13.1 %collective-permute-start.10 = (bf16[2,2,128,128]{3,2,1,0:T(8,128)(2,1)}, bf16[2,2,128,128]{3,2,1,0:T(8,128)(2,1)S(1)}, u32[]{:S(2)}, u32[]{:S(2)}) collective-permute-start(bf16[2,2,128,128]{3,2,1,0:T(8,128)(2,1)} %get-tuple-element.27), channel_id=1, source_target_pairs={{0,4},{1,5},{2,6},{3,7},{4,0},{5,1},{6,2},{7,3},{8,12},{9,13},{10,... | collective-permute-start | bytes 393224 | tf_op jit(solution)/shard_map/ppermute | solution.py:429
  63.6 12.6 %collective-permute-start.12 = (bf16[2,2,128,128]{3,2,1,0:T(8,128)(2,1)}, bf16[2,2,128,128]{3,2,1,0:T(8,128)(2,1)S(1)}, u32[]{:S(2)}, u32[]{:S(2)}) collective-permute-start(bf16[2,2,128,128]{3,2,1,0:T(8,128)(2,1)} %get-tuple-element.28), channel_id=1, source_target_pairs={{0,6},{1,7},{2,4},{3,5},{4,2},{5,3},{6,0},{7,1},{8,14},{9,15},{10,... | collective-permute-start | bytes 393224 | tf_op jit(solution)/shard_map/ppermute | solution.py:429
  70.2 7.6 %copy-start.11 = (bf16[2,2,128,128]{3,2,1,0:T(8,128)(2,1)}, bf16[2,2,128,128]{3,2,1,0:T(8,128)(2,1)S(1)}, u32[]{:S(2)}) copy-start(bf16[2,2,128,128]{3,2,1,0:T(8,128)(2,1)S(1)} %collective-permute-done.8.refs_2_) | copy-start | bytes 393220
  70.2 7.5 %collective-permute-start.9 = (bf16[2,2,128,128]{3,2,1,0:T(8,128)(2,1)S(1)}, bf16[2,2,128,128]{3,2,1,0:T(8,128)(2,1)S(1)}, u32[]{:S(2)}, u32[]{:S(2)}) collective-permute-start(bf16[2,2,128,128]{3,2,1,0:T(8,128)(2,1)S(1)} %collective-permute-done.8.refs_2_), channel_id=1, source_target_pairs={{0,1},{1,0},{2,3},{3,2},{4,5},{5,4},{6,7},{7,6},{8,9},{9,8},{10,11... | collective-permute-start | bytes 393224 | tf_op jit(solution)/shard_map/ppermute | solution.py:432
  76.3 1.5 %copy-start.12 = (bf16[2,2,128,128]{3,2,1,0:T(8,128)(2,1)}, bf16[2,2,128,128]{3,2,1,0:T(8,128)(2,1)S(1)}, u32[]{:S(2)}) copy-start(bf16[2,2,128,128]{3,2,1,0:T(8,128)(2,1)S(1)} %collective-permute-done.10.refs_4_) | copy-start | bytes 393220
  76.3 1.5 %collective-permute-start.11 = (bf16[2,2,128,128]{3,2,1,0:T(8,128)(2,1)S(1)}, bf16[2,2,128,128]{3,2,1,0:T(8,128)(2,1)S(1)}, u32[]{:S(2)}, u32[]{:S(2)}) collective-permute-start(bf16[2,2,128,128]{3,2,1,0:T(8,128)(2,1)S(1)} %collective-permute-done.10.refs_4_), channel_id=1, source_target_pairs={{0,1},{1,0},{2,3},{3,2},{4,5},{5,4},{6,7},{7,6},{8,9},{9,8},{10,11... | collective-permute-start | bytes 393224 | tf_op jit(solution)/shard_map/ppermute | solution.py:432
  76.3 1.5 %copy-start.13 = (bf16[2,2,128,128]{3,2,1,0:T(8,128)(2,1)}, bf16[2,2,128,128]{3,2,1,0:T(8,128)(2,1)S(1)}, u32[]{:S(2)}) copy-start(bf16[2,2,128,128]{3,2,1,0:T(8,128)(2,1)S(1)} %collective-permute-done.12.refs_6_) | copy-start | bytes 393220
  76.3 1.5 %collective-permute-start.13 = (bf16[2,2,128,128]{3,2,1,0:T(8,128)(2,1)S(1)}, bf16[2,2,128,128]{3,2,1,0:T(8,128)(2,1)S(1)}, u32[]{:S(2)}, u32[]{:S(2)}) collective-permute-start(bf16[2,2,128,128]{3,2,1,0:T(8,128)(2,1)S(1)} %collective-permute-done.12.refs_6_), channel_id=1, source_target_pairs={{0,1},{1,0},{2,3},{3,2},{4,5},{5,4},{6,7},{7,6},{8,9},{9,8},{10,11... | collective-permute-start | bytes 393224 | tf_op jit(solution)/shard_map/ppermute | solution.py:432
  78.5 17.4 %copy-start.17 = (s32[1,8,1]{1,2,0:T(1,128)S(1)}, s32[1,8,1]{1,2,0:T(1,128)}, u32[]{:S(2)}) copy-start(s32[1,8,1]{1,2,0:T(1,128)} %param.15) | copy-start | bytes 100
  95.5 17.8 %copy-start.1 = (bf16[256,1024]{1,0:T(8,128)(2,1)S(1)}, bf16[256,1024]{1,0:T(8,128)(2,1)}, u32[]{:S(2)}) copy-start(bf16[256,1024]{1,0:T(8,128)(2,1)} %expert.1) | copy-start | bytes 1572868
  95.5 14.3 %collective-permute-start.14 = (bf16[256,1024]{1,0:T(8,128)(2,1)}, bf16[256,1024]{1,0:T(8,128)(2,1)S(1)}, u32[]{:S(2)}, u32[]{:S(2)}) collective-permute-start(bf16[256,1024]{1,0:T(8,128)(2,1)} %expert.1), channel_id=1, source_target_pairs={{0,1},{1,0},{2,3},{3,2},{4,5},{5,4},{6,7},{7,6},{8,9},{9,8},{10,11... | collective-permute-start | bytes 1572872 | tf_op jit(solution)/shard_map/ppermute | solution.py:457
  110.9 13.0 %collective-permute-start.18 = (bf16[128,1024]{1,0:T(8,128)(2,1)S(1)}, bf16[128,1024]{1,0:T(8,128)(2,1)S(1)}, u32[]{:S(2)}, u32[]{:S(2)}) collective-permute-start(bf16[128,1024]{1,0:T(8,128)(2,1)S(1)} %get-tuple-element.35), channel_id=1, source_target_pairs={{0,14},{1,15},{2,12},{3,13},{4,10},{5,11},{6,8},{7,9},{8,22},{9,23... | collective-permute-start | bytes 786440 | tf_op jit(solution)/shard_map/ppermute | solution.py:470
  113.4 32.0 %collective-permute-start.17 = (bf16[128,1024]{1,0:T(8,128)(2,1)S(1)}, bf16[128,1024]{1,0:T(8,128)(2,1)S(1)}, u32[]{:S(2)}, u32[]{:S(2)}) collective-permute-start(bf16[128,1024]{1,0:T(8,128)(2,1)S(1)} %get-tuple-element.33), channel_id=1, source_target_pairs={{0,12},{1,13},{2,14},{3,15},{4,8},{5,9},{6,10},{7,11},{8,20},{9,21... | collective-permute-start | bytes 786440 | tf_op jit(solution)/shard_map/ppermute | solution.py:470
  116.7 28.7 %collective-permute-start.15 = (bf16[128,1024]{1,0:T(8,128)(2,1)S(1)}, bf16[128,1024]{1,0:T(8,128)(2,1)S(1)}, u32[]{:S(2)}, u32[]{:S(2)}) collective-permute-start(bf16[128,1024]{1,0:T(8,128)(2,1)S(1)} %get-tuple-element.34), channel_id=1, source_target_pairs={{0,8},{1,9},{2,10},{3,11},{4,12},{5,13},{6,14},{7,15},{8,16},{9,17... | collective-permute-start | bytes 786440 | tf_op jit(solution)/shard_map/ppermute | solution.py:470
  118.2 27.2 %collective-permute-start.16 = (bf16[128,1024]{1,0:T(8,128)(2,1)S(1)}, bf16[128,1024]{1,0:T(8,128)(2,1)S(1)}, u32[]{:S(2)}, u32[]{:S(2)}) collective-permute-start(bf16[128,1024]{1,0:T(8,128)(2,1)S(1)} %get-tuple-element.32), channel_id=1, source_target_pairs={{0,10},{1,11},{2,8},{3,9},{4,14},{5,15},{6,12},{7,13},{8,18},{9,19... | collective-permute-start | bytes 786440 | tf_op jit(solution)/shard_map/ppermute | solution.py:470
  (5 other events, 3.4 us)

commit v2 on v1

v2 whole, which is shorter than its diff:
```python
from functools import partial

import jax
import jax.numpy as jnp
from jax import lax
from jax.experimental import pallas as pl
from jax.experimental.pallas import tpu as pltpu
from jax.sharding import PartitionSpec as P

EXPERTS = 8
BLOCK = 128
CHIPS = 4
CORES = 2
CAP = 2
PARTS = 3
EXTRA = 16
F32 = jnp.float32
BF16 = jnp.bfloat16
VMEM_LIMIT = 16 * 1024 * 1024


def lane_route(count, hop):
    route = []
    for i in range(count):
        base, chip, core = i - i % EXPERTS, i % EXPERTS // CORES, i % CORES
        route.append((i, base + (chip + hop) % CHIPS * CORES + core))
    return route


def pair_route(count):
    return [(i, i ^ 1) for i in range(count)]


def chip_route(count, k):
    return [(i, i ^ (CORES * k)) for i in range(count)]


def home_route(sections, count, hop):
    return [
        (s * count + i, (s + 1) % sections * count + j)
        for s in range(sections)
        for i, j in lane_route(count, hop)
    ]


def mm(a, b, dims=((1,), (0,))):
    return lax.dot_general(a, b, (dims, ((), ())), preferred_element_type=F32)


def halves(a):
    high = a.astype(BF16)
    return high, (a - high.astype(F32)).astype(BF16)


def mm3(a, b):
    (ah, al), (bh, bl) = a, b
    return mm(ah, bh) + (mm(ah, bl) + mm(al, bh))


def place_iota():
    row = lax.broadcasted_iota(jnp.int32, (BLOCK, BLOCK), 0)
    col = lax.broadcasted_iota(jnp.int32, (BLOCK, BLOCK), 1)
    return row, col


def lower_inverse(negs):
    row, col = place_iota()
    eye = jnp.where(row == col, 1.0, 0.0).astype(F32)
    small = 16
    near = row // small == col // small
    diag = [jnp.where(near, n, 0.0) for n in negs]
    total = [eye + d for d in diag]
    power = [d.astype(BF16) for d in diag]
    for _ in range((small - 1).bit_length() - 1):
        power = [mm(p, p).astype(BF16) for p in power]
        total = [t + mm(t.astype(BF16), p) for t, p in zip(total, power)]
    size = small
    while size < BLOCK:
        off = (row // (2 * size) == col // (2 * size)) & (row // size != col // size)
        cross = [jnp.where(off, n, 0.0).astype(BF16) for n in negs]
        short = [t.astype(BF16) for t in total]
        left = [mm(t, c).astype(BF16) for t, c in zip(short, cross)]
        total = [t + mm(m, s) for t, m, s in zip(total, left, short)]
        size *= 2
    return total


def unit(v):
    return v * lax.rsqrt(jnp.sum(v * v, axis=-1, keepdims=True) + 1e-06)


def attach_kernel(x_ref, decay_ref, out_ref, sem):
    copy = pltpu.make_async_copy(x_ref, out_ref.at[pl.ds(0, BLOCK), :], sem)
    copy.start()
    rest = decay_ref[...]
    heads = rest.shape[0]
    row = lax.broadcasted_iota(jnp.int32, (EXTRA, BLOCK), 0)
    parts = []
    for _ in range(PARTS):
        parts.append(rest.astype(BF16).astype(F32))
        rest = rest - parts[-1]
    for h in range(heads):
        block = jnp.zeros((EXTRA, BLOCK), F32)
        for n, part in enumerate(parts):
            block = jnp.where(row == n, part[h : h + 1, :], block)
        out_ref[BLOCK:, h * BLOCK : (h + 1) * BLOCK] = block.astype(BF16)
    copy.wait()


def attach(x, decay):
    vmem = pl.BlockSpec(memory_space=pltpu.VMEM)
    return pl.pallas_call(
        attach_kernel,
        out_shape=jax.ShapeDtypeStruct((BLOCK + EXTRA, x.shape[1]), BF16),
        in_specs=[pl.BlockSpec(memory_space=pl.ANY), vmem],
        out_specs=vmem,
        scratch_shapes=[pltpu.SemaphoreType.DMA],
        compiler_params=pltpu.CompilerParams(vmem_limit_bytes=VMEM_LIMIT),
        name="attach_decay",
    )(x, decay)


def running_decay(parts):
    row, col = place_iota()
    upto = jnp.where(row <= col, 1.0, 0.0).astype(BF16)
    return jnp.sum(mm(parts, upto), axis=0, keepdims=True)


def block_terms(projs, cums):
    row, col = place_iota()
    hd = BLOCK
    q = [unit(p[:, :hd].astype(BF16).astype(F32)) for p in projs]
    k = [unit(p[:, hd : 2 * hd].astype(BF16).astype(F32)) for p in projs]
    v = [p[:, 2 * hd : 3 * hd].astype(BF16).astype(F32) for p in projs]
    beta = [jax.nn.sigmoid(p[:, 3 * hd :]) for p in projs]
    across = [jnp.broadcast_to(c, (BLOCK, BLOCK)) for c in cums]
    down = [jnp.transpose(a) for a in across]
    kb = [a.astype(BF16) for a in k]
    inner = [
        mm(jnp.concatenate([a.astype(BF16), b], axis=0), b, ((1,), (1,))) for a, b in zip(q, kb)
    ]
    ratio = [
        jnp.where(row >= col, jnp.exp(jnp.where(row >= col, d - a, 0.0)), 0.0)
        for d, a in zip(down, across)
    ]
    negs = [
        jnp.where(row > col, -(b * r * i[BLOCK:]), 0.0) for b, r, i in zip(beta, ratio, inner)
    ]
    growth = [jnp.exp(d) for d in down]
    rhs = [
        jnp.concatenate([b * g * a, b * c], axis=1) for b, g, a, c in zip(beta, growth, k, v)
    ]
    inv = lower_inverse(negs)
    solved = [mm(t.astype(BF16), r.astype(BF16)).astype(BF16) for t, r in zip(inv, rhs)]
    scores = [(i[:BLOCK] * r).astype(BF16) for i, r in zip(inner, ratio)]
    inside = [mm(s, w) for s, w in zip(scores, solved)]
    last = [d[BLOCK - 1 :, :] for d in down]
    tail = [(jnp.exp(e - d) * a).astype(BF16) for e, d, a in zip(last, down, k)]
    step = [mm(w, t, ((0,), (0,))) for w, t in zip(solved, tail)]
    fade = [jnp.exp(e) for e in last]
    reads = [g * a - i[:, :hd] for g, a, i in zip(growth, q, inside)]
    local = [i[:, hd:] for i in inside]
    return reads, local, step, fade


def where_am_i():
    place = lax.axis_index("seq")
    inner = jnp.bitwise_and(place, EXPERTS - 1)
    return place - inner, inner // CORES, jnp.bitwise_and(inner, 1)


def routes(kinds_ref, base):
    kinds = [kinds_ref[base + b] for b in range(EXPERTS)]
    ranks = []
    for b in range(EXPERTS):
        rank = jnp.int32(0)
        for earlier in range(b):
            rank = rank + jnp.where(kinds[earlier] == kinds[b], 1, 0)
        ranks.append(rank)
    return kinds, ranks


def sources(kinds, ranks, kind):
    found = []
    for slot in range(CAP):
        block = jnp.int32(0)
        for b in range(EXPERTS):
            block = block + jnp.where((kinds[b] == kind) & (ranks[b] == slot), b, 0)
        found.append(block)
    return found


def arrivals(chip, core):
    return [
        jnp.bitwise_and(chip + hop, CHIPS - 1) * CORES + (core if side == 0 else 1 - core)
        for hop in (0, 3, 1, 2)
        for side in (0, 1)
    ]


def normed(x, gain):
    xf = x.astype(F32)
    return (xf * lax.rsqrt(jnp.mean(xf * xf, axis=-1, keepdims=True) + 1e-06) * gain).astype(BF16)


def pair_terms(gain_ref, weight_ref, x_refs, norm_ref, put):
    _, chip, core = where_am_i()
    at = pl.ds(pl.multiple_of((chip * CORES + core) * BLOCK, BLOCK), BLOCK)
    gain = gain_ref[...]
    for j, ref in enumerate(x_refs):
        norm_ref[j * BLOCK : (j + 1) * BLOCK, :] = normed(ref[:BLOCK, :], gain)
    both = mm(norm_ref[...], weight_ref[...])
    reads, local, step, fade = block_terms(
        [both[:BLOCK], both[BLOCK:]], [running_decay(ref[BLOCK:, at]) for ref in x_refs]
    )
    for i in range(len(x_refs)):
        put(i, reads[i].astype(BF16), local[i], step[i], jnp.broadcast_to(fade[i], (8, BLOCK)))


def term_scratch(count, width):
    return [pltpu.VMEM((count * BLOCK, width), BF16)]


def term_shapes(count):
    return (
        ((count, BLOCK, BLOCK), BF16),
        ((count, BLOCK, BLOCK), F32),
        ((count, 2 * BLOCK, BLOCK), F32),
        ((count, 8, BLOCK), F32),
    )


def terms_kernel(gain_ref, weight_ref, left_ref, right_ref, *refs):
    outs, scratch = refs[:4], refs[4:]

    def put(j, *values):
        for ref, value in zip(outs, values):
            ref[j] = value

    pair_terms(gain_ref, weight_ref, (left_ref, right_ref), *scratch, put)


def terms(gain, weight, blocks):
    count = len(blocks)
    width = blocks[0].shape[1]
    vmem = pl.BlockSpec(memory_space=pltpu.VMEM)
    return pl.pallas_call(
        terms_kernel,
        out_shape=tuple(jax.ShapeDtypeStruct(*s) for s in term_shapes(count)),
        in_specs=[vmem] * 4,
        out_specs=(vmem,) * 4,
        scratch_shapes=term_scratch(count, width),
        compiler_params=pltpu.CompilerParams(vmem_limit_bytes=VMEM_LIMIT),
        cost_estimate=pl.CostEstimate(
            flops=4 * 10**9, bytes_accessed=3 * 10**6, transcendentals=10**5
        ),
        name="chunk_terms",
    )(gain, weight, *blocks)


def mix_kernel(counts, late, kinds_ref, out_gain_ref, *refs):
    base, chip, core = where_am_i()
    blocks = arrivals(chip, core)
    groups = [refs[4 * g : 4 * g + 4] for g in range(len(counts))]
    refs = refs[4 * len(counts) :]
    if late:
        gain_ref, weight_ref, left_ref, right_ref = refs[:4]
        refs = refs[4:]
    else:
        start_ref, refs = refs[0], refs[1:]
    outs, refs = refs[:CHIPS], refs[CHIPS:]
    scr, on_scr, refs = refs[:4], refs[4], refs[5:]
    at = 0
    for group, count in zip(groups, counts):
        for j in range(count):
            for ref, keep in zip(group, scr):
                keep[blocks[at]] = ref[j]
            at += 1
    if late:

        def put(j, *values):
            for ref, value in zip(scr, values):
                ref[blocks[at + j]] = value

        pair_terms(gain_ref, weight_ref, (left_ref, right_ref), *refs, put)
    reads_scr, local_scr, step_scr, fade_scr = scr
    state = jnp.zeros((BLOCK, BLOCK), F32) if late else start_ref[...]
    out_gain = out_gain_ref[...]
    for b in range(EXPERTS):
        split = halves(state)
        move = step_scr[b]
        mixed = mm(reads_scr[b], split[0], ((1,), (1,))) + local_scr[b]
        on_scr[b] = normed(mixed, out_gain)
        if b + 1 < EXPERTS:
            erase = mm3(split, halves(move[:BLOCK]))
            state = fade_scr[b][0:1, :] * state - erase + move[BLOCK:]
    kinds, ranks = routes(kinds_ref, base)
    for k in range(CHIPS):
        there = jnp.bitwise_xor(chip, k)
        for side in range(CORES):
            found = sources(kinds, ranks, there * CORES + side)
            for slot in range(CAP):
                outs[k][side, slot] = on_scr[found[slot]]


def mix(kinds, out_gain, groups, start=None, late=()):
    counts = tuple(g[0].shape[0] for g in groups)
    vmem = pl.BlockSpec(memory_space=pltpu.VMEM)
    extra = list(late) if late else [start]
    operands = [kinds, out_gain] + [a for g in groups for a in g] + extra
    sent = jax.ShapeDtypeStruct((CORES, CAP, BLOCK, BLOCK), BF16)
    return pl.pallas_call(
        partial(mix_kernel, counts, bool(late)),
        out_shape=(sent,) * CHIPS,
        in_specs=[pl.BlockSpec(memory_space=pltpu.SMEM)] + [vmem] * (len(operands) - 1),
        out_specs=(vmem,) * CHIPS,
        scratch_shapes=[pltpu.VMEM(*s) for s in term_shapes(EXPERTS)]
        + [pltpu.VMEM((EXPERTS, BLOCK, BLOCK), BF16)]
        + (term_scratch(2, late[2].shape[1]) if late else []),
        compiler_params=pltpu.CompilerParams(vmem_limit_bytes=VMEM_LIMIT),
        cost_estimate=pl.CostEstimate(
            flops=3 * 10**10, bytes_accessed=4 * 10**6, transcendentals=10**5
        ),
        name="state_walk",
    )(*operands)


def home_kernel(kinds_ref, own_ref, other_ref, *outs):
    base, chip, core = where_am_i()
    kinds, ranks = routes(kinds_ref, base)
    for k in range(CHIPS):
        home = jnp.bitwise_and(chip + k, CHIPS - 1) * CORES + core
        kind, rank = jnp.int32(0), jnp.int32(0)
        for b in range(EXPERTS):
            kind = kind + jnp.where(home == b, kinds[b], 0)
            rank = rank + jnp.where(home == b, ranks[b], 0)
        here = kind // CORES == chip
        mine = jnp.bitwise_and(kind, 1) == core
        outs[k][...] = jnp.zeros_like(outs[k])
        for slot in range(CAP):
            rows = slice(slot * BLOCK, (slot + 1) * BLOCK)

            @pl.when(here & mine & (rank == slot))
            def _():
                outs[k][...] = own_ref[rows, :]

            @pl.when(here & jnp.logical_not(mine) & (rank == slot))
            def _():
                outs[k][...] = other_ref[rows, :]


def homeward(kinds, own, other):
    vmem = pl.BlockSpec(memory_space=pltpu.VMEM)
    rows, width = own.shape
    return pl.pallas_call(
        home_kernel,
        out_shape=(jax.ShapeDtypeStruct((rows // CAP, width), BF16),) * CHIPS,
        in_specs=[pl.BlockSpec(memory_space=pltpu.SMEM), vmem, vmem],
        out_specs=(vmem,) * CHIPS,
        compiler_params=pltpu.CompilerParams(vmem_limit_bytes=VMEM_LIMIT),
        name="homeward",
    )(kinds, own, other)


def project(kinds_ref, gain_ref, out_weight_ref, x_refs, on_refs, x_scr, on_scr, h_ref, hn_ref, sem):
    base, chip, core = where_am_i()
    kinds, ranks = routes(kinds_ref, base)
    found = sources(kinds, ranks, chip * CORES + core)
    for slot in range(CAP):
        for block, ref in zip(arrivals(chip, core), x_refs):

            @pl.when(block == found[slot])
            def _():
                rows = ref.at[pl.ds(0, BLOCK), :]
                pltpu.make_async_copy(rows, x_scr.at[slot], sem.at[slot]).start()

    for k in range(CHIPS):
        there = jnp.bitwise_xor(chip, k)
        for side in range(CORES):
            head = there * CORES + (core if side == 0 else 1 - core)
            at = pl.ds(pl.multiple_of(head * BLOCK, BLOCK), BLOCK)
            got = on_refs[k * CORES + side]
            for slot in range(CAP):
                on_scr[slot * BLOCK : (slot + 1) * BLOCK, at] = got[core, slot]
    for slot in range(CAP):
        rows = slice(slot * BLOCK, (slot + 1) * BLOCK)
        added = mm(on_scr[rows, :], out_weight_ref[...])
        rows_of_x = x_refs[0].at[pl.ds(0, BLOCK), :]
        pltpu.make_async_copy(rows_of_x, x_scr.at[slot], sem.at[slot]).wait()
        hidden = (x_scr[slot].astype(F32) + added).astype(BF16)
        h_ref[rows, :] = hidden
        hn_ref[rows, :] = normed(hidden, gain_ref[...])


def project_kernel(kinds_ref, gain_ref, out_weight_ref, *refs):
    x_refs, on_refs = refs[:EXPERTS], refs[EXPERTS : 2 * EXPERTS]
    h_ref, hn_ref, x_scr, on_scr, sem = refs[2 * EXPERTS :]
    project(kinds_ref, gain_ref, out_weight_ref, x_refs, on_refs, x_scr, on_scr, h_ref, hn_ref, sem)


def expert_kernel(tile, kinds_ref, gain_ref, out_weight_ref, *refs):
    x_refs, on_refs = refs[:EXPERTS], refs[EXPERTS : 2 * EXPERTS]
    gate_ref, up_ref, down_ref, out_ref = refs[2 * EXPERTS : 2 * EXPERTS + 4]
    x_scr, on_scr, h_scr, hn_scr, act_scr, sem = refs[2 * EXPERTS + 4 :]
    project(
        kinds_ref, gain_ref, out_weight_ref, x_refs, on_refs, x_scr, on_scr, h_scr, hn_scr, sem
    )
    rows = hn_scr[...]
    for at in range(0, gate_ref.shape[3], tile):
        part = slice(at, at + tile)
        gate = mm(rows, gate_ref[0, 0, :, part])
        up = mm(rows, up_ref[0, 0, :, part])
        act_scr[:, part] = (gate / (1.0 + jnp.exp(-gate)) * up).astype(BF16)
    width = out_ref.shape[1]
    for at in range(0, width, width // 2):
        part = slice(at, at + width // 2)
        ffn = mm(act_scr[...], down_ref[0, 0, :, part]).astype(BF16).astype(F32)
        out_ref[:, part] = (h_scr[:, part].astype(F32) + ffn).astype(BF16)


def expert(kinds, gain, out_weight, blocks, ons, gate, up, down):
    rows, width = CAP * BLOCK, blocks[0].shape[1]
    vmem = pl.BlockSpec(memory_space=pltpu.VMEM)
    return pl.pallas_call(
        partial(expert_kernel, min(512, gate.shape[3])),
        out_shape=jax.ShapeDtypeStruct((rows, width), BF16),
        in_specs=[pl.BlockSpec(memory_space=pltpu.SMEM), vmem, vmem]
        + [pl.BlockSpec(memory_space=pl.ANY)] * EXPERTS
        + [vmem] * (EXPERTS + 3),
        out_specs=vmem,
        scratch_shapes=[
            pltpu.VMEM((CAP, BLOCK, width), BF16),
            pltpu.VMEM((rows, width), BF16),
            pltpu.VMEM((rows, width), BF16),
            pltpu.VMEM((rows, width), BF16),
            pltpu.VMEM((rows, gate.shape[3]), BF16),
            pltpu.SemaphoreType.DMA((CAP,)),
        ],
        compiler_params=pltpu.CompilerParams(vmem_limit_bytes=VMEM_LIMIT),
        name="expert",
    )(kinds, gain, out_weight, *blocks, *ons, gate, up, down)


def project_only(kinds, gain, out_weight, blocks, ons):
    rows, width = CAP * BLOCK, blocks[0].shape[1]
    vmem = pl.BlockSpec(memory_space=pltpu.VMEM)
    return pl.pallas_call(
        project_kernel,
        out_shape=(jax.ShapeDtypeStruct((rows, width), BF16),) * 2,
        in_specs=[pl.BlockSpec(memory_space=pltpu.SMEM), vmem, vmem]
        + [pl.BlockSpec(memory_space=pl.ANY)] * EXPERTS
        + [vmem] * EXPERTS,
        out_specs=(vmem, vmem),
        scratch_shapes=[
            pltpu.VMEM((CAP, BLOCK, width), BF16),
            pltpu.VMEM((rows, width), BF16),
            pltpu.SemaphoreType.DMA((CAP,)),
        ],
        compiler_params=pltpu.CompilerParams(vmem_limit_bytes=VMEM_LIMIT),
        name="project",
    )(kinds, gain, out_weight, *blocks, *ons)


def group_start(place, count, groups_of_terms):
    groups = count // EXPERTS
    ein = partial(jnp.einsum, precision=lax.Precision.HIGHEST)
    eye = jnp.eye(BLOCK, dtype=F32)
    step = jnp.concatenate([g[2] for g in groups_of_terms], axis=0)
    fade = jnp.concatenate([g[3] for g in groups_of_terms], axis=0)
    inner = place % EXPERTS
    order = jnp.argsort(jnp.stack(arrivals(inner // CORES, inner % CORES)))
    step, fade = jnp.take(step, order, axis=0), jnp.take(fade, order, axis=0)
    moves = fade[:, 0, :][:, None, :] * eye - step[:, :BLOCK]
    adds = step[:, BLOCK:]
    total, added = moves[0], adds[0]
    for b in range(1, EXPERTS):
        total, added = ein("ij,jk->ik", total, moves[b]), ein("vk,kj->vj", added, moves[b]) + adds[b]
    peers = [[g * EXPERTS + e for g in range(groups)] for e in range(EXPERTS)]
    gather = partial(lax.all_gather, axis_name="seq", axis_index_groups=peers)
    totals, addeds = gather(total), gather(added)

    def one(hop, state):
        return ein(
            "vk,kj->vj", state, lax.dynamic_index_in_dim(totals, hop, 0, False)
        ) + lax.dynamic_index_in_dim(addeds, hop, 0, False)

    return lax.fori_loop(0, place // EXPERTS, one, jnp.zeros((BLOCK, BLOCK), F32))


def per_device(
    held,
    log_decay,
    route_ids,
    norm_gain,
    qkv_weight,
    beta_weight,
    out_gain,
    out_weight,
    ffn_gain,
    gate_weight,
    up_weight,
    down_weight,
):
    count = lax.axis_size("seq")
    sections = lax.axis_size("segment")
    groups = count // EXPERTS
    place = lax.axis_index("seq")
    inner = place % EXPERTS
    width = held.shape[2]
    pair = partial(lax.ppermute, axis_name="seq", perm=pair_route(count))
    kinds = route_ids.reshape(-1)

    def hop(block, by):
        return lax.ppermute(block, "seq", lane_route(count, by))

    own = attach(held[0], log_decay[0].T)
    left = hop(own, 1)
    own_other = pair(own)
    later, _ = lax.optimization_barrier((own, own_other))
    right = hop(later, -1)

    def head_columns(at):
        return lax.dynamic_slice_in_dim(qkv_weight[0], at * width + inner * BLOCK, BLOCK, 1)

    beta_column = lax.dynamic_slice_in_dim(beta_weight[0], inner, 1, 1)
    weight = jnp.concatenate(
        [head_columns(0), head_columns(1), head_columns(2)]
        + [jnp.broadcast_to(beta_column, (width, BLOCK))],
        axis=1,
    )

    known = [terms(norm_gain, weight, (own, own_other))]
    left, _ = lax.optimization_barrier((left, known[0][0]))
    far = hop(left, 1)
    near = [(own, own_other), (left, pair(left))]
    known.append(terms(norm_gain, weight, near[1]))
    near.append((right, pair(right)))
    known.append(terms(norm_gain, weight, near[2]))
    far, *_ = lax.optimization_barrier((far, known[1][0], known[2][0]))
    last = (far, pair(far))
    if groups > 1:
        known.append(terms(norm_gain, weight, last))
        sends = mix(kinds, out_gain, known, start=group_start(place, count, known))
    else:
        sends = mix(kinds, out_gain, known, late=(norm_gain, weight, *last))

    got = [sends[0]] + [lax.ppermute(sends[k], "seq", chip_route(count, k)) for k in range(1, CHIPS)]
    ons = []
    for block in got:
        ons += [block, pair(block)]
    blocks = [block for two in near + [last] for block in two]

    if groups == 1:
        finished = expert(
            kinds, ffn_gain, out_weight[0], blocks, ons, gate_weight, up_weight, down_weight
        )
    else:
        hidden, hn = project_only(kinds, ffn_gain, out_weight[0], blocks, ons)
        peers = [[g * EXPERTS + e for g in range(groups)] for e in range(EXPERTS)]
        rows = lax.all_gather(hn, "seq", axis_index_groups=peers, tiled=True)
        gate = jnp.dot(rows, gate_weight[0, 0], preferred_element_type=F32)
        up = jnp.dot(rows, up_weight[0, 0], preferred_element_type=F32)
        act = (jax.nn.silu(gate) * up).astype(BF16)
        part = jnp.dot(act, down_weight[0, 0], preferred_element_type=F32)
        ffn = lax.psum_scatter(
            part, "seq", scatter_dimension=0, axis_index_groups=peers, tiled=True
        ).astype(BF16)
        finished = (hidden.astype(F32) + ffn.astype(F32)).astype(BF16)

    def send_home(block, by):
        return lax.ppermute(block, ("segment", "seq"), home_route(sections, count, by))

    here, right_home, far_home, left_home = homeward(kinds, finished, pair(finished))
    passed = hop(far_home, 1)
    from_right = send_home(left_home, -1)
    from_here = send_home(here, 0)
    from_left = send_home(passed + right_home, 1)
    return (from_left + from_right + from_here)[None]


def solution(mesh):
    placed = (
        P("segment", "seq", None),
        P("segment", "seq", None),
        P("segment", None, None),
        P("segment", None),
        P("segment", None, None),
        P("segment", None, None),
        P("segment", None),
        P("segment", None, None),
        P("segment", None),
        P("segment", "seq", None, None),
        P("segment", "seq", None, None),
        P("segment", "seq", None, None),
    )
    return jax.shard_map(
        per_device, mesh=mesh, in_specs=placed, out_specs=P("segment", "seq", None), check_vma=False
    )
```

time: 147 us -> 88.6 us (0.60)
  blocking collectives: 16.2 us -> 0 us
  Pallas kernels: 37.2 us -> 22 us
  between operations: 12.9 us -> 0.26 us
  local copies, waits for them, and re-layouts: 9.5 us -> 3.12 us
  other arithmetic: 6.36 us -> 0.94 us
    all_gather x1 -> x0, blocking collectives: 16.2 us -> none  [per_device(): lax.all_gather(log_decay[0].T, 'seq', axis_index_groups=members if groups...]
    pallas_call x4 -> x7, Pallas kernels: 37.2 us -> 22 us  [the longest x1 8.9 us: expert(): pl.pallas_call(partial(expert_kernel, min(512, gate.shape[3])), out_shape...]
    ppermute x9 -> x8, waiting for transfers between devices: 26.7 us -> 15.3 us  [the longest x3 12.2 us: send_home(): lax.ppermute(block, ('segment', 'seq'), home_route(sections, count, by))]
    ppermute x3 -> x4, waiting for transfers between devices: 9.88 us -> 18.6 us  [hop(): return lax.ppermute(block, 'seq', lane_route(count, by))]
    ppermute x9 -> x8, starting transfers between devices: 9.13 us -> 6.35 us  [the longest x3 5.39 us: send_home(): lax.ppermute(block, ('segment', 'seq'), home_route(sections, count, by))]
    ppermute x3 -> x4, starting transfers between devices: 4.75 us -> 7.25 us  [hop(): return lax.ppermute(block, 'seq', lane_route(count, by))]
    select_n x5 -> x0, other arithmetic: 2.16 us -> none  [the longest x2 1.18 us: per_device(): send = jnp.where(which == at, front, send)]
    dynamic_slice x4 -> x0, local copies, waits for them, and re-layouts: 2.11 us -> none  [the longest x1 0.68 us: per_device(): slot = lax.dynamic_index_in_dim(rank, home, 0, False)]
  transfers between devices with their start and end apart: 19 -> 19, of which waited for: 5 -> 12; matrix products, arithmetic and copies ran while one was open for 8% -> 2% of each run, Pallas kernels for 8% -> 8%
where the time goes in v2:
time: 88.6 us; the launch traced here: 88.4 us
  waiting for transfers between devices  43.6 us (49%)
  Pallas kernels  22 us (25%)
  starting transfers between devices  18.6 us (21%)
  local copies, waits for them, and re-layouts  3.12 us (4%)
  other arithmetic  0.94 us (1%)
    ppermute x4, waiting for transfers between devices, hop(): return lax.ppermute(block, 'seq', lane_route(count, by))  18.6 us
    ppermute x3, waiting for transfers between devices, send_home(): lax.ppermute(block, ('segment', 'seq'), home_route(sections, count, by))  12.2 us
    pallas_call x1, Pallas kernels, expert(): pl.pallas_call(partial(expert_kernel, min(512, gate.shape[3])), out_shape...  8.9 us
    ppermute x3, waiting for transfers between devices, per_device(): lax.ppermute(sends[k], 'seq', chip_route(count, k))  8.59 us
    pallas_call x3, Pallas kernels, terms(): pl.pallas_call(terms_kernel, out_shape=tuple((jax.ShapeDtypeStruct(*s) fo...  7.39 us
    ppermute x4, starting transfers between devices, hop(): return lax.ppermute(block, 'seq', lane_route(count, by))  7.25 us
    ppermute x3, starting transfers between devices, send_home(): lax.ppermute(block, ('segment', 'seq'), home_route(sections, count, by))  5.39 us
    pallas_call x1, Pallas kernels, mix(): pl.pallas_call(partial(mix_kernel, counts, bool(late)), out_shape=(sent,)...  4.8 us
  transfers between devices with their start and end apart: 19, of which 12 were waited for; matrix products, arithmetic and copies ran while one was open for 2% of the time, Pallas kernels for 8%

profile of v2, /device:TPU:0, one launch (start us, length us, event | category | flops | bytes accessed | tf_op | source)
XLA Modules:
  0.0 88.4 jit_solution(2606271509080372564)
XLA Ops:
  0.0 1.0 %copy-done.2 = bf16[1,128,1024]{2,1,0:T(8,128)(2,1)S(1)} copy-done((bf16[1,128,1024]{2,1,0:T(8,128)(2,1)S(1)}, bf16[1,128,1024]{2,1,0:T(8,128)(2,1)}, u32[]{:S(2)}) %copy-start.2) | copy-done | bytes 262168
  1.0 0.7 copy-done.3
  1.7 0.5 collective-permute-start
  2.2 2.6 %collective-permute-start.1 = (bf16[144,1024]{1,0:T(8,128)(2,1)S(1)}, bf16[144,1024]{1,0:T(8,128)(2,1)S(1)}, u32[]{:S(2)}, u32[]{:S(2)}) collective-permute-start(bf16[144,1024]{1,0:T(8,128)(2,1)S(1)} %attach_decay.1.left_ref.refs_0_), channel_id=1, source_target_pairs={{0,2},{1,3},{2,4},{3,5},{4,6},{5,7},{6,0},{7,1},{8,10},{9,11},{10,... | collective-permute-start | bytes 884744 | tf_op jit(solution)/shard_map/ppermute | solution.py:514
  4.9 1.2 %dynamic-slice_bitcast_fusion.2 = (bf16[1024,128]{1,0:T(8,128)(2,1)S(1)}, bf16[1024,128]{1,0:T(8,128)(2,1)S(1)}, bf16[1024,128]{1,0:T(8,128)(2,1)S(1)}) fusion(bf16[1,1024,3072]{2,1,0:T(8,128)(2,1)} %param.16, s32[]{:T(128)S(6)} %select_n.20, s32[]{:T(128)S(6)} %select_n.22, s32[]{:T(128)S(6)} %select_n.21), kind=kLoop, calls=%fused_computation.4 | loop fusion | bytes 1572876 | tf_op jit(solution)/shard_map/dynamic_slice | solution.py:523
  6.4 2.2 %collective-permute-start.3 = (bf16[144,1024]{1,0:T(8,128)(2,1)S(1)}, bf16[144,1024]{1,0:T(8,128)(2,1)S(1)}, u32[]{:S(2)}, u32[]{:S(2)}) collective-permute-start(bf16[144,1024]{1,0:T(8,128)(2,1)S(1)} %attach_decay.1.left_ref.refs_0_), channel_id=1, source_target_pairs={{0,6},{1,7},{2,0},{3,1},{4,2},{5,3},{6,4},{7,5},{8,14},{9,15},{10,... | collective-permute-start | bytes 884744 | tf_op jit(solution)/shard_map/ppermute | solution.py:514
  8.6 2.5 %chunk_terms.3 = (bf16[2,128,128]{2,1,0:T(8,128)(2,1)S(1)}, f32[2,128,128]{2,1,0:T(8,128)S(1)}, f32[2,256,128]{2,1,0:T(8,128)S(1)}, f32[2,8,128]{2,1,0:T(8,128)S(1)}) custom-call(f32[1,1024]{1,0:T(1,128)S(1)} %copy-done.6, bf16[1024,512]{1,0:T(8,128)(2,1)S(1)} %pad_maximum_fusion.weight_ref.refs_13_, bf16[144,1024]{1,0:T(8,128)(2,1)S(1)} %attach_decay.1.left_ref.refs_0_, ...), custom_call_target="tpu_custom_call" | custom-call | flops 4000000000 | bytes 3000000 | tf_op jit(solution)/shard_map/chunk_terms/pallas_call | solution.py:247
  11.1 3.7 %collective-permute-done.1.left_ref.refs_2_ = bf16[144,1024]{1,0:T(8,128)(2,1)S(1)} collective-permute-done((bf16[144,1024]{1,0:T(8,128)(2,1)S(1)}, bf16[144,1024]{1,0:T(8,128)(2,1)S(1)}, u32[]{:S(2)}, u32[]{:S(2)}) %collective-permute-start.1) | collective-permute-done | bytes 294944 | tf_op jit(solution)/shard_map/ppermute | solution.py:514
  14.8 6.0 %collective-permute-done.3.left_ref.refs_4_ = bf16[144,1024]{1,0:T(8,128)(2,1)S(1)} collective-permute-done((bf16[144,1024]{1,0:T(8,128)(2,1)S(1)}, bf16[144,1024]{1,0:T(8,128)(2,1)S(1)}, u32[]{:S(2)}, u32[]{:S(2)}) %collective-permute-start.3) | collective-permute-done | bytes 294944 | tf_op jit(solution)/shard_map/ppermute | solution.py:514
  20.9 2.5 %chunk_terms.4 = (bf16[2,128,128]{2,1,0:T(8,128)(2,1)S(1)}, f32[2,128,128]{2,1,0:T(8,128)S(1)}, f32[2,256,128]{2,1,0:T(8,128)S(1)}, f32[2,8,128]{2,1,0:T(8,128)S(1)}) custom-call(f32[1,1024]{1,0:T(1,128)S(1)} %copy-done.6, bf16[1024,512]{1,0:T(8,128)(2,1)S(1)} %pad_maximum_fusion.weight_ref.refs_13_, ...), custom_call_target="tpu_custom_call" | custom-call | flops 4000000000 | bytes 3000000 | tf_op jit(solution)/shard_map/chunk_terms/pallas_call | solution.py:247
  23.4 2.5 %chunk_terms.5 = (bf16[2,128,128]{2,1,0:T(8,128)(2,1)S(1)}, f32[2,128,128]{2,1,0:T(8,128)S(1)}, f32[2,256,128]{2,1,0:T(8,128)S(1)}, f32[2,8,128]{2,1,0:T(8,128)S(1)}) custom-call(f32[1,1024]{1,0:T(1,128)S(1)} %copy-done.6, bf16[1024,512]{1,0:T(8,128)(2,1)S(1)} %pad_maximum_fusion.weight_ref.refs_13_, ...), custom_call_target="tpu_custom_call" | custom-call | flops 4000000000 | bytes 3000000 | tf_op jit(solution)/shard_map/chunk_terms/pallas_call | solution.py:247
  25.9 4.1 %collective-permute-done.5.refs_14_.refs_6_ = bf16[144,1024]{1,0:T(8,128)(2,1)S(1)} collective-permute-done((bf16[144,1024]{1,0:T(8,128)(2,1)S(1)}, bf16[144,1024]{1,0:T(8,128)(2,1)S(1)}, u32[]{:S(2)}, u32[]{:S(2)}) %collective-permute-start.5) | collective-permute-done | bytes 294944 | tf_op jit(solution)/shard_map/ppermute | solution.py:514
  30.0 1.6 %collective-permute-done.6.refs_15_.refs_7_ = bf16[144,1024]{1,0:T(8,128)(2,1)S(1)} collective-permute-done((bf16[144,1024]{1,0:T(8,128)(2,1)S(1)}, bf16[144,1024]{1,0:T(8,128)(2,1)S(1)}, u32[]{:S(2)}, u32[]{:S(2)}) %collective-permute-start.6) | collective-permute-done | bytes 294944 | tf_op jit(solution)/shard_map/ppermute | solution.py:540
  31.6 4.8 %state_walk.1 = (bf16[2,2,128,128]{3,2,1,0:T(8,128)(2,1)S(1)}, bf16[2,2,128,128]{3,2,1,0:T(8,128)(2,1)S(1)}, bf16[2,2,128,128]{3,2,1,0:T(8,128)(2,1)S(1)}, bf16[2,2,128,128]{3,2,1,0:T(8,128)(2,1)S(1)}) custom-call(s32[8]{0:T(128)S(1)} %bitcast.23, f32[1,128]{1,0:T(1,128)S(1)} %copy-done.7, bf16[2,128,128]{2,1,0:T(8,128)(2,1)S(1)} %get-tuple-element.28.refs_0_, ...), custom_call_target="tpu_custom_call" | custom-call | flops 30000001024 | bytes 4000000 | tf_op jit(solution)/shard_map/state_walk/pallas_call | solution.py:312
  36.5 2.3 %collective-permute-start.10 = (bf16[2,2,128,128]{3,2,1,0:T(8,128)(2,1)S(1)}, bf16[2,2,128,128]{3,2,1,0:T(8,128)(2,1)S(1)}, u32[]{:S(2)}, u32[]{:S(2)}) collective-permute-start(bf16[2,2,128,128]{3,2,1,0:T(8,128)(2,1)S(1)} %get-tuple-element.45), channel_id=1, source_target_pairs={{0,4},{1,5},{2,6},{3,7},{4,0},{5,1},{6,2},{7,3},{8,12},{9,13},{10,... | collective-permute-start | bytes 393224 | tf_op jit(solution)/shard_map/ppermute | solution.py:547
  38.8 2.1 %collective-permute-start.12 = (bf16[2,2,128,128]{3,2,1,0:T(8,128)(2,1)S(1)}, bf16[2,2,128,128]{3,2,1,0:T(8,128)(2,1)S(1)}, u32[]{:S(2)}, u32[]{:S(2)}) collective-permute-start(bf16[2,2,128,128]{3,2,1,0:T(8,128)(2,1)S(1)} %get-tuple-element.46), channel_id=1, source_target_pairs={{0,6},{1,7},{2,4},{3,5},{4,2},{5,3},{6,0},{7,1},{8,14},{9,15},{10,... | collective-permute-start | bytes 393224 | tf_op jit(solution)/shard_map/ppermute | solution.py:547
  40.9 3.1 %collective-permute-done.8.refs_10_ = bf16[2,2,128,128]{3,2,1,0:T(8,128)(2,1)S(1)} collective-permute-done((bf16[2,2,128,128]{3,2,1,0:T(8,128)(2,1)S(1)}, bf16[2,2,128,128]{3,2,1,0:T(8,128)(2,1)S(1)}, u32[]{:S(2)}, u32[]{:S(2)}) %collective-permute-start.8) | collective-permute-done | bytes 131104 | tf_op jit(solution)/shard_map/ppermute | solution.py:547
  44.0 5.5 %collective-permute-done.10.refs_12_ = bf16[2,2,128,128]{3,2,1,0:T(8,128)(2,1)S(1)} collective-permute-done((bf16[2,2,128,128]{3,2,1,0:T(8,128)(2,1)S(1)}, bf16[2,2,128,128]{3,2,1,0:T(8,128)(2,1)S(1)}, u32[]{:S(2)}, u32[]{:S(2)}) %collective-permute-start.10) | collective-permute-done | bytes 131104 | tf_op jit(solution)/shard_map/ppermute | solution.py:547
  49.5 0.5 collective-permute-start.13
  50.0 0.8 collective-permute-done.11.refs_13_
  51.1 8.9 %expert.1.own_ref = bf16[256,1024]{1,0:T(8,128)(2,1)S(1)} custom-call(s32[8]{0:T(128)S(1)} %bitcast.24, f32[1,1024]{1,0:T(1,128)S(1)} %copy-done.4, bf16[1024,1024]{1,0:T(8,128)(2,1)S(1)} %bitcast.20, bf16[144,1024]{1,0:T(8,128)(2,1)S(1)} %attach_decay.1.left_ref.refs_0_, bf16[144,1024]{1,0:T(8,128)(2,1)S(1)} %collective-permute-done.right_ref.refs_1_, ...), custom_call_target="tpu_custom_call" | custom-call | tf_op jit(solution)/shard_map/expert/pallas_call | solution.py:424
  60.0 0.4 collective-permute-start.14
  60.4 1.6 %collective-permute-done.14.other_ref = bf16[256,1024]{1,0:T(8,128)(2,1)S(1)} collective-permute-done((bf16[256,1024]{1,0:T(8,128)(2,1)S(1)}, bf16[256,1024]{1,0:T(8,128)(2,1)S(1)}, u32[]{:S(2)}, u32[]{:S(2)}) %collective-permute-start.14) | collective-permute-done | bytes 524320 | tf_op jit(solution)/shard_map/ppermute | solution.py:573
  62.0 0.8 homeward.1
  62.8 2.4 %collective-permute-start.15 = (bf16[128,1024]{1,0:T(8,128)(2,1)S(1)}, bf16[128,1024]{1,0:T(8,128)(2,1)S(1)}, u32[]{:S(2)}, u32[]{:S(2)}) collective-permute-start(bf16[128,1024]{1,0:T(8,128)(2,1)S(1)} %get-tuple-element.47), channel_id=1, source_target_pairs={{0,2},{1,3},{2,4},{3,5},{4,6},{5,7},{6,0},{7,1},{8,10},{9,11},{10,... | collective-permute-start | bytes 786440 | tf_op jit(solution)/shard_map/ppermute | solution.py:514
  65.3 2.4 %collective-permute-start.17 = (bf16[128,1024]{1,0:T(8,128)(2,1)S(1)}, bf16[128,1024]{1,0:T(8,128)(2,1)S(1)}, u32[]{:S(2)}, u32[]{:S(2)}) collective-permute-start(bf16[128,1024]{1,0:T(8,128)(2,1)S(1)} %get-tuple-element.49), channel_id=1, source_target_pairs={{0,14},{1,15},{2,8},{3,9},{4,10},{5,11},{6,12},{7,13},{8,22},{9,23... | collective-permute-start | bytes 786440 | tf_op jit(solution)/shard_map/ppermute | solution.py:571
  67.6 1.5 %collective-permute-start.18 = (bf16[128,1024]{1,0:T(8,128)(2,1)S(1)}, bf16[128,1024]{1,0:T(8,128)(2,1)S(1)}, u32[]{:S(2)}, u32[]{:S(2)}) collective-permute-start(bf16[128,1024]{1,0:T(8,128)(2,1)S(1)} %get-tuple-element.50), channel_id=1, source_target_pairs={{0,8},{1,9},{2,10},{3,11},{4,12},{5,13},{6,14},{7,15},{8,16},{9,17... | collective-permute-start | bytes 786440 | tf_op jit(solution)/shard_map/ppermute | solution.py:571
  69.1 4.7 %collective-permute-done.15 = bf16[128,1024]{1,0:T(8,128)(2,1)S(1)} collective-permute-done((bf16[128,1024]{1,0:T(8,128)(2,1)S(1)}, bf16[128,1024]{1,0:T(8,128)(2,1)S(1)}, u32[]{:S(2)}, u32[]{:S(2)}) %collective-permute-start.15) | collective-permute-done | bytes 262176 | tf_op jit(solution)/shard_map/ppermute | solution.py:514
  73.9 1.5 %collective-permute-start.16 = (bf16[128,1024]{1,0:T(8,128)(2,1)S(1)}, bf16[128,1024]{1,0:T(8,128)(2,1)S(1)}, u32[]{:S(2)}, u32[]{:S(2)}) collective-permute-start(bf16[128,1024]{1,0:T(8,128)(2,1)S(1)} %add.34), channel_id=1, source_target_pairs={{0,10},{1,11},{2,12},{3,13},{4,14},{5,15},{6,8},{7,9},{8,18},{9,19... | collective-permute-start | bytes 786440 | tf_op jit(solution)/shard_map/ppermute | solution.py:571
  75.5 5.8 %collective-permute-done.17 = bf16[128,1024]{1,0:T(8,128)(2,1)S(1)} collective-permute-done((bf16[128,1024]{1,0:T(8,128)(2,1)S(1)}, bf16[128,1024]{1,0:T(8,128)(2,1)S(1)}, u32[]{:S(2)}, u32[]{:S(2)}) %collective-permute-start.17) | collective-permute-done | bytes 262176 | tf_op jit(solution)/shard_map/ppermute | solution.py:571
  81.3 6.4 %collective-permute-done.18 = bf16[128,1024]{1,0:T(8,128)(2,1)S(1)} collective-permute-done((bf16[128,1024]{1,0:T(8,128)(2,1)S(1)}, bf16[128,1024]{1,0:T(8,128)(2,1)S(1)}, u32[]{:S(2)}, u32[]{:S(2)}) %collective-permute-start.18) | collective-permute-done | bytes 262176 | tf_op jit(solution)/shard_map/ppermute | solution.py:571
  87.6 0.8 add_bitcast_fusion
  (50 shorter events, 0.8 us)
Async XLA Ops:
  0.0 4.9 %copy-start = (bf16[1,1024,8]{1,2,0:T(8,128)(2,1)S(1)}, bf16[1,1024,8]{1,2,0:T(8,128)(2,1)}, u32[]{:S(2)}) copy-start(bf16[1,1024,8]{1,2,0:T(8,128)(2,1)} %param.17) | copy-start | bytes 49156
  0.0 1.0 %copy-start.2 = (bf16[1,128,1024]{2,1,0:T(8,128)(2,1)S(1)}, bf16[1,128,1024]{2,1,0:T(8,128)(2,1)}, u32[]{:S(2)}) copy-start(bf16[1,128,1024]{2,1,0:T(8,128)(2,1)} %param.12) | copy-start | bytes 786436
  1.7 6.9 %copy-start.6 = (f32[1,1024]{1,0:T(1,128)S(1)}, f32[1,1024]{1,0:T(1,128)}, u32[]{:S(2)}) copy-start(f32[1,1024]{1,0:T(1,128)} %refs_12_.1) | copy-start | bytes 12292
  1.7 4.7 %collective-permute-start = (bf16[144,1024]{1,0:T(8,128)(2,1)S(1)}, bf16[144,1024]{1,0:T(8,128)(2,1)S(1)}, u32[]{:S(2)}, u32[]{:S(2)}) collective-permute-start(bf16[144,1024]{1,0:T(8,128)(2,1)S(1)} %attach_decay.1.left_ref.refs_0_), channel_id=1, source_target_pairs={{0,1},{1,0},{2,3},{3,2},{4,5},{5,4},{6,7},{7,6},{8,9},{9,8},{10,11... | collective-permute-start | bytes 884744 | tf_op jit(solution)/shard_map/ppermute | solution.py:518
  2.2 12.6 %collective-permute-start.1 = (bf16[144,1024]{1,0:T(8,128)(2,1)S(1)}, bf16[144,1024]{1,0:T(8,128)(2,1)S(1)}, u32[]{:S(2)}, u32[]{:S(2)}) collective-permute-start(bf16[144,1024]{1,0:T(8,128)(2,1)S(1)} %attach_decay.1.left_ref.refs_0_), channel_id=1, source_target_pairs={{0,2},{1,3},{2,4},{3,5},{4,6},{5,7},{6,0},{7,1},{8,10},{9,11},{10,... | collective-permute-start | bytes 884744 | tf_op jit(solution)/shard_map/ppermute | solution.py:514
  6.4 14.4 %collective-permute-start.3 = (bf16[144,1024]{1,0:T(8,128)(2,1)S(1)}, bf16[144,1024]{1,0:T(8,128)(2,1)S(1)}, u32[]{:S(2)}, u32[]{:S(2)}) collective-permute-start(bf16[144,1024]{1,0:T(8,128)(2,1)S(1)} %attach_decay.1.left_ref.refs_0_), channel_id=1, source_target_pairs={{0,6},{1,7},{2,0},{3,1},{4,2},{5,3},{6,4},{7,5},{8,14},{9,15},{10,... | collective-permute-start | bytes 884744 | tf_op jit(solution)/shard_map/ppermute | solution.py:514
  14.8 6.1 %collective-permute-start.2 = (bf16[144,1024]{1,0:T(8,128)(2,1)S(1)}, bf16[144,1024]{1,0:T(8,128)(2,1)S(1)}, u32[]{:S(2)}, u32[]{:S(2)}) collective-permute-start(bf16[144,1024]{1,0:T(8,128)(2,1)S(1)} %collective-permute-done.1.left_ref.refs_2_), channel_id=1, source_target_pairs={{0,1},{1,0},{2,3},{3,2},{4,5},{5,4},{6,7},{7,6},{8,9},{9,8},{10,11... | collective-permute-start | bytes 884744 | tf_op jit(solution)/shard_map/ppermute | solution.py:535
  14.8 15.2 %collective-permute-start.5 = (bf16[144,1024]{1,0:T(8,128)(2,1)S(1)}, bf16[144,1024]{1,0:T(8,128)(2,1)S(1)}, u32[]{:S(2)}, u32[]{:S(2)}) collective-permute-start(bf16[144,1024]{1,0:T(8,128)(2,1)S(1)} %collective-permute-done.1.left_ref.refs_2_), channel_id=1, source_target_pairs={{0,2},{1,3},{2,4},{3,5},{4,6},{5,7},{6,0},{7,1},{8,10},{9,11},{10,... | collective-permute-start | bytes 884744 | tf_op jit(solution)/shard_map/ppermute | solution.py:514
  20.8 2.5 %collective-permute-start.4 = (bf16[144,1024]{1,0:T(8,128)(2,1)S(1)}, bf16[144,1024]{1,0:T(8,128)(2,1)S(1)}, u32[]{:S(2)}, u32[]{:S(2)}) collective-permute-start(bf16[144,1024]{1,0:T(8,128)(2,1)S(1)} %collective-permute-done.3.left_ref.refs_4_), channel_id=1, source_target_pairs={{0,1},{1,0},{2,3},{3,2},{4,5},{5,4},{6,7},{7,6},{8,9},{9,8},{10,11... | collective-permute-start | bytes 884744 | tf_op jit(solution)/shard_map/ppermute | solution.py:537
  23.3 8.2 %copy-start.5 = (s32[1,8,1]{1,2,0:T(1,128)S(1)}, s32[1,8,1]{1,2,0:T(1,128)}, u32[]{:S(2)}) copy-start(s32[1,8,1]{1,2,0:T(1,128)} %param.14) | copy-start | bytes 100
  23.4 8.2 %copy-start.7 = (f32[1,128]{1,0:T(1,128)S(1)}, f32[1,128]{1,0:T(1,128)}, u32[]{:S(2)}) copy-start(f32[1,128]{1,0:T(1,128)} %out_gain_ref.1) | copy-start | bytes 1540
  30.0 1.6 %collective-permute-start.6 = (bf16[144,1024]{1,0:T(8,128)(2,1)S(1)}, bf16[144,1024]{1,0:T(8,128)(2,1)S(1)}, u32[]{:S(2)}, u32[]{:S(2)}) collective-permute-start(bf16[144,1024]{1,0:T(8,128)(2,1)S(1)} %collective-permute-done.5.refs_14_.refs_6_), channel_id=1, source_target_pairs={{0,1},{1,0},{2,3},{3,2},{4,5},{5,4},{6,7},{7,6},{8,9},{9,8},{10,11... | collective-permute-start | bytes 884744 | tf_op jit(solution)/shard_map/ppermute | solution.py:540
  31.6 19.5 %slice-start = ((s8[8388608]{0:T(1024)(128)(4,1)}), s8[4194304]{0:T(1024)(128)(4,1)S(1)}, s32[]{:S(2)}) async-start(s8[8388608]{0:T(1024)(128)(4,1)} %bitcast.14), calls=%async_computation | async-start | bytes 8388608
  31.6 19.5 %slice-start.2 = ((s8[8388608]{0:T(1024)(128)(4,1)}), s8[4194304]{0:T(1024)(128)(4,1)S(1)}, s32[]{:S(2)}) async-start(s8[8388608]{0:T(1024)(128)(4,1)} %bitcast.16), calls=%async_computation.2 | async-start | bytes 8388608
  31.6 19.5 %slice-start.4 = ((s8[8388608]{0:T(1024)(128)(4,1)}), s8[4194304]{0:T(1024)(128)(4,1)S(1)}, s32[]{:S(2)}) async-start(s8[8388608]{0:T(1024)(128)(4,1)} %bitcast.18), calls=%async_computation.4 | async-start | bytes 8388608
  31.6 19.5 %slice-start.1 = ((s8[8388608]{0:T(1024)(128)(4,1)}), s8[4194304]{0:T(1024)(128)(4,1)S(1)}, s32[]{:S(2)}) async-start(s8[8388608]{0:T(1024)(128)(4,1)} %bitcast.14), calls=%async_computation.1 | async-start | bytes 8388608
  31.6 19.5 %slice-start.3 = ((s8[8388608]{0:T(1024)(128)(4,1)}), s8[4194304]{0:T(1024)(128)(4,1)S(1)}, s32[]{:S(2)}) async-start(s8[8388608]{0:T(1024)(128)(4,1)} %bitcast.16), calls=%async_computation.3 | async-start | bytes 8388608
  31.6 19.5 %slice-start.5 = ((s8[8388608]{0:T(1024)(128)(4,1)}), s8[4194304]{0:T(1024)(128)(4,1)S(1)}, s32[]{:S(2)}) async-start(s8[8388608]{0:T(1024)(128)(4,1)} %bitcast.18), calls=%async_computation.5 | async-start | bytes 8388608
  31.6 19.5 %copy-start.1 = (bf16[1,1024,1024]{2,1,0:T(8,128)(2,1)S(1)}, bf16[1,1024,1024]{2,1,0:T(8,128)(2,1)}, u32[]{:S(2)}) copy-start(bf16[1,1024,1024]{2,1,0:T(8,128)(2,1)} %param.19) | copy-start | bytes 6291460
  31.6 19.5 %copy-start.4 = (f32[1,1024]{1,0:T(1,128)S(1)}, f32[1,1024]{1,0:T(1,128)}, u32[]{:S(2)}) copy-start(f32[1,1024]{1,0:T(1,128)} %gain_ref.7) | copy-start | bytes 12292
  36.4 7.5 %collective-permute-start.8 = (bf16[2,2,128,128]{3,2,1,0:T(8,128)(2,1)S(1)}, bf16[2,2,128,128]{3,2,1,0:T(8,128)(2,1)S(1)}, u32[]{:S(2)}, u32[]{:S(2)}) collective-permute-start(bf16[2,2,128,128]{3,2,1,0:T(8,128)(2,1)S(1)} %get-tuple-element.44), channel_id=1, source_target_pairs={{0,2},{1,3},{2,0},{3,1},{4,6},{5,7},{6,4},{7,5},{8,10},{9,11},{10,... | collective-permute-start | bytes 393224 | tf_op jit(solution)/shard_map/ppermute | solution.py:547
  36.5 13.0 %collective-permute-start.10 = (bf16[2,2,128,128]{3,2,1,0:T(8,128)(2,1)S(1)}, bf16[2,2,128,128]{3,2,1,0:T(8,128)(2,1)S(1)}, u32[]{:S(2)}, u32[]{:S(2)}) collective-permute-start(bf16[2,2,128,128]{3,2,1,0:T(8,128)(2,1)S(1)} %get-tuple-element.45), channel_id=1, source_target_pairs={{0,4},{1,5},{2,6},{3,7},{4,0},{5,1},{6,2},{7,3},{8,12},{9,13},{10,... | collective-permute-start | bytes 393224 | tf_op jit(solution)/shard_map/ppermute | solution.py:547
  38.8 10.7 %collective-permute-start.12 = (bf16[2,2,128,128]{3,2,1,0:T(8,128)(2,1)S(1)}, bf16[2,2,128,128]{3,2,1,0:T(8,128)(2,1)S(1)}, u32[]{:S(2)}, u32[]{:S(2)}) collective-permute-start(bf16[2,2,128,128]{3,2,1,0:T(8,128)(2,1)S(1)} %get-tuple-element.46), channel_id=1, source_target_pairs={{0,6},{1,7},{2,4},{3,5},{4,2},{5,3},{6,0},{7,1},{8,14},{9,15},{10,... | collective-permute-start | bytes 393224 | tf_op jit(solution)/shard_map/ppermute | solution.py:547
  40.9 9.1 %collective-permute-start.7 = (bf16[2,2,128,128]{3,2,1,0:T(8,128)(2,1)S(1)}, bf16[2,2,128,128]{3,2,1,0:T(8,128)(2,1)S(1)}, u32[]{:S(2)}, u32[]{:S(2)}) collective-permute-start(bf16[2,2,128,128]{3,2,1,0:T(8,128)(2,1)S(1)} %get-tuple-element.43.refs_8_), channel_id=1, source_target_pairs={{0,1},{1,0},{2,3},{3,2},{4,5},{5,4},{6,7},{7,6},{8,9},{9,8},{10,11... | collective-permute-start | bytes 393224 | tf_op jit(solution)/shard_map/ppermute | solution.py:550
  44.0 6.0 %collective-permute-start.9 = (bf16[2,2,128,128]{3,2,1,0:T(8,128)(2,1)S(1)}, bf16[2,2,128,128]{3,2,1,0:T(8,128)(2,1)S(1)}, u32[]{:S(2)}, u32[]{:S(2)}) collective-permute-start(bf16[2,2,128,128]{3,2,1,0:T(8,128)(2,1)S(1)} %collective-permute-done.8.refs_10_), channel_id=1, source_target_pairs={{0,1},{1,0},{2,3},{3,2},{4,5},{5,4},{6,7},{7,6},{8,9},{9,8},{10,11... | collective-permute-start | bytes 393224 | tf_op jit(solution)/shard_map/ppermute | solution.py:550
  49.5 1.3 %collective-permute-start.11 = (bf16[2,2,128,128]{3,2,1,0:T(8,128)(2,1)S(1)}, bf16[2,2,128,128]{3,2,1,0:T(8,128)(2,1)S(1)}, u32[]{:S(2)}, u32[]{:S(2)}) collective-permute-start(bf16[2,2,128,128]{3,2,1,0:T(8,128)(2,1)S(1)} %collective-permute-done.10.refs_12_), channel_id=1, source_target_pairs={{0,1},{1,0},{2,3},{3,2},{4,5},{5,4},{6,7},{7,6},{8,9},{9,8},{10,11... | collective-permute-start | bytes 393224 | tf_op jit(solution)/shard_map/ppermute | solution.py:550
  49.5 1.5 %collective-permute-start.13 = (bf16[2,2,128,128]{3,2,1,0:T(8,128)(2,1)S(1)}, bf16[2,2,128,128]{3,2,1,0:T(8,128)(2,1)S(1)}, u32[]{:S(2)}, u32[]{:S(2)}) collective-permute-start(bf16[2,2,128,128]{3,2,1,0:T(8,128)(2,1)S(1)} %collective-permute-done.12.refs_14_), channel_id=1, source_target_pairs={{0,1},{1,0},{2,3},{3,2},{4,5},{5,4},{6,7},{7,6},{8,9},{9,8},{10,11... | collective-permute-start | bytes 393224 | tf_op jit(solution)/shard_map/ppermute | solution.py:550
  60.0 2.0 %collective-permute-start.14 = (bf16[256,1024]{1,0:T(8,128)(2,1)S(1)}, bf16[256,1024]{1,0:T(8,128)(2,1)S(1)}, u32[]{:S(2)}, u32[]{:S(2)}) collective-permute-start(bf16[256,1024]{1,0:T(8,128)(2,1)S(1)} %expert.1.own_ref), channel_id=1, source_target_pairs={{0,1},{1,0},{2,3},{3,2},{4,5},{5,4},{6,7},{7,6},{8,9},{9,8},{10,11... | collective-permute-start | bytes 1572872 | tf_op jit(solution)/shard_map/ppermute | solution.py:573
  62.8 11.0 %collective-permute-start.15 = (bf16[128,1024]{1,0:T(8,128)(2,1)S(1)}, bf16[128,1024]{1,0:T(8,128)(2,1)S(1)}, u32[]{:S(2)}, u32[]{:S(2)}) collective-permute-start(bf16[128,1024]{1,0:T(8,128)(2,1)S(1)} %get-tuple-element.47), channel_id=1, source_target_pairs={{0,2},{1,3},{2,4},{3,5},{4,6},{5,7},{6,0},{7,1},{8,10},{9,11},{10,... | collective-permute-start | bytes 786440 | tf_op jit(solution)/shard_map/ppermute | solution.py:514
  65.3 16.0 %collective-permute-start.17 = (bf16[128,1024]{1,0:T(8,128)(2,1)S(1)}, bf16[128,1024]{1,0:T(8,128)(2,1)S(1)}, u32[]{:S(2)}, u32[]{:S(2)}) collective-permute-start(bf16[128,1024]{1,0:T(8,128)(2,1)S(1)} %get-tuple-element.49), channel_id=1, source_target_pairs={{0,14},{1,15},{2,8},{3,9},{4,10},{5,11},{6,12},{7,13},{8,22},{9,23... | collective-permute-start | bytes 786440 | tf_op jit(solution)/shard_map/ppermute | solution.py:571
  67.6 20.0 %collective-permute-start.18 = (bf16[128,1024]{1,0:T(8,128)(2,1)S(1)}, bf16[128,1024]{1,0:T(8,128)(2,1)S(1)}, u32[]{:S(2)}, u32[]{:S(2)}) collective-permute-start(bf16[128,1024]{1,0:T(8,128)(2,1)S(1)} %get-tuple-element.50), channel_id=1, source_target_pairs={{0,8},{1,9},{2,10},{3,11},{4,12},{5,13},{6,14},{7,15},{8,16},{9,17... | collective-permute-start | bytes 786440 | tf_op jit(solution)/shard_map/ppermute | solution.py:571
  73.9 13.7 %collective-permute-start.16 = (bf16[128,1024]{1,0:T(8,128)(2,1)S(1)}, bf16[128,1024]{1,0:T(8,128)(2,1)S(1)}, u32[]{:S(2)}, u32[]{:S(2)}) collective-permute-start(bf16[128,1024]{1,0:T(8,128)(2,1)S(1)} %add.34), channel_id=1, source_target_pairs={{0,10},{1,11},{2,12},{3,13},{4,14},{5,15},{6,8},{7,9},{8,18},{9,19... | collective-permute-start | bytes 786440 | tf_op jit(solution)/shard_map/ppermute | solution.py:571
  (1 other events, 0.7 us)

commit v3 on v2

--- a/solution.py
+++ b/solution.py
@@ -13,7 +13,7 @@
 CORES = 2
 CAP = 2
 PARTS = 3
-EXTRA = 16
+EXTRA = 32
 F32 = jnp.float32
 BF16 = jnp.bfloat16
 VMEM_LIMIT = 16 * 1024 * 1024
@@ -89,41 +89,55 @@
     return v * lax.rsqrt(jnp.sum(v * v, axis=-1, keepdims=True) + 1e-06)
 
 
-def attach_kernel(x_ref, decay_ref, out_ref, sem):
-    copy = pltpu.make_async_copy(x_ref, out_ref.at[pl.ds(0, BLOCK), :], sem)
-    copy.start()
-    rest = decay_ref[...]
-    heads = rest.shape[0]
-    row = lax.broadcasted_iota(jnp.int32, (EXTRA, BLOCK), 0)
+def attach_kernel(x_ref, decay_ref, out_ref, x_scr, decay_scr, sem):
+    copies = [
+        pltpu.make_async_copy(x_ref, x_scr, sem.at[0]),
+        pltpu.make_async_copy(decay_ref, decay_scr, sem.at[1]),
+    ]
+    for copy in copies:
+        copy.start()
+    for copy in copies:
+        copy.wait()
+    columns = x_ref.shape[1] // BLOCK
+    for c in range(columns):
+        out_ref[c * BLOCK : (c + 1) * BLOCK, :] = x_scr[:, c * BLOCK : (c + 1) * BLOCK]
+    rest = decay_scr[...]
     parts = []
     for _ in range(PARTS):
         parts.append(rest.astype(BF16).astype(F32))
         rest = rest - parts[-1]
-    for h in range(heads):
-        block = jnp.zeros((EXTRA, BLOCK), F32)
-        for n, part in enumerate(parts):
-            block = jnp.where(row == n, part[h : h + 1, :], block)
-        out_ref[BLOCK:, h * BLOCK : (h + 1) * BLOCK] = block.astype(BF16)
-    copy.wait()
+    parts.append(jnp.zeros((EXTRA - PARTS * rest.shape[0], BLOCK), F32))
+    out_ref[columns * BLOCK :, :] = jnp.concatenate(parts, axis=0).astype(BF16)
 
 
 def attach(x, decay):
-    vmem = pl.BlockSpec(memory_space=pltpu.VMEM)
+    hbm = pl.BlockSpec(memory_space=pltpu.HBM)
     return pl.pallas_call(
         attach_kernel,
-        out_shape=jax.ShapeDtypeStruct((BLOCK + EXTRA, x.shape[1]), BF16),
-        in_specs=[pl.BlockSpec(memory_space=pl.ANY), vmem],
-        out_specs=vmem,
-        scratch_shapes=[pltpu.SemaphoreType.DMA],
+        out_shape=jax.ShapeDtypeStruct((x.size // BLOCK + EXTRA, BLOCK), BF16),
+        in_specs=[hbm, hbm],
+        out_specs=pl.BlockSpec(memory_space=pltpu.VMEM),
+        scratch_shapes=[
+            pltpu.VMEM(x.shape, BF16),
+            pltpu.VMEM(decay.shape, F32),
+            pltpu.SemaphoreType.DMA((2,)),
+        ],
         compiler_params=pltpu.CompilerParams(vmem_limit_bytes=VMEM_LIMIT),
         name="attach_decay",
     )(x, decay)
 
 
-def running_decay(parts):
+def rows_of(ref):
+    columns = ref.shape[0] // BLOCK
+    return jnp.concatenate([ref[c * BLOCK : (c + 1) * BLOCK, :] for c in range(columns)], axis=1)
+
+
+def running_decay(parts, head, heads):
     row, col = place_iota()
     upto = jnp.where(row <= col, 1.0, 0.0).astype(BF16)
-    return jnp.sum(mm(parts, upto), axis=0, keepdims=True)
+    line = lax.broadcasted_iota(jnp.int32, parts.shape, 0)
+    mine = jnp.where((line % heads == head) & (line < PARTS * heads), parts.astype(F32), 0.0)
+    return jnp.sum(mm(mine.astype(BF16), upto), axis=0, keepdims=True)
 
 
 def block_terms(projs, cums):
@@ -205,13 +219,15 @@
 
 def pair_terms(gain_ref, weight_ref, x_refs, norm_ref, put):
     _, chip, core = where_am_i()
-    at = pl.ds(pl.multiple_of((chip * CORES + core) * BLOCK, BLOCK), BLOCK)
+    head = chip * CORES + core
     gain = gain_ref[...]
+    columns = x_refs[0].shape[0] // BLOCK
     for j, ref in enumerate(x_refs):
-        norm_ref[j * BLOCK : (j + 1) * BLOCK, :] = normed(ref[:BLOCK, :], gain)
+        norm_ref[j * BLOCK : (j + 1) * BLOCK, :] = normed(rows_of(ref), gain)
     both = mm(norm_ref[...], weight_ref[...])
     reads, local, step, fade = block_terms(
-        [both[:BLOCK], both[BLOCK:]], [running_decay(ref[BLOCK:, at]) for ref in x_refs]
+        [both[:BLOCK], both[BLOCK:]],
+        [running_decay(ref[columns * BLOCK :, :], head, columns) for ref in x_refs],
     )
     for i in range(len(x_refs)):
         put(i, reads[i].astype(BF16), local[i], step[i], jnp.broadcast_to(fade[i], (8, BLOCK)))
@@ -242,7 +258,7 @@
 
 def terms(gain, weight, blocks):
     count = len(blocks)
-    width = blocks[0].shape[1]
+    width = gain.shape[1]
     vmem = pl.BlockSpec(memory_space=pltpu.VMEM)
     return pl.pallas_call(
         terms_kernel,
@@ -316,7 +332,7 @@
         out_specs=(vmem,) * CHIPS,
         scratch_shapes=[pltpu.VMEM(*s) for s in term_shapes(EXPERTS)]
         + [pltpu.VMEM((EXPERTS, BLOCK, BLOCK), BF16)]
-        + (term_scratch(2, late[2].shape[1]) if late else []),
+        + (term_scratch(2, late[0].shape[1]) if late else []),
         compiler_params=pltpu.CompilerParams(vmem_limit_bytes=VMEM_LIMIT),
         cost_estimate=pl.CostEstimate(
             flops=3 * 10**10, bytes_accessed=4 * 10**6, transcendentals=10**5
@@ -371,7 +387,7 @@
 
             @pl.when(block == found[slot])
             def _():
-                rows = ref.at[pl.ds(0, BLOCK), :]
+                rows = ref.at[pl.ds(0, x_scr.shape[1]), :]
                 pltpu.make_async_copy(rows, x_scr.at[slot], sem.at[slot]).start()
 
     for k in range(CHIPS):
@@ -385,9 +401,9 @@
     for slot in range(CAP):
         rows = slice(slot * BLOCK, (slot + 1) * BLOCK)
         added = mm(on_scr[rows, :], out_weight_ref[...])
-        rows_of_x = x_refs[0].at[pl.ds(0, BLOCK), :]
+        rows_of_x = x_refs[0].at[pl.ds(0, x_scr.shape[1]), :]
         pltpu.make_async_copy(rows_of_x, x_scr.at[slot], sem.at[slot]).wait()
-        hidden = (x_scr[slot].astype(F32) + added).astype(BF16)
+        hidden = (rows_of(x_scr.at[slot]).astype(F32) + added).astype(BF16)
         h_ref[rows, :] = hidden
         hn_ref[rows, :] = normed(hidden, gain_ref[...])
 
@@ -419,7 +435,7 @@
 
 
 def expert(kinds, gain, out_weight, blocks, ons, gate, up, down):
-    rows, width = CAP * BLOCK, blocks[0].shape[1]
+    rows, width = CAP * BLOCK, gain.shape[1]
     vmem = pl.BlockSpec(memory_space=pltpu.VMEM)
     return pl.pallas_call(
         partial(expert_kernel, min(512, gate.shape[3])),
@@ -429,7 +445,7 @@
         + [vmem] * (EXPERTS + 3),
         out_specs=vmem,
         scratch_shapes=[
-            pltpu.VMEM((CAP, BLOCK, width), BF16),
+            pltpu.VMEM((CAP, width, BLOCK), BF16),
             pltpu.VMEM((rows, width), BF16),
             pltpu.VMEM((rows, width), BF16),
             pltpu.VMEM((rows, width), BF16),
@@ -442,7 +458,7 @@
 
 
 def project_only(kinds, gain, out_weight, blocks, ons):
-    rows, width = CAP * BLOCK, blocks[0].shape[1]
+    rows, width = CAP * BLOCK, gain.shape[1]
     vmem = pl.BlockSpec(memory_space=pltpu.VMEM)
     return pl.pallas_call(
         project_kernel,
@@ -452,7 +468,7 @@
         + [vmem] * EXPERTS,
         out_specs=(vmem, vmem),
         scratch_shapes=[
-            pltpu.VMEM((CAP, BLOCK, width), BF16),
+            pltpu.VMEM((CAP, width, BLOCK), BF16),
             pltpu.VMEM((rows, width), BF16),
             pltpu.SemaphoreType.DMA((CAP,)),
         ],

time: 88.6 us -> 85.6 us (0.966)
  waiting for transfers between devices: 43.6 us -> 40.3 us
    ppermute x4, waiting for transfers between devices: 18.6 us -> 15.5 us  [hop(): return lax.ppermute(block, 'seq', lane_route(count, by))]
  transfers between devices with their start and end apart: 19 -> 19, of which waited for: 12 -> 12; matrix products, arithmetic and copies ran while one was open for 2% -> 2% of each run, Pallas kernels for 8% -> 9%
where the time goes in v3:
time: 85.6 us; the launch traced here: 85.4 us
  waiting for transfers between devices  40.3 us (47%)
  Pallas kernels  22 us (26%)
  starting transfers between devices  18.9 us (22%)
  local copies, waits for them, and re-layouts  3.12 us (4%)
  other arithmetic  0.93 us (1%)
    ppermute x4, waiting for transfers between devices, hop(): return lax.ppermute(block, 'seq', lane_route(count, by))  15.5 us
    ppermute x3, waiting for transfers between devices, send_home(): lax.ppermute(block, ('segment', 'seq'), home_route(sections, count, by))  12.1 us
    pallas_call x1, Pallas kernels, expert(): pl.pallas_call(partial(expert_kernel, min(512, gate.shape[3])), out_shape...  8.9 us
    ppermute x3, waiting for transfers between devices, per_device(): lax.ppermute(sends[k], 'seq', chip_route(count, k))  8.59 us
    ppermute x4, starting transfers between devices, hop(): return lax.ppermute(block, 'seq', lane_route(count, by))  7.71 us
    pallas_call x3, Pallas kernels, terms(): pl.pallas_call(terms_kernel, out_shape=tuple((jax.ShapeDtypeStruct(*s) fo...  7.4 us
    ppermute x3, starting transfers between devices, send_home(): lax.ppermute(block, ('segment', 'seq'), home_route(sections, count, by))  5.72 us
    pallas_call x1, Pallas kernels, mix(): pl.pallas_call(partial(mix_kernel, counts, bool(late)), out_shape=(sent,)...  4.75 us
  transfers between devices with their start and end apart: 19, of which 12 were waited for; matrix products, arithmetic and copies ran while one was open for 2% of the time, Pallas kernels for 9%

profile of v3, /device:TPU:0, one launch (start us, length us, event | category | flops | bytes accessed | tf_op | source)
XLA Modules:
  0.0 85.4 jit_solution(10897468124604461728)
XLA Ops:
  0.0 1.0 %copy-done.2 = bf16[1,128,1024]{2,1,0:T(8,128)(2,1)S(1)} copy-done((bf16[1,128,1024]{2,1,0:T(8,128)(2,1)S(1)}, bf16[1,128,1024]{2,1,0:T(8,128)(2,1)}, u32[]{:S(2)}) %copy-start.2) | copy-done | bytes 262168
  1.0 0.7 copy-done.3
  1.8 3.1 %collective-permute-start.1 = (bf16[1056,128]{1,0:T(8,128)(2,1)S(1)}, bf16[1056,128]{1,0:T(8,128)(2,1)S(1)}, u32[]{:S(2)}, u32[]{:S(2)}) collective-permute-start(bf16[1056,128]{1,0:T(8,128)(2,1)S(1)} %attach_decay.1.left_ref.refs_0_), channel_id=1, source_target_pairs={{0,2},{1,3},{2,4},{3,5},{4,6},{5,7},{6,0},{7,1},{8,10},{9,11},{10,... | collective-permute-start | bytes 811016 | tf_op jit(solution)/shard_map/ppermute | solution.py:530
  4.9 1.2 %dynamic-slice_bitcast_fusion.2 = (bf16[1024,128]{1,0:T(8,128)(2,1)S(1)}, bf16[1024,128]{1,0:T(8,128)(2,1)S(1)}, bf16[1024,128]{1,0:T(8,128)(2,1)S(1)}) fusion(bf16[1,1024,3072]{2,1,0:T(8,128)(2,1)} %param.16, s32[]{:T(128)S(6)} %select_n.20, s32[]{:T(128)S(6)} %select_n.22, s32[]{:T(128)S(6)} %select_n.21), kind=kLoop, calls=%fused_computation.4 | loop fusion | bytes 1572876 | tf_op jit(solution)/shard_map/dynamic_slice | solution.py:539
  6.1 0.2 broadcast_in_dim.11
  6.4 2.2 %collective-permute-start.3 = (bf16[1056,128]{1,0:T(8,128)(2,1)S(1)}, bf16[1056,128]{1,0:T(8,128)(2,1)S(1)}, u32[]{:S(2)}, u32[]{:S(2)}) collective-permute-start(bf16[1056,128]{1,0:T(8,128)(2,1)S(1)} %attach_decay.1.left_ref.refs_0_), channel_id=1, source_target_pairs={{0,6},{1,7},{2,0},{3,1},{4,2},{5,3},{6,4},{7,5},{8,14},{9,15},{10,... | collective-permute-start | bytes 811016 | tf_op jit(solution)/shard_map/ppermute | solution.py:530
  8.6 2.5 %chunk_terms.3 = (bf16[2,128,128]{2,1,0:T(8,128)(2,1)S(1)}, f32[2,128,128]{2,1,0:T(8,128)S(1)}, f32[2,256,128]{2,1,0:T(8,128)S(1)}, f32[2,8,128]{2,1,0:T(8,128)S(1)}) custom-call(f32[1,1024]{1,0:T(1,128)S(1)} %copy-done.6, bf16[1024,512]{1,0:T(8,128)(2,1)S(1)} %pad_maximum_fusion.weight_ref.refs_13_, bf16[1056,128]{1,0:T(8,128)(2,1)S(1)} %attach_decay.1.left_ref.refs_0_, ...), custom_call_target="tpu_custom_call" | custom-call | flops 4000000000 | bytes 3000000 | tf_op jit(solution)/shard_map/chunk_terms/pallas_call | solution.py:263
  11.1 3.1 %collective-permute-done.1.left_ref.refs_2_ = bf16[1056,128]{1,0:T(8,128)(2,1)S(1)} collective-permute-done((bf16[1056,128]{1,0:T(8,128)(2,1)S(1)}, bf16[1056,128]{1,0:T(8,128)(2,1)S(1)}, u32[]{:S(2)}, u32[]{:S(2)}) %collective-permute-start.1) | collective-permute-done | bytes 270368 | tf_op jit(solution)/shard_map/ppermute | solution.py:530
  14.2 4.9 %collective-permute-done.3.left_ref.refs_4_ = bf16[1056,128]{1,0:T(8,128)(2,1)S(1)} collective-permute-done((bf16[1056,128]{1,0:T(8,128)(2,1)S(1)}, bf16[1056,128]{1,0:T(8,128)(2,1)S(1)}, u32[]{:S(2)}, u32[]{:S(2)}) %collective-permute-start.3) | collective-permute-done | bytes 270368 | tf_op jit(solution)/shard_map/ppermute | solution.py:530
  19.2 2.5 %chunk_terms.4 = (bf16[2,128,128]{2,1,0:T(8,128)(2,1)S(1)}, f32[2,128,128]{2,1,0:T(8,128)S(1)}, f32[2,256,128]{2,1,0:T(8,128)S(1)}, f32[2,8,128]{2,1,0:T(8,128)S(1)}) custom-call(f32[1,1024]{1,0:T(1,128)S(1)} %copy-done.6, bf16[1024,512]{1,0:T(8,128)(2,1)S(1)} %pad_maximum_fusion.weight_ref.refs_13_, ...), custom_call_target="tpu_custom_call" | custom-call | flops 4000000000 | bytes 3000000 | tf_op jit(solution)/shard_map/chunk_terms/pallas_call | solution.py:263
  21.7 2.5 %chunk_terms.5 = (bf16[2,128,128]{2,1,0:T(8,128)(2,1)S(1)}, f32[2,128,128]{2,1,0:T(8,128)S(1)}, f32[2,256,128]{2,1,0:T(8,128)S(1)}, f32[2,8,128]{2,1,0:T(8,128)S(1)}) custom-call(f32[1,1024]{1,0:T(1,128)S(1)} %copy-done.6, bf16[1024,512]{1,0:T(8,128)(2,1)S(1)} %pad_maximum_fusion.weight_ref.refs_13_, ...), custom_call_target="tpu_custom_call" | custom-call | flops 4000000000 | bytes 3000000 | tf_op jit(solution)/shard_map/chunk_terms/pallas_call | solution.py:263
  24.2 2.9 %collective-permute-done.5.refs_14_.refs_6_ = bf16[1056,128]{1,0:T(8,128)(2,1)S(1)} collective-permute-done((bf16[1056,128]{1,0:T(8,128)(2,1)S(1)}, bf16[1056,128]{1,0:T(8,128)(2,1)S(1)}, u32[]{:S(2)}, u32[]{:S(2)}) %collective-permute-start.5) | collective-permute-done | bytes 270368 | tf_op jit(solution)/shard_map/ppermute | solution.py:530
  27.1 1.5 %collective-permute-done.6.refs_15_.refs_7_ = bf16[1056,128]{1,0:T(8,128)(2,1)S(1)} collective-permute-done((bf16[1056,128]{1,0:T(8,128)(2,1)S(1)}, bf16[1056,128]{1,0:T(8,128)(2,1)S(1)}, u32[]{:S(2)}, u32[]{:S(2)}) %collective-permute-start.6) | collective-permute-done | bytes 270368 | tf_op jit(solution)/shard_map/ppermute | solution.py:556
  28.7 4.8 %state_walk.1 = (bf16[2,2,128,128]{3,2,1,0:T(8,128)(2,1)S(1)}, bf16[2,2,128,128]{3,2,1,0:T(8,128)(2,1)S(1)}, bf16[2,2,128,128]{3,2,1,0:T(8,128)(2,1)S(1)}, bf16[2,2,128,128]{3,2,1,0:T(8,128)(2,1)S(1)}) custom-call(s32[8]{0:T(128)S(1)} %bitcast.23, f32[1,128]{1,0:T(1,128)S(1)} %copy-done.7, bf16[2,128,128]{2,1,0:T(8,128)(2,1)S(1)} %get-tuple-element.28.refs_0_, ...), custom_call_target="tpu_custom_call" | custom-call | flops 30000001024 | bytes 4000000 | tf_op jit(solution)/shard_map/state_walk/pallas_call | solution.py:328
  33.5 2.3 %collective-permute-start.10 = (bf16[2,2,128,128]{3,2,1,0:T(8,128)(2,1)S(1)}, bf16[2,2,128,128]{3,2,1,0:T(8,128)(2,1)S(1)}, u32[]{:S(2)}, u32[]{:S(2)}) collective-permute-start(bf16[2,2,128,128]{3,2,1,0:T(8,128)(2,1)S(1)} %get-tuple-element.45), channel_id=1, source_target_pairs={{0,4},{1,5},{2,6},{3,7},{4,0},{5,1},{6,2},{7,3},{8,12},{9,13},{10,... | collective-permute-start | bytes 393224 | tf_op jit(solution)/shard_map/ppermute | solution.py:563
  35.8 2.1 %collective-permute-start.12 = (bf16[2,2,128,128]{3,2,1,0:T(8,128)(2,1)S(1)}, bf16[2,2,128,128]{3,2,1,0:T(8,128)(2,1)S(1)}, u32[]{:S(2)}, u32[]{:S(2)}) collective-permute-start(bf16[2,2,128,128]{3,2,1,0:T(8,128)(2,1)S(1)} %get-tuple-element.46), channel_id=1, source_target_pairs={{0,6},{1,7},{2,4},{3,5},{4,2},{5,3},{6,0},{7,1},{8,14},{9,15},{10,... | collective-permute-start | bytes 393224 | tf_op jit(solution)/shard_map/ppermute | solution.py:563
  37.9 3.1 %collective-permute-done.8.refs_10_ = bf16[2,2,128,128]{3,2,1,0:T(8,128)(2,1)S(1)} collective-permute-done((bf16[2,2,128,128]{3,2,1,0:T(8,128)(2,1)S(1)}, bf16[2,2,128,128]{3,2,1,0:T(8,128)(2,1)S(1)}, u32[]{:S(2)}, u32[]{:S(2)}) %collective-permute-start.8) | collective-permute-done | bytes 131104 | tf_op jit(solution)/shard_map/ppermute | solution.py:563
  41.0 5.5 %collective-permute-done.10.refs_12_ = bf16[2,2,128,128]{3,2,1,0:T(8,128)(2,1)S(1)} collective-permute-done((bf16[2,2,128,128]{3,2,1,0:T(8,128)(2,1)S(1)}, bf16[2,2,128,128]{3,2,1,0:T(8,128)(2,1)S(1)}, u32[]{:S(2)}, u32[]{:S(2)}) %collective-permute-start.10) | collective-permute-done | bytes 131104 | tf_op jit(solution)/shard_map/ppermute | solution.py:563
  46.5 0.5 collective-permute-start.13
  47.0 0.8 collective-permute-done.11.refs_13_
  48.1 8.9 %expert.1.own_ref = bf16[256,1024]{1,0:T(8,128)(2,1)S(1)} custom-call(s32[8]{0:T(128)S(1)} %bitcast.24, f32[1,1024]{1,0:T(1,128)S(1)} %copy-done.4, bf16[1024,1024]{1,0:T(8,128)(2,1)S(1)} %bitcast.20, bf16[1056,128]{1,0:T(8,128)(2,1)S(1)} %attach_decay.1.left_ref.refs_0_, bf16[1056,128]{1,0:T(8,128)(2,1)S(1)} %collective-permute-done.right_ref.refs_1_, ...), custom_call_target="tpu_custom_call" | custom-call | tf_op jit(solution)/shard_map/expert/pallas_call | solution.py:440
  57.0 0.4 collective-permute-start.14
  57.4 1.6 %collective-permute-done.14.other_ref = bf16[256,1024]{1,0:T(8,128)(2,1)S(1)} collective-permute-done((bf16[256,1024]{1,0:T(8,128)(2,1)S(1)}, bf16[256,1024]{1,0:T(8,128)(2,1)S(1)}, u32[]{:S(2)}, u32[]{:S(2)}) %collective-permute-start.14) | collective-permute-done | bytes 524320 | tf_op jit(solution)/shard_map/ppermute | solution.py:589
  59.0 0.8 homeward.1
  59.8 2.4 %collective-permute-start.15 = (bf16[128,1024]{1,0:T(8,128)(2,1)S(1)}, bf16[128,1024]{1,0:T(8,128)(2,1)S(1)}, u32[]{:S(2)}, u32[]{:S(2)}) collective-permute-start(bf16[128,1024]{1,0:T(8,128)(2,1)S(1)} %get-tuple-element.47), channel_id=1, source_target_pairs={{0,2},{1,3},{2,4},{3,5},{4,6},{5,7},{6,0},{7,1},{8,10},{9,11},{10,... | collective-permute-start | bytes 786440 | tf_op jit(solution)/shard_map/ppermute | solution.py:530
  62.2 2.5 %collective-permute-start.17 = (bf16[128,1024]{1,0:T(8,128)(2,1)S(1)}, bf16[128,1024]{1,0:T(8,128)(2,1)S(1)}, u32[]{:S(2)}, u32[]{:S(2)}) collective-permute-start(bf16[128,1024]{1,0:T(8,128)(2,1)S(1)} %get-tuple-element.49), channel_id=1, source_target_pairs={{0,14},{1,15},{2,8},{3,9},{4,10},{5,11},{6,12},{7,13},{8,22},{9,23... | collective-permute-start | bytes 786440 | tf_op jit(solution)/shard_map/ppermute | solution.py:587
  64.8 1.5 %collective-permute-start.18 = (bf16[128,1024]{1,0:T(8,128)(2,1)S(1)}, bf16[128,1024]{1,0:T(8,128)(2,1)S(1)}, u32[]{:S(2)}, u32[]{:S(2)}) collective-permute-start(bf16[128,1024]{1,0:T(8,128)(2,1)S(1)} %get-tuple-element.50), channel_id=1, source_target_pairs={{0,8},{1,9},{2,10},{3,11},{4,12},{5,13},{6,14},{7,15},{8,16},{9,17... | collective-permute-start | bytes 786440 | tf_op jit(solution)/shard_map/ppermute | solution.py:587
  66.3 4.6 %collective-permute-done.15 = bf16[128,1024]{1,0:T(8,128)(2,1)S(1)} collective-permute-done((bf16[128,1024]{1,0:T(8,128)(2,1)S(1)}, bf16[128,1024]{1,0:T(8,128)(2,1)S(1)}, u32[]{:S(2)}, u32[]{:S(2)}) %collective-permute-start.15) | collective-permute-done | bytes 262176 | tf_op jit(solution)/shard_map/ppermute | solution.py:530
  70.9 1.7 %collective-permute-start.16 = (bf16[128,1024]{1,0:T(8,128)(2,1)S(1)}, bf16[128,1024]{1,0:T(8,128)(2,1)S(1)}, u32[]{:S(2)}, u32[]{:S(2)}) collective-permute-start(bf16[128,1024]{1,0:T(8,128)(2,1)S(1)} %add.34), channel_id=1, source_target_pairs={{0,10},{1,11},{2,12},{3,13},{4,14},{5,15},{6,8},{7,9},{8,18},{9,19... | collective-permute-start | bytes 786440 | tf_op jit(solution)/shard_map/ppermute | solution.py:587
  72.6 5.6 %collective-permute-done.17 = bf16[128,1024]{1,0:T(8,128)(2,1)S(1)} collective-permute-done((bf16[128,1024]{1,0:T(8,128)(2,1)S(1)}, bf16[128,1024]{1,0:T(8,128)(2,1)S(1)}, u32[]{:S(2)}, u32[]{:S(2)}) %collective-permute-start.17) | collective-permute-done | bytes 262176 | tf_op jit(solution)/shard_map/ppermute | solution.py:587
  78.2 6.5 %collective-permute-done.18 = bf16[128,1024]{1,0:T(8,128)(2,1)S(1)} collective-permute-done((bf16[128,1024]{1,0:T(8,128)(2,1)S(1)}, bf16[128,1024]{1,0:T(8,128)(2,1)S(1)}, u32[]{:S(2)}, u32[]{:S(2)}) %collective-permute-start.18) | collective-permute-done | bytes 262176 | tf_op jit(solution)/shard_map/ppermute | solution.py:587
  84.7 0.7 add_bitcast_fusion
  (50 shorter events, 0.7 us)
Async XLA Ops:
  0.0 4.8 %copy-start = (bf16[1,1024,8]{1,2,0:T(8,128)(2,1)S(1)}, bf16[1,1024,8]{1,2,0:T(8,128)(2,1)}, u32[]{:S(2)}) copy-start(bf16[1,1024,8]{1,2,0:T(8,128)(2,1)} %param.17) | copy-start | bytes 49156
  0.0 1.0 %copy-start.2 = (bf16[1,128,1024]{2,1,0:T(8,128)(2,1)S(1)}, bf16[1,128,1024]{2,1,0:T(8,128)(2,1)}, u32[]{:S(2)}) copy-start(bf16[1,128,1024]{2,1,0:T(8,128)(2,1)} %param.12) | copy-start | bytes 786436
  1.8 6.9 %copy-start.6 = (f32[1,1024]{1,0:T(1,128)S(1)}, f32[1,1024]{1,0:T(1,128)}, u32[]{:S(2)}) copy-start(f32[1,1024]{1,0:T(1,128)} %refs_12_.1) | copy-start | bytes 12292
  1.8 12.5 %collective-permute-start.1 = (bf16[1056,128]{1,0:T(8,128)(2,1)S(1)}, bf16[1056,128]{1,0:T(8,128)(2,1)S(1)}, u32[]{:S(2)}, u32[]{:S(2)}) collective-permute-start(bf16[1056,128]{1,0:T(8,128)(2,1)S(1)} %attach_decay.1.left_ref.refs_0_), channel_id=1, source_target_pairs={{0,2},{1,3},{2,4},{3,5},{4,6},{5,7},{6,0},{7,1},{8,10},{9,11},{10,... | collective-permute-start | bytes 811016 | tf_op jit(solution)/shard_map/ppermute | solution.py:530
  4.8 1.6 %collective-permute-start = (bf16[1056,128]{1,0:T(8,128)(2,1)S(1)}, bf16[1056,128]{1,0:T(8,128)(2,1)S(1)}, u32[]{:S(2)}, u32[]{:S(2)}) collective-permute-start(bf16[1056,128]{1,0:T(8,128)(2,1)S(1)} %attach_decay.1.left_ref.refs_0_), channel_id=1, source_target_pairs={{0,1},{1,0},{2,3},{3,2},{4,5},{5,4},{6,7},{7,6},{8,9},{9,8},{10,11... | collective-permute-start | bytes 811016 | tf_op jit(solution)/shard_map/ppermute | solution.py:534
  6.4 12.7 %collective-permute-start.3 = (bf16[1056,128]{1,0:T(8,128)(2,1)S(1)}, bf16[1056,128]{1,0:T(8,128)(2,1)S(1)}, u32[]{:S(2)}, u32[]{:S(2)}) collective-permute-start(bf16[1056,128]{1,0:T(8,128)(2,1)S(1)} %attach_decay.1.left_ref.refs_0_), channel_id=1, source_target_pairs={{0,6},{1,7},{2,0},{3,1},{4,2},{5,3},{6,4},{7,5},{8,14},{9,15},{10,... | collective-permute-start | bytes 811016 | tf_op jit(solution)/shard_map/ppermute | solution.py:530
  14.2 5.0 %collective-permute-start.2 = (bf16[1056,128]{1,0:T(8,128)(2,1)S(1)}, bf16[1056,128]{1,0:T(8,128)(2,1)S(1)}, u32[]{:S(2)}, u32[]{:S(2)}) collective-permute-start(bf16[1056,128]{1,0:T(8,128)(2,1)S(1)} %collective-permute-done.1.left_ref.refs_2_), channel_id=1, source_target_pairs={{0,1},{1,0},{2,3},{3,2},{4,5},{5,4},{6,7},{7,6},{8,9},{9,8},{10,11... | collective-permute-start | bytes 811016 | tf_op jit(solution)/shard_map/ppermute | solution.py:551
  14.2 12.8 %collective-permute-start.5 = (bf16[1056,128]{1,0:T(8,128)(2,1)S(1)}, bf16[1056,128]{1,0:T(8,128)(2,1)S(1)}, u32[]{:S(2)}, u32[]{:S(2)}) collective-permute-start(bf16[1056,128]{1,0:T(8,128)(2,1)S(1)} %collective-permute-done.1.left_ref.refs_2_), channel_id=1, source_target_pairs={{0,2},{1,3},{2,4},{3,5},{4,6},{5,7},{6,0},{7,1},{8,10},{9,11},{10,... | collective-permute-start | bytes 811016 | tf_op jit(solution)/shard_map/ppermute | solution.py:530
  19.1 2.6 %collective-permute-start.4 = (bf16[1056,128]{1,0:T(8,128)(2,1)S(1)}, bf16[1056,128]{1,0:T(8,128)(2,1)S(1)}, u32[]{:S(2)}, u32[]{:S(2)}) collective-permute-start(bf16[1056,128]{1,0:T(8,128)(2,1)S(1)} %collective-permute-done.3.left_ref.refs_4_), channel_id=1, source_target_pairs={{0,1},{1,0},{2,3},{3,2},{4,5},{5,4},{6,7},{7,6},{8,9},{9,8},{10,11... | collective-permute-start | bytes 811016 | tf_op jit(solution)/shard_map/ppermute | solution.py:553
  21.7 6.9 %copy-start.5 = (s32[1,8,1]{1,2,0:T(1,128)S(1)}, s32[1,8,1]{1,2,0:T(1,128)}, u32[]{:S(2)}) copy-start(s32[1,8,1]{1,2,0:T(1,128)} %param.14) | copy-start | bytes 100
  21.7 6.9 %copy-start.7 = (f32[1,128]{1,0:T(1,128)S(1)}, f32[1,128]{1,0:T(1,128)}, u32[]{:S(2)}) copy-start(f32[1,128]{1,0:T(1,128)} %out_gain_ref.1) | copy-start | bytes 1540
  27.1 1.5 %collective-permute-start.6 = (bf16[1056,128]{1,0:T(8,128)(2,1)S(1)}, bf16[1056,128]{1,0:T(8,128)(2,1)S(1)}, u32[]{:S(2)}, u32[]{:S(2)}) collective-permute-start(bf16[1056,128]{1,0:T(8,128)(2,1)S(1)} %collective-permute-done.5.refs_14_.refs_6_), channel_id=1, source_target_pairs={{0,1},{1,0},{2,3},{3,2},{4,5},{5,4},{6,7},{7,6},{8,9},{9,8},{10,11... | collective-permute-start | bytes 811016 | tf_op jit(solution)/shard_map/ppermute | solution.py:556
  28.6 19.4 %slice-start = ((s8[8388608]{0:T(1024)(128)(4,1)}), s8[4194304]{0:T(1024)(128)(4,1)S(1)}, s32[]{:S(2)}) async-start(s8[8388608]{0:T(1024)(128)(4,1)} %bitcast.14), calls=%async_computation | async-start | bytes 8388608
  28.6 19.4 %slice-start.2 = ((s8[8388608]{0:T(1024)(128)(4,1)}), s8[4194304]{0:T(1024)(128)(4,1)S(1)}, s32[]{:S(2)}) async-start(s8[8388608]{0:T(1024)(128)(4,1)} %bitcast.16), calls=%async_computation.2 | async-start | bytes 8388608
  28.6 19.4 %slice-start.4 = ((s8[8388608]{0:T(1024)(128)(4,1)}), s8[4194304]{0:T(1024)(128)(4,1)S(1)}, s32[]{:S(2)}) async-start(s8[8388608]{0:T(1024)(128)(4,1)} %bitcast.18), calls=%async_computation.4 | async-start | bytes 8388608
  28.6 19.4 %slice-start.1 = ((s8[8388608]{0:T(1024)(128)(4,1)}), s8[4194304]{0:T(1024)(128)(4,1)S(1)}, s32[]{:S(2)}) async-start(s8[8388608]{0:T(1024)(128)(4,1)} %bitcast.14), calls=%async_computation.1 | async-start | bytes 8388608
  28.6 19.4 %slice-start.3 = ((s8[8388608]{0:T(1024)(128)(4,1)}), s8[4194304]{0:T(1024)(128)(4,1)S(1)}, s32[]{:S(2)}) async-start(s8[8388608]{0:T(1024)(128)(4,1)} %bitcast.16), calls=%async_computation.3 | async-start | bytes 8388608
  28.7 19.4 %slice-start.5 = ((s8[8388608]{0:T(1024)(128)(4,1)}), s8[4194304]{0:T(1024)(128)(4,1)S(1)}, s32[]{:S(2)}) async-start(s8[8388608]{0:T(1024)(128)(4,1)} %bitcast.18), calls=%async_computation.5 | async-start | bytes 8388608
  28.7 19.4 %copy-start.1 = (bf16[1,1024,1024]{2,1,0:T(8,128)(2,1)S(1)}, bf16[1,1024,1024]{2,1,0:T(8,128)(2,1)}, u32[]{:S(2)}) copy-start(bf16[1,1024,1024]{2,1,0:T(8,128)(2,1)} %param.19) | copy-start | bytes 6291460
  28.7 19.4 %copy-start.4 = (f32[1,1024]{1,0:T(1,128)S(1)}, f32[1,1024]{1,0:T(1,128)}, u32[]{:S(2)}) copy-start(f32[1,1024]{1,0:T(1,128)} %gain_ref.7) | copy-start | bytes 12292
  33.4 7.5 %collective-permute-start.8 = (bf16[2,2,128,128]{3,2,1,0:T(8,128)(2,1)S(1)}, bf16[2,2,128,128]{3,2,1,0:T(8,128)(2,1)S(1)}, u32[]{:S(2)}, u32[]{:S(2)}) collective-permute-start(bf16[2,2,128,128]{3,2,1,0:T(8,128)(2,1)S(1)} %get-tuple-element.44), channel_id=1, source_target_pairs={{0,2},{1,3},{2,0},{3,1},{4,6},{5,7},{6,4},{7,5},{8,10},{9,11},{10,... | collective-permute-start | bytes 393224 | tf_op jit(solution)/shard_map/ppermute | solution.py:563
  33.5 13.0 %collective-permute-start.10 = (bf16[2,2,128,128]{3,2,1,0:T(8,128)(2,1)S(1)}, bf16[2,2,128,128]{3,2,1,0:T(8,128)(2,1)S(1)}, u32[]{:S(2)}, u32[]{:S(2)}) collective-permute-start(bf16[2,2,128,128]{3,2,1,0:T(8,128)(2,1)S(1)} %get-tuple-element.45), channel_id=1, source_target_pairs={{0,4},{1,5},{2,6},{3,7},{4,0},{5,1},{6,2},{7,3},{8,12},{9,13},{10,... | collective-permute-start | bytes 393224 | tf_op jit(solution)/shard_map/ppermute | solution.py:563
  35.8 10.7 %collective-permute-start.12 = (bf16[2,2,128,128]{3,2,1,0:T(8,128)(2,1)S(1)}, bf16[2,2,128,128]{3,2,1,0:T(8,128)(2,1)S(1)}, u32[]{:S(2)}, u32[]{:S(2)}) collective-permute-start(bf16[2,2,128,128]{3,2,1,0:T(8,128)(2,1)S(1)} %get-tuple-element.46), channel_id=1, source_target_pairs={{0,6},{1,7},{2,4},{3,5},{4,2},{5,3},{6,0},{7,1},{8,14},{9,15},{10,... | collective-permute-start | bytes 393224 | tf_op jit(solution)/shard_map/ppermute | solution.py:563
  37.9 9.1 %collective-permute-start.7 = (bf16[2,2,128,128]{3,2,1,0:T(8,128)(2,1)S(1)}, bf16[2,2,128,128]{3,2,1,0:T(8,128)(2,1)S(1)}, u32[]{:S(2)}, u32[]{:S(2)}) collective-permute-start(bf16[2,2,128,128]{3,2,1,0:T(8,128)(2,1)S(1)} %get-tuple-element.43.refs_8_), channel_id=1, source_target_pairs={{0,1},{1,0},{2,3},{3,2},{4,5},{5,4},{6,7},{7,6},{8,9},{9,8},{10,11... | collective-permute-start | bytes 393224 | tf_op jit(solution)/shard_map/ppermute | solution.py:566
  41.0 6.0 %collective-permute-start.9 = (bf16[2,2,128,128]{3,2,1,0:T(8,128)(2,1)S(1)}, bf16[2,2,128,128]{3,2,1,0:T(8,128)(2,1)S(1)}, u32[]{:S(2)}, u32[]{:S(2)}) collective-permute-start(bf16[2,2,128,128]{3,2,1,0:T(8,128)(2,1)S(1)} %collective-permute-done.8.refs_10_), channel_id=1, source_target_pairs={{0,1},{1,0},{2,3},{3,2},{4,5},{5,4},{6,7},{7,6},{8,9},{9,8},{10,11... | collective-permute-start | bytes 393224 | tf_op jit(solution)/shard_map/ppermute | solution.py:566
  46.5 1.3 %collective-permute-start.11 = (bf16[2,2,128,128]{3,2,1,0:T(8,128)(2,1)S(1)}, bf16[2,2,128,128]{3,2,1,0:T(8,128)(2,1)S(1)}, u32[]{:S(2)}, u32[]{:S(2)}) collective-permute-start(bf16[2,2,128,128]{3,2,1,0:T(8,128)(2,1)S(1)} %collective-permute-done.10.refs_12_), channel_id=1, source_target_pairs={{0,1},{1,0},{2,3},{3,2},{4,5},{5,4},{6,7},{7,6},{8,9},{9,8},{10,11... | collective-permute-start | bytes 393224 | tf_op jit(solution)/shard_map/ppermute | solution.py:566
  46.5 1.5 %collective-permute-start.13 = (bf16[2,2,128,128]{3,2,1,0:T(8,128)(2,1)S(1)}, bf16[2,2,128,128]{3,2,1,0:T(8,128)(2,1)S(1)}, u32[]{:S(2)}, u32[]{:S(2)}) collective-permute-start(bf16[2,2,128,128]{3,2,1,0:T(8,128)(2,1)S(1)} %collective-permute-done.12.refs_14_), channel_id=1, source_target_pairs={{0,1},{1,0},{2,3},{3,2},{4,5},{5,4},{6,7},{7,6},{8,9},{9,8},{10,11... | collective-permute-start | bytes 393224 | tf_op jit(solution)/shard_map/ppermute | solution.py:566
  57.0 2.0 %collective-permute-start.14 = (bf16[256,1024]{1,0:T(8,128)(2,1)S(1)}, bf16[256,1024]{1,0:T(8,128)(2,1)S(1)}, u32[]{:S(2)}, u32[]{:S(2)}) collective-permute-start(bf16[256,1024]{1,0:T(8,128)(2,1)S(1)} %expert.1.own_ref), channel_id=1, source_target_pairs={{0,1},{1,0},{2,3},{3,2},{4,5},{5,4},{6,7},{7,6},{8,9},{9,8},{10,11... | collective-permute-start | bytes 1572872 | tf_op jit(solution)/shard_map/ppermute | solution.py:589
  59.8 11.0 %collective-permute-start.15 = (bf16[128,1024]{1,0:T(8,128)(2,1)S(1)}, bf16[128,1024]{1,0:T(8,128)(2,1)S(1)}, u32[]{:S(2)}, u32[]{:S(2)}) collective-permute-start(bf16[128,1024]{1,0:T(8,128)(2,1)S(1)} %get-tuple-element.47), channel_id=1, source_target_pairs={{0,2},{1,3},{2,4},{3,5},{4,6},{5,7},{6,0},{7,1},{8,10},{9,11},{10,... | collective-permute-start | bytes 786440 | tf_op jit(solution)/shard_map/ppermute | solution.py:530
  62.2 16.0 %collective-permute-start.17 = (bf16[128,1024]{1,0:T(8,128)(2,1)S(1)}, bf16[128,1024]{1,0:T(8,128)(2,1)S(1)}, u32[]{:S(2)}, u32[]{:S(2)}) collective-permute-start(bf16[128,1024]{1,0:T(8,128)(2,1)S(1)} %get-tuple-element.49), channel_id=1, source_target_pairs={{0,14},{1,15},{2,8},{3,9},{4,10},{5,11},{6,12},{7,13},{8,22},{9,23... | collective-permute-start | bytes 786440 | tf_op jit(solution)/shard_map/ppermute | solution.py:587
  64.8 19.9 %collective-permute-start.18 = (bf16[128,1024]{1,0:T(8,128)(2,1)S(1)}, bf16[128,1024]{1,0:T(8,128)(2,1)S(1)}, u32[]{:S(2)}, u32[]{:S(2)}) collective-permute-start(bf16[128,1024]{1,0:T(8,128)(2,1)S(1)} %get-tuple-element.50), channel_id=1, source_target_pairs={{0,8},{1,9},{2,10},{3,11},{4,12},{5,13},{6,14},{7,15},{8,16},{9,17... | collective-permute-start | bytes 786440 | tf_op jit(solution)/shard_map/ppermute | solution.py:587
  70.9 13.8 %collective-permute-start.16 = (bf16[128,1024]{1,0:T(8,128)(2,1)S(1)}, bf16[128,1024]{1,0:T(8,128)(2,1)S(1)}, u32[]{:S(2)}, u32[]{:S(2)}) collective-permute-start(bf16[128,1024]{1,0:T(8,128)(2,1)S(1)} %add.34), channel_id=1, source_target_pairs={{0,10},{1,11},{2,12},{3,13},{4,14},{5,15},{6,8},{7,9},{8,18},{9,19... | collective-permute-start | bytes 786440 | tf_op jit(solution)/shard_map/ppermute | solution.py:587
  (1 other events, 0.7 us)

commit v4 on v3

--- a/solution.py
+++ b/solution.py
@@ -13,6 +13,7 @@
 CORES = 2
 CAP = 2
 PARTS = 3
+HOPS = (0, 3, 1, 2)
 EXTRA = 32
 F32 = jnp.float32
 BF16 = jnp.bfloat16
@@ -207,7 +208,7 @@
 def arrivals(chip, core):
     return [
         jnp.bitwise_and(chip + hop, CHIPS - 1) * CORES + (core if side == 0 else 1 - core)
-        for hop in (0, 3, 1, 2)
+        for hop in HOPS
         for side in (0, 1)
     ]
 
@@ -229,8 +230,18 @@
         [both[:BLOCK], both[BLOCK:]],
         [running_decay(ref[columns * BLOCK :, :], head, columns) for ref in x_refs],
     )
-    for i in range(len(x_refs)):
-        put(i, reads[i].astype(BF16), local[i], step[i], jnp.broadcast_to(fade[i], (8, BLOCK)))
+    for i, spot in ((0, core), (1, 1 - core)):
+        put((0, 1), spot, reads[i].astype(BF16), local[i])
+    ahead = core == 0
+    step = [jnp.where(ahead, step[0], step[1]), jnp.where(ahead, step[1], step[0])]
+    fade = [jnp.where(ahead, fade[0], fade[1]), jnp.where(ahead, fade[1], fade[0])]
+    first, second = step
+    cross = mm3(halves(first), halves(second[:BLOCK]))
+    both_move = fade[1] * first[:BLOCK] + fade[0] * second[:BLOCK] - cross[:BLOCK]
+    both_add = fade[1] * first[BLOCK:] - cross[BLOCK:] + second[BLOCK:]
+    put((2, 3), 0, first, jnp.broadcast_to(fade[0], (8, BLOCK)))
+    both_step = jnp.concatenate([both_move, both_add], axis=0)
+    put((2, 3), 1, both_step, jnp.broadcast_to(fade[0] * fade[1], (8, BLOCK)))
 
 
 def term_scratch(count, width):
@@ -249,9 +260,9 @@
 def terms_kernel(gain_ref, weight_ref, left_ref, right_ref, *refs):
     outs, scratch = refs[:4], refs[4:]
 
-    def put(j, *values):
-        for ref, value in zip(outs, values):
-            ref[j] = value
+    def put(which, spot, *values):
+        for n, value in zip(which, values):
+            outs[n][spot] = value
 
     pair_terms(gain_ref, weight_ref, (left_ref, right_ref), *scratch, put)
 
@@ -274,11 +285,10 @@
     )(gain, weight, *blocks)
 
 
-def mix_kernel(counts, late, kinds_ref, out_gain_ref, *refs):
+def mix_kernel(pairs, late, kinds_ref, out_gain_ref, *refs):
     base, chip, core = where_am_i()
-    blocks = arrivals(chip, core)
-    groups = [refs[4 * g : 4 * g + 4] for g in range(len(counts))]
-    refs = refs[4 * len(counts) :]
+    groups = [refs[4 * g : 4 * g + 4] for g in range(pairs)]
+    refs = refs[4 * pairs :]
     if late:
         gain_ref, weight_ref, left_ref, right_ref = refs[:4]
         refs = refs[4:]
@@ -286,30 +296,36 @@
         start_ref, refs = refs[0], refs[1:]
     outs, refs = refs[:CHIPS], refs[CHIPS:]
     scr, on_scr, refs = refs[:4], refs[4], refs[5:]
-    at = 0
-    for group, count in zip(groups, counts):
-        for j in range(count):
-            for ref, keep in zip(group, scr):
-                keep[blocks[at]] = ref[j]
-            at += 1
+    for group, hop in zip(groups, HOPS):
+        spot = jnp.bitwise_and(chip + hop, CHIPS - 1) * CORES
+        for ref, keep in zip(group, scr):
+            for i in range(CORES):
+                keep[spot + i] = ref[i]
     if late:
-
-        def put(j, *values):
-            for ref, value in zip(scr, values):
-                ref[blocks[at + j]] = value
+        late_spot = jnp.bitwise_and(chip + HOPS[-1], CHIPS - 1) * CORES
+
+        def put(which, spot, *values):
+            for n, value in zip(which, values):
+                scr[n][late_spot + spot] = value
 
         pair_terms(gain_ref, weight_ref, (left_ref, right_ref), *refs, put)
     reads_scr, local_scr, step_scr, fade_scr = scr
     state = jnp.zeros((BLOCK, BLOCK), F32) if late else start_ref[...]
     out_gain = out_gain_ref[...]
-    for b in range(EXPERTS):
+
+    def after(split, state, at):
+        move = step_scr[at]
+        return fade_scr[at][0:1, :] * state - mm3(split, halves(move[:BLOCK])) + move[BLOCK:]
+
+    for c in range(CHIPS):
+        at = c * CORES
         split = halves(state)
-        move = step_scr[b]
-        mixed = mm(reads_scr[b], split[0], ((1,), (1,))) + local_scr[b]
-        on_scr[b] = normed(mixed, out_gain)
-        if b + 1 < EXPERTS:
-            erase = mm3(split, halves(move[:BLOCK]))
-            state = fade_scr[b][0:1, :] * state - erase + move[BLOCK:]
+        between = after(split, state, at)
+        if c + 1 < CHIPS:
+            state = after(split, state, at + 1)
+        for b, before in ((at, split[0]), (at + 1, between.astype(BF16))):
+            mixed = mm(reads_scr[b], before, ((1,), (1,))) + local_scr[b]
+            on_scr[b] = normed(mixed, out_gain)
     kinds, ranks = routes(kinds_ref, base)
     for k in range(CHIPS):
         there = jnp.bitwise_xor(chip, k)
@@ -320,13 +336,12 @@
 
 
 def mix(kinds, out_gain, groups, start=None, late=()):
-    counts = tuple(g[0].shape[0] for g in groups)
     vmem = pl.BlockSpec(memory_space=pltpu.VMEM)
     extra = list(late) if late else [start]
     operands = [kinds, out_gain] + [a for g in groups for a in g] + extra
     sent = jax.ShapeDtypeStruct((CORES, CAP, BLOCK, BLOCK), BF16)
     return pl.pallas_call(
-        partial(mix_kernel, counts, bool(late)),
+        partial(mix_kernel, len(groups), bool(late)),
         out_shape=(sent,) * CHIPS,
         in_specs=[pl.BlockSpec(memory_space=pltpu.SMEM)] + [vmem] * (len(operands) - 1),
         out_specs=(vmem,) * CHIPS,
@@ -378,49 +393,80 @@
     )(kinds, own, other)
 
 
-def project(kinds_ref, gain_ref, out_weight_ref, x_refs, on_refs, x_scr, on_scr, h_ref, hn_ref, sem):
+def add_heads(half, out_weight_ref, on_refs, on_scr):
+    _, chip, core = where_am_i()
+    for k in range(CHIPS // 2):
+        there = jnp.bitwise_and(jnp.bitwise_xor(chip, k), 1)
+        for side in range(CORES):
+            head = there * CORES + (core if side == 0 else 1 - core)
+            at = pl.ds(pl.multiple_of(head * BLOCK, BLOCK), BLOCK)
+            for slot in range(CAP):
+                on_scr[slot * BLOCK : (slot + 1) * BLOCK, at] = on_refs[k * CORES + side][core, slot]
+    depth = on_scr.shape[1]
+    part = jnp.bitwise_xor(chip // 2, half)
+    rows = pl.ds(pl.multiple_of(part * depth, depth), depth)
+    return mm(on_scr[...], out_weight_ref[rows, :])
+
+
+def early_kernel(kinds_ref, out_weight_ref, *refs):
+    x_refs, on_refs = refs[:EXPERTS], refs[EXPERTS : EXPERTS + CHIPS]
+    out_ref, x_scr, on_scr, sem = refs[EXPERTS + CHIPS :]
     base, chip, core = where_am_i()
     kinds, ranks = routes(kinds_ref, base)
     found = sources(kinds, ranks, chip * CORES + core)
+    size = x_scr.shape[1]
     for slot in range(CAP):
         for block, ref in zip(arrivals(chip, core), x_refs):
 
             @pl.when(block == found[slot])
             def _():
-                rows = ref.at[pl.ds(0, x_scr.shape[1]), :]
+                rows = ref.at[pl.ds(0, size), :]
                 pltpu.make_async_copy(rows, x_scr.at[slot], sem.at[slot]).start()
 
-    for k in range(CHIPS):
-        there = jnp.bitwise_xor(chip, k)
-        for side in range(CORES):
-            head = there * CORES + (core if side == 0 else 1 - core)
-            at = pl.ds(pl.multiple_of(head * BLOCK, BLOCK), BLOCK)
-            got = on_refs[k * CORES + side]
-            for slot in range(CAP):
-                on_scr[slot * BLOCK : (slot + 1) * BLOCK, at] = got[core, slot]
+    added = add_heads(0, out_weight_ref, on_refs, on_scr)
     for slot in range(CAP):
         rows = slice(slot * BLOCK, (slot + 1) * BLOCK)
-        added = mm(on_scr[rows, :], out_weight_ref[...])
-        rows_of_x = x_refs[0].at[pl.ds(0, x_scr.shape[1]), :]
-        pltpu.make_async_copy(rows_of_x, x_scr.at[slot], sem.at[slot]).wait()
-        hidden = (rows_of(x_scr.at[slot]).astype(F32) + added).astype(BF16)
-        h_ref[rows, :] = hidden
-        hn_ref[rows, :] = normed(hidden, gain_ref[...])
-
-
-def project_kernel(kinds_ref, gain_ref, out_weight_ref, *refs):
-    x_refs, on_refs = refs[:EXPERTS], refs[EXPERTS : 2 * EXPERTS]
-    h_ref, hn_ref, x_scr, on_scr, sem = refs[2 * EXPERTS :]
-    project(kinds_ref, gain_ref, out_weight_ref, x_refs, on_refs, x_scr, on_scr, h_ref, hn_ref, sem)
-
-
-def expert_kernel(tile, kinds_ref, gain_ref, out_weight_ref, *refs):
-    x_refs, on_refs = refs[:EXPERTS], refs[EXPERTS : 2 * EXPERTS]
-    gate_ref, up_ref, down_ref, out_ref = refs[2 * EXPERTS : 2 * EXPERTS + 4]
-    x_scr, on_scr, h_scr, hn_scr, act_scr, sem = refs[2 * EXPERTS + 4 :]
-    project(
-        kinds_ref, gain_ref, out_weight_ref, x_refs, on_refs, x_scr, on_scr, h_scr, hn_scr, sem
-    )
+        pltpu.make_async_copy(x_refs[0].at[pl.ds(0, size), :], x_scr.at[slot], sem.at[slot]).wait()
+        out_ref[rows, :] = rows_of(x_scr.at[slot]).astype(F32) + added[rows]
+
+
+def early_project(kinds, out_weight, blocks, ons):
+    rows, width = CAP * BLOCK, out_weight.shape[1]
+    vmem = pl.BlockSpec(memory_space=pltpu.VMEM)
+    return pl.pallas_call(
+        early_kernel,
+        out_shape=jax.ShapeDtypeStruct((rows, width), F32),
+        in_specs=[pl.BlockSpec(memory_space=pltpu.SMEM), vmem]
+        + [pl.BlockSpec(memory_space=pl.ANY)] * EXPERTS
+        + [vmem] * len(ons),
+        out_specs=vmem,
+        scratch_shapes=[
+            pltpu.VMEM((CAP, width, BLOCK), BF16),
+            pltpu.VMEM((rows, width // 2), BF16),
+            pltpu.SemaphoreType.DMA((CAP,)),
+        ],
+        compiler_params=pltpu.CompilerParams(vmem_limit_bytes=VMEM_LIMIT),
+        cost_estimate=pl.CostEstimate(flops=0, bytes_accessed=0, transcendentals=0),
+        name="early_project",
+    )(kinds, out_weight, *blocks, *ons)
+
+
+def project(gain_ref, out_weight_ref, early_ref, on_refs, on_scr, h_ref, hn_ref):
+    hidden = (early_ref[...] + add_heads(1, out_weight_ref, on_refs, on_scr)).astype(BF16)
+    h_ref[...] = hidden
+    hn_ref[...] = normed(hidden, gain_ref[...])
+
+
+def project_kernel(gain_ref, out_weight_ref, early_ref, *refs):
+    h_ref, hn_ref, on_scr = refs[CHIPS:]
+    project(gain_ref, out_weight_ref, early_ref, refs[:CHIPS], on_scr, h_ref, hn_ref)
+
+
+def expert_kernel(tile, gain_ref, out_weight_ref, early_ref, *refs):
+    on_refs = refs[:CHIPS]
+    gate_ref, up_ref, down_ref, out_ref = refs[CHIPS : CHIPS + 4]
+    on_scr, h_scr, hn_scr, act_scr = refs[CHIPS + 4 :]
+    project(gain_ref, out_weight_ref, early_ref, on_refs, on_scr, h_scr, hn_scr)
     rows = hn_scr[...]
     for at in range(0, gate_ref.shape[3], tile):
         part = slice(at, at + tile)
@@ -434,62 +480,52 @@
         out_ref[:, part] = (h_scr[:, part].astype(F32) + ffn).astype(BF16)
 
 
-def expert(kinds, gain, out_weight, blocks, ons, gate, up, down):
-    rows, width = CAP * BLOCK, gain.shape[1]
+def expert(gain, out_weight, early, ons, gate, up, down):
+    rows, width = early.shape
     vmem = pl.BlockSpec(memory_space=pltpu.VMEM)
     return pl.pallas_call(
         partial(expert_kernel, min(512, gate.shape[3])),
         out_shape=jax.ShapeDtypeStruct((rows, width), BF16),
-        in_specs=[pl.BlockSpec(memory_space=pltpu.SMEM), vmem, vmem]
-        + [pl.BlockSpec(memory_space=pl.ANY)] * EXPERTS
-        + [vmem] * (EXPERTS + 3),
+        in_specs=[vmem] * (len(ons) + 6),
         out_specs=vmem,
         scratch_shapes=[
-            pltpu.VMEM((CAP, width, BLOCK), BF16),
-            pltpu.VMEM((rows, width), BF16),
+            pltpu.VMEM((rows, width // 2), BF16),
             pltpu.VMEM((rows, width), BF16),
             pltpu.VMEM((rows, width), BF16),
             pltpu.VMEM((rows, gate.shape[3]), BF16),
-            pltpu.SemaphoreType.DMA((CAP,)),
         ],
         compiler_params=pltpu.CompilerParams(vmem_limit_bytes=VMEM_LIMIT),
         name="expert",
-    )(kinds, gain, out_weight, *blocks, *ons, gate, up, down)
-
-
-def project_only(kinds, gain, out_weight, blocks, ons):
-    rows, width = CAP * BLOCK, gain.shape[1]
+    )(gain, out_weight, early, *ons, gate, up, down)
+
+
+def project_only(gain, out_weight, early, ons):
+    rows, width = early.shape
     vmem = pl.BlockSpec(memory_space=pltpu.VMEM)
     return pl.pallas_call(
         project_kernel,
         out_shape=(jax.ShapeDtypeStruct((rows, width), BF16),) * 2,
-        in_specs=[pl.BlockSpec(memory_space=pltpu.SMEM), vmem, vmem]
-        + [pl.BlockSpec(memory_space=pl.ANY)] * EXPERTS
-        + [vmem] * EXPERTS,
+        in_specs=[vmem] * (len(ons) + 3),
         out_specs=(vmem, vmem),
-        scratch_shapes=[
-            pltpu.VMEM((CAP, width, BLOCK), BF16),
-            pltpu.VMEM((rows, width), BF16),
-            pltpu.SemaphoreType.DMA((CAP,)),
-        ],
+        scratch_shapes=[pltpu.VMEM((rows, width // 2), BF16)],
         compiler_params=pltpu.CompilerParams(vmem_limit_bytes=VMEM_LIMIT),
         name="project",
-    )(kinds, gain, out_weight, *blocks, *ons)
+    )(gain, out_weight, early, *ons)
 
 
 def group_start(place, count, groups_of_terms):
     groups = count // EXPERTS
     ein = partial(jnp.einsum, precision=lax.Precision.HIGHEST)
     eye = jnp.eye(BLOCK, dtype=F32)
-    step = jnp.concatenate([g[2] for g in groups_of_terms], axis=0)
-    fade = jnp.concatenate([g[3] for g in groups_of_terms], axis=0)
-    inner = place % EXPERTS
-    order = jnp.argsort(jnp.stack(arrivals(inner // CORES, inner % CORES)))
+    step = jnp.stack([g[2][1] for g in groups_of_terms], axis=0)
+    fade = jnp.stack([g[3][1] for g in groups_of_terms], axis=0)
+    chip = place % EXPERTS // CORES
+    order = jnp.argsort((chip + jnp.array(HOPS)) % CHIPS)
     step, fade = jnp.take(step, order, axis=0), jnp.take(fade, order, axis=0)
     moves = fade[:, 0, :][:, None, :] * eye - step[:, :BLOCK]
     adds = step[:, BLOCK:]
     total, added = moves[0], adds[0]
-    for b in range(1, EXPERTS):
+    for b in range(1, CHIPS):
         total, added = ein("ij,jk->ik", total, moves[b]), ein("vk,kj->vj", added, moves[b]) + adds[b]
     peers = [[g * EXPERTS + e for g in range(groups)] for e in range(EXPERTS)]
     gather = partial(lax.all_gather, axis_name="seq", axis_index_groups=peers)
@@ -531,9 +567,8 @@
 
     own = attach(held[0], log_decay[0].T)
     left = hop(own, 1)
+    right = hop(own, -1)
     own_other = pair(own)
-    later, _ = lax.optimization_barrier((own, own_other))
-    right = hop(later, -1)
 
     def head_columns(at):
         return lax.dynamic_slice_in_dim(qkv_weight[0], at * width + inner * BLOCK, BLOCK, 1)
@@ -546,8 +581,9 @@
     )
 
     known = [terms(norm_gain, weight, (own, own_other))]
-    left, _ = lax.optimization_barrier((left, known[0][0]))
-    far = hop(left, 1)
+    right, _ = lax.optimization_barrier((right, known[0][0]))
+    far = hop(right, -1)
+    left, _ = lax.optimization_barrier((left, right))
     near = [(own, own_other), (left, pair(left))]
     known.append(terms(norm_gain, weight, near[1]))
     near.append((right, pair(right)))
@@ -561,17 +597,17 @@
         sends = mix(kinds, out_gain, known, late=(norm_gain, weight, *last))
 
     got = [sends[0]] + [lax.ppermute(sends[k], "seq", chip_route(count, k)) for k in range(1, CHIPS)]
-    ons = []
-    for block in got:
-        ons += [block, pair(block)]
     blocks = [block for two in near + [last] for block in two]
+    near_heads = [got[0], pair(got[0]), got[1], pair(got[1])]
+    early = early_project(kinds, out_weight[0], blocks, near_heads)
+    far_heads = [got[2], pair(got[2]), got[3], pair(got[3])]
 
     if groups == 1:
         finished = expert(
-            kinds, ffn_gain, out_weight[0], blocks, ons, gate_weight, up_weight, down_weight
+            ffn_gain, out_weight[0], early, far_heads, gate_weight, up_weight, down_weight
         )
     else:
-        hidden, hn = project_only(kinds, ffn_gain, out_weight[0], blocks, ons)
+        hidden, hn = project_only(ffn_gain, out_weight[0], early, far_heads)
         peers = [[g * EXPERTS + e for g in range(groups)] for e in range(EXPERTS)]
         rows = lax.all_gather(hn, "seq", axis_index_groups=peers, tiled=True)
         gate = jnp.dot(rows, gate_weight[0, 0], preferred_element_type=F32)

time: 85.6 us -> 83.3 us (0.973)
  waiting for transfers between devices: 40.3 us -> 34.5 us
  starting transfers between devices: 18.9 us -> 22.3 us
    ppermute x4, waiting for transfers between devices: 15.5 us -> 9.14 us  [hop(): return lax.ppermute(block, 'seq', lane_route(count, by))]
    ppermute x4, starting transfers between devices: 7.71 us -> 11.6 us  [hop(): return lax.ppermute(block, 'seq', lane_route(count, by))]
    pallas_call x1, Pallas kernels: 8.9 us -> 7.37 us  [expert(): pl.pallas_call(partial(expert_kernel, min(512, gate.shape[3])), out_shape...]
    ppermute x3, waiting for transfers between devices: 8.59 us -> 9.93 us  [per_device(): lax.ppermute(sends[k], 'seq', chip_route(count, k))]
    ppermute x4, waiting for transfers between devices: 1.02 us -> 0.01 us  [the longest x2 0.01 us: per_device(): near_heads = [got[0], pair(got[0]), got[1], pair(got[1])]]
    pallas_call x1 -> x2, Pallas kernels: 4.75 us -> 5.76 us  [the longest x1 4.28 us: mix(): pl.pallas_call(partial(mix_kernel, len(groups), bool(late)), out_shape=(s...]
  transfers between devices with their start and end apart: 19 -> 19, of which waited for: 12 -> 10; matrix products, arithmetic and copies ran while one was open for 2% -> 2% of each run, Pallas kernels for 9% -> 11%
where the time goes in v4:
time: 83.3 us; the launch traced here: 83.1 us
  waiting for transfers between devices  34.5 us (41%)
  starting transfers between devices  22.3 us (27%)
  Pallas kernels  21.9 us (26%)
  local copies, waits for them, and re-layouts  3.14 us (4%)
  other arithmetic  0.93 us (1%)
    ppermute x3, waiting for transfers between devices, send_home(): lax.ppermute(block, ('segment', 'seq'), home_route(sections, count, by))  12.3 us
    ppermute x4, starting transfers between devices, hop(): return lax.ppermute(block, 'seq', lane_route(count, by))  11.6 us
    ppermute x3, waiting for transfers between devices, per_device(): lax.ppermute(sends[k], 'seq', chip_route(count, k))  9.93 us
    ppermute x4, waiting for transfers between devices, hop(): return lax.ppermute(block, 'seq', lane_route(count, by))  9.14 us
    pallas_call x3, Pallas kernels, terms(): pl.pallas_call(terms_kernel, out_shape=tuple((jax.ShapeDtypeStruct(*s) fo...  7.9 us
    pallas_call x1, Pallas kernels, expert(): pl.pallas_call(partial(expert_kernel, min(512, gate.shape[3])), out_shape...  7.37 us
    ppermute x3, starting transfers between devices, send_home(): lax.ppermute(block, ('segment', 'seq'), home_route(sections, count, by))  5.34 us
    ppermute x3, starting transfers between devices, per_device(): lax.ppermute(sends[k], 'seq', chip_route(count, k))  4.45 us
  transfers between devices with their start and end apart: 19, of which 10 were waited for; matrix products, arithmetic and copies ran while one was open for 2% of the time, Pallas kernels for 11%

profile of v4, /device:TPU:0, one launch (start us, length us, event | category | flops | bytes accessed | tf_op | source)
XLA Modules:
  0.0 83.1 jit_solution(3831825844099800313)
XLA Ops:
  0.0 1.0 %copy-done.2 = bf16[1,128,1024]{2,1,0:T(8,128)(2,1)S(1)} copy-done((bf16[1,128,1024]{2,1,0:T(8,128)(2,1)S(1)}, bf16[1,128,1024]{2,1,0:T(8,128)(2,1)}, u32[]{:S(2)}) %copy-start.2) | copy-done | bytes 262168
  1.0 0.7 copy-done.3
  1.8 5.1 %collective-permute-start.2 = (bf16[1056,128]{1,0:T(8,128)(2,1)S(1)}, bf16[1056,128]{1,0:T(8,128)(2,1)S(1)}, u32[]{:S(2)}, u32[]{:S(2)}) collective-permute-start(bf16[1056,128]{1,0:T(8,128)(2,1)S(1)} %attach_decay.1.left_ref.refs_0_), channel_id=1, source_target_pairs={{0,6},{1,7},{2,0},{3,1},{4,2},{5,3},{6,4},{7,5},{8,14},{9,15},{10,... | collective-permute-start | bytes 811016 | tf_op jit(solution)/shard_map/ppermute | solution.py:566
  6.9 1.2 %dynamic-slice_bitcast_fusion.2 = (bf16[1024,128]{1,0:T(8,128)(2,1)S(1)}, bf16[1024,128]{1,0:T(8,128)(2,1)S(1)}, bf16[1024,128]{1,0:T(8,128)(2,1)S(1)}) fusion(bf16[1,1024,3072]{2,1,0:T(8,128)(2,1)} %param.16, s32[]{:T(128)S(6)} %select_n.20, s32[]{:T(128)S(6)} %select_n.22, s32[]{:T(128)S(6)} %select_n.21), kind=kLoop, calls=%fused_computation.4 | loop fusion | bytes 1572876 | tf_op jit(solution)/shard_map/dynamic_slice | solution.py:574
  8.4 2.6 %chunk_terms.3 = (bf16[2,128,128]{2,1,0:T(8,128)(2,1)S(1)}, f32[2,128,128]{2,1,0:T(8,128)S(1)}, f32[2,256,128]{2,1,0:T(8,128)S(1)}, f32[2,8,128]{2,1,0:T(8,128)S(1)}) custom-call(f32[1,1024]{1,0:T(1,128)S(1)} %copy-done.6, bf16[1024,512]{1,0:T(8,128)(2,1)S(1)} %pad_maximum_fusion.weight_ref.refs_13_, bf16[1056,128]{1,0:T(8,128)(2,1)S(1)} %attach_decay.1.left_ref.refs_0_, ...), custom_call_target="tpu_custom_call" | custom-call | flops 4000000000 | bytes 3000000 | tf_op jit(solution)/shard_map/chunk_terms/pallas_call | solution.py:274
  11.1 2.7 %collective-permute-done.2.left_ref.refs_4_ = bf16[1056,128]{1,0:T(8,128)(2,1)S(1)} collective-permute-done((bf16[1056,128]{1,0:T(8,128)(2,1)S(1)}, bf16[1056,128]{1,0:T(8,128)(2,1)S(1)}, u32[]{:S(2)}, u32[]{:S(2)}) %collective-permute-start.2) | collective-permute-done | bytes 270368 | tf_op jit(solution)/shard_map/ppermute | solution.py:566
  13.8 4.3 %collective-permute-start.5 = (bf16[1056,128]{1,0:T(8,128)(2,1)S(1)}, bf16[1056,128]{1,0:T(8,128)(2,1)S(1)}, u32[]{:S(2)}, u32[]{:S(2)}) collective-permute-start(bf16[1056,128]{1,0:T(8,128)(2,1)S(1)} %collective-permute-done.2.left_ref.refs_4_), channel_id=1, source_target_pairs={{0,6},{1,7},{2,0},{3,1},{4,2},{5,3},{6,4},{7,5},{8,14},{9,15},{10,... | collective-permute-start | bytes 811016 | tf_op jit(solution)/shard_map/ppermute | solution.py:566
  18.0 1.4 %collective-permute-done.1.left_ref.refs_2_ = bf16[1056,128]{1,0:T(8,128)(2,1)S(1)} collective-permute-done((bf16[1056,128]{1,0:T(8,128)(2,1)S(1)}, bf16[1056,128]{1,0:T(8,128)(2,1)S(1)}, u32[]{:S(2)}, u32[]{:S(2)}) %collective-permute-start.1) | collective-permute-done | bytes 270368 | tf_op jit(solution)/shard_map/ppermute | solution.py:566
  19.5 2.6 %chunk_terms.5 = (bf16[2,128,128]{2,1,0:T(8,128)(2,1)S(1)}, f32[2,128,128]{2,1,0:T(8,128)S(1)}, f32[2,256,128]{2,1,0:T(8,128)S(1)}, f32[2,8,128]{2,1,0:T(8,128)S(1)}) custom-call(f32[1,1024]{1,0:T(1,128)S(1)} %copy-done.6, bf16[1024,512]{1,0:T(8,128)(2,1)S(1)} %pad_maximum_fusion.weight_ref.refs_13_, ...), custom_call_target="tpu_custom_call" | custom-call | flops 4000000000 | bytes 3000000 | tf_op jit(solution)/shard_map/chunk_terms/pallas_call | solution.py:274
  22.2 2.6 %chunk_terms.4 = (bf16[2,128,128]{2,1,0:T(8,128)(2,1)S(1)}, f32[2,128,128]{2,1,0:T(8,128)S(1)}, f32[2,256,128]{2,1,0:T(8,128)S(1)}, f32[2,8,128]{2,1,0:T(8,128)S(1)}) custom-call(f32[1,1024]{1,0:T(1,128)S(1)} %copy-done.6, bf16[1024,512]{1,0:T(8,128)(2,1)S(1)} %pad_maximum_fusion.weight_ref.refs_13_, ...), custom_call_target="tpu_custom_call" | custom-call | flops 4000000000 | bytes 3000000 | tf_op jit(solution)/shard_map/chunk_terms/pallas_call | solution.py:274
  24.8 0.3 collective-permute-done.5.refs_14_.refs_6_
  25.1 0.3 collective-permute-start.6
  25.4 1.3 %collective-permute-done.6.refs_15_.refs_7_ = bf16[1056,128]{1,0:T(8,128)(2,1)S(1)} collective-permute-done((bf16[1056,128]{1,0:T(8,128)(2,1)S(1)}, bf16[1056,128]{1,0:T(8,128)(2,1)S(1)}, u32[]{:S(2)}, u32[]{:S(2)}) %collective-permute-start.6) | collective-permute-done | bytes 270368 | tf_op jit(solution)/shard_map/ppermute | solution.py:592
  26.7 4.3 %state_walk.1 = (bf16[2,2,128,128]{3,2,1,0:T(8,128)(2,1)S(1)}, bf16[2,2,128,128]{3,2,1,0:T(8,128)(2,1)S(1)}, bf16[2,2,128,128]{3,2,1,0:T(8,128)(2,1)S(1)}, bf16[2,2,128,128]{3,2,1,0:T(8,128)(2,1)S(1)}) custom-call(s32[8]{0:T(128)S(1)} %bitcast.24, f32[1,128]{1,0:T(1,128)S(1)} %copy-done.7, bf16[2,128,128]{2,1,0:T(8,128)(2,1)S(1)} %get-tuple-element.28.refs_0_, ...), custom_call_target="tpu_custom_call" | custom-call | flops 30000001024 | bytes 4000000 | tf_op jit(solution)/shard_map/state_walk/pallas_call | solution.py:343
  31.0 1.5 %collective-permute-start.8 = (bf16[2,2,128,128]{3,2,1,0:T(8,128)(2,1)S(1)}, bf16[2,2,128,128]{3,2,1,0:T(8,128)(2,1)S(1)}, u32[]{:S(2)}, u32[]{:S(2)}) collective-permute-start(bf16[2,2,128,128]{3,2,1,0:T(8,128)(2,1)S(1)} %get-tuple-element.44), channel_id=1, source_target_pairs={{0,2},{1,3},{2,0},{3,1},{4,6},{5,7},{6,4},{7,5},{8,10},{9,11},{10,... | collective-permute-start | bytes 393224 | tf_op jit(solution)/shard_map/ppermute | solution.py:599
  32.5 2.8 %collective-permute-start.10 = (bf16[2,2,128,128]{3,2,1,0:T(8,128)(2,1)S(1)}, bf16[2,2,128,128]{3,2,1,0:T(8,128)(2,1)S(1)}, u32[]{:S(2)}, u32[]{:S(2)}) collective-permute-start(bf16[2,2,128,128]{3,2,1,0:T(8,128)(2,1)S(1)} %get-tuple-element.45), channel_id=1, source_target_pairs={{0,4},{1,5},{2,6},{3,7},{4,0},{5,1},{6,2},{7,3},{8,12},{9,13},{10,... | collective-permute-start | bytes 393224 | tf_op jit(solution)/shard_map/ppermute | solution.py:599
  35.2 0.2 collective-permute-start.12
  35.5 3.4 %collective-permute-done.8.refs_10_ = bf16[2,2,128,128]{3,2,1,0:T(8,128)(2,1)S(1)} collective-permute-done((bf16[2,2,128,128]{3,2,1,0:T(8,128)(2,1)S(1)}, bf16[2,2,128,128]{3,2,1,0:T(8,128)(2,1)S(1)}, u32[]{:S(2)}, u32[]{:S(2)}) %collective-permute-start.8) | collective-permute-done | bytes 131104 | tf_op jit(solution)/shard_map/ppermute | solution.py:599
  38.9 6.5 %collective-permute-done.10.refs_0_ = bf16[2,2,128,128]{3,2,1,0:T(8,128)(2,1)S(1)} collective-permute-done((bf16[2,2,128,128]{3,2,1,0:T(8,128)(2,1)S(1)}, bf16[2,2,128,128]{3,2,1,0:T(8,128)(2,1)S(1)}, u32[]{:S(2)}, u32[]{:S(2)}) %collective-permute-start.10) | collective-permute-done | bytes 131104 | tf_op jit(solution)/shard_map/ppermute | solution.py:599
  45.4 0.5 collective-permute-start.13
  45.9 1.5 %early_project.1.early_ref = f32[256,1024]{1,0:T(8,128)S(1)} custom-call(s32[8]{0:T(128)S(1)} %bitcast.25, bf16[1024,1024]{1,0:T(8,128)(2,1)S(1)} %bitcast.20, bf16[1056,128]{1,0:T(8,128)(2,1)S(1)} %attach_decay.1.left_ref.refs_0_, bf16[1056,128]{1,0:T(8,128)(2,1)S(1)} %collective-permute-done.right_ref.refs_1_, ...), custom_call_target="tpu_custom_call" | custom-call | tf_op jit(solution)/shard_map/early_project/pallas_call | solution.py:436
  47.5 7.4 %expert.1.own_ref = bf16[256,1024]{1,0:T(8,128)(2,1)S(1)} custom-call(f32[1,1024]{1,0:T(1,128)S(1)} %copy-done.4, bf16[1024,1024]{1,0:T(8,128)(2,1)S(1)} %bitcast.21, f32[256,1024]{1,0:T(8,128)S(1)} %early_project.1.early_ref, bf16[2,2,128,128]{3,2,1,0:T(8,128)(2,1)S(1)} %collective-permute-done.10.refs_0_, ...), custom_call_target="tpu_custom_call" | custom-call | tf_op jit(solution)/shard_map/expert/pallas_call | solution.py:486
  55.0 1.9 %collective-permute-done.14.other_ref = bf16[256,1024]{1,0:T(8,128)(2,1)S(1)} collective-permute-done((bf16[256,1024]{1,0:T(8,128)(2,1)S(1)}, bf16[256,1024]{1,0:T(8,128)(2,1)S(1)}, u32[]{:S(2)}, u32[]{:S(2)}) %collective-permute-start.14) | collective-permute-done | bytes 524320 | tf_op jit(solution)/shard_map/ppermute | solution.py:625
  56.9 0.8 homeward.1
  57.7 2.2 %collective-permute-start.15 = (bf16[128,1024]{1,0:T(8,128)(2,1)S(1)}, bf16[128,1024]{1,0:T(8,128)(2,1)S(1)}, u32[]{:S(2)}, u32[]{:S(2)}) collective-permute-start(bf16[128,1024]{1,0:T(8,128)(2,1)S(1)} %get-tuple-element.47), channel_id=1, source_target_pairs={{0,2},{1,3},{2,4},{3,5},{4,6},{5,7},{6,0},{7,1},{8,10},{9,11},{10,... | collective-permute-start | bytes 786440 | tf_op jit(solution)/shard_map/ppermute | solution.py:566
  59.9 2.6 %collective-permute-start.17 = (bf16[128,1024]{1,0:T(8,128)(2,1)S(1)}, bf16[128,1024]{1,0:T(8,128)(2,1)S(1)}, u32[]{:S(2)}, u32[]{:S(2)}) collective-permute-start(bf16[128,1024]{1,0:T(8,128)(2,1)S(1)} %get-tuple-element.49), channel_id=1, source_target_pairs={{0,14},{1,15},{2,8},{3,9},{4,10},{5,11},{6,12},{7,13},{8,22},{9,23... | collective-permute-start | bytes 786440 | tf_op jit(solution)/shard_map/ppermute | solution.py:623
  62.5 1.5 %collective-permute-start.18 = (bf16[128,1024]{1,0:T(8,128)(2,1)S(1)}, bf16[128,1024]{1,0:T(8,128)(2,1)S(1)}, u32[]{:S(2)}, u32[]{:S(2)}) collective-permute-start(bf16[128,1024]{1,0:T(8,128)(2,1)S(1)} %get-tuple-element.50), channel_id=1, source_target_pairs={{0,8},{1,9},{2,10},{3,11},{4,12},{5,13},{6,14},{7,15},{8,16},{9,17... | collective-permute-start | bytes 786440 | tf_op jit(solution)/shard_map/ppermute | solution.py:623
  64.0 4.8 %collective-permute-done.15 = bf16[128,1024]{1,0:T(8,128)(2,1)S(1)} collective-permute-done((bf16[128,1024]{1,0:T(8,128)(2,1)S(1)}, bf16[128,1024]{1,0:T(8,128)(2,1)S(1)}, u32[]{:S(2)}, u32[]{:S(2)}) %collective-permute-start.15) | collective-permute-done | bytes 262176 | tf_op jit(solution)/shard_map/ppermute | solution.py:566
  68.8 1.2 %collective-permute-start.16 = (bf16[128,1024]{1,0:T(8,128)(2,1)S(1)}, bf16[128,1024]{1,0:T(8,128)(2,1)S(1)}, u32[]{:S(2)}, u32[]{:S(2)}) collective-permute-start(bf16[128,1024]{1,0:T(8,128)(2,1)S(1)} %add.34), channel_id=1, source_target_pairs={{0,10},{1,11},{2,12},{3,13},{4,14},{5,15},{6,8},{7,9},{8,18},{9,19... | collective-permute-start | bytes 786440 | tf_op jit(solution)/shard_map/ppermute | solution.py:623
  70.1 6.1 %collective-permute-done.17 = bf16[128,1024]{1,0:T(8,128)(2,1)S(1)} collective-permute-done((bf16[128,1024]{1,0:T(8,128)(2,1)S(1)}, bf16[128,1024]{1,0:T(8,128)(2,1)S(1)}, u32[]{:S(2)}, u32[]{:S(2)}) %collective-permute-start.17) | collective-permute-done | bytes 262176 | tf_op jit(solution)/shard_map/ppermute | solution.py:623
  76.2 6.1 %collective-permute-done.18 = bf16[128,1024]{1,0:T(8,128)(2,1)S(1)} collective-permute-done((bf16[128,1024]{1,0:T(8,128)(2,1)S(1)}, bf16[128,1024]{1,0:T(8,128)(2,1)S(1)}, u32[]{:S(2)}, u32[]{:S(2)}) %collective-permute-start.18) | collective-permute-done | bytes 262176 | tf_op jit(solution)/shard_map/ppermute | solution.py:623
  82.3 0.7 add_bitcast_fusion
  (51 shorter events, 0.7 us)
Async XLA Ops:
  0.0 6.9 %copy-start = (bf16[1,1024,8]{1,2,0:T(8,128)(2,1)S(1)}, bf16[1,1024,8]{1,2,0:T(8,128)(2,1)}, u32[]{:S(2)}) copy-start(bf16[1,1024,8]{1,2,0:T(8,128)(2,1)} %param.17) | copy-start | bytes 49156
  0.0 1.0 %copy-start.2 = (bf16[1,128,1024]{2,1,0:T(8,128)(2,1)S(1)}, bf16[1,128,1024]{2,1,0:T(8,128)(2,1)}, u32[]{:S(2)}) copy-start(bf16[1,128,1024]{2,1,0:T(8,128)(2,1)} %param.12) | copy-start | bytes 786436
  1.8 6.7 %copy-start.6 = (f32[1,1024]{1,0:T(1,128)S(1)}, f32[1,1024]{1,0:T(1,128)}, u32[]{:S(2)}) copy-start(f32[1,1024]{1,0:T(1,128)} %refs_12_.1) | copy-start | bytes 12292
  1.8 12.0 %collective-permute-start.2 = (bf16[1056,128]{1,0:T(8,128)(2,1)S(1)}, bf16[1056,128]{1,0:T(8,128)(2,1)S(1)}, u32[]{:S(2)}, u32[]{:S(2)}) collective-permute-start(bf16[1056,128]{1,0:T(8,128)(2,1)S(1)} %attach_decay.1.left_ref.refs_0_), channel_id=1, source_target_pairs={{0,6},{1,7},{2,0},{3,1},{4,2},{5,3},{6,4},{7,5},{8,14},{9,15},{10,... | collective-permute-start | bytes 811016 | tf_op jit(solution)/shard_map/ppermute | solution.py:566
  6.9 12.6 %collective-permute-start.1 = (bf16[1056,128]{1,0:T(8,128)(2,1)S(1)}, bf16[1056,128]{1,0:T(8,128)(2,1)S(1)}, u32[]{:S(2)}, u32[]{:S(2)}) collective-permute-start(bf16[1056,128]{1,0:T(8,128)(2,1)S(1)} %attach_decay.1.left_ref.refs_0_), channel_id=1, source_target_pairs={{0,2},{1,3},{2,4},{3,5},{4,6},{5,7},{6,0},{7,1},{8,10},{9,11},{10,... | collective-permute-start | bytes 811016 | tf_op jit(solution)/shard_map/ppermute | solution.py:566
  6.9 1.6 %collective-permute-start = (bf16[1056,128]{1,0:T(8,128)(2,1)S(1)}, bf16[1056,128]{1,0:T(8,128)(2,1)S(1)}, u32[]{:S(2)}, u32[]{:S(2)}) collective-permute-start(bf16[1056,128]{1,0:T(8,128)(2,1)S(1)} %attach_decay.1.left_ref.refs_0_), channel_id=1, source_target_pairs={{0,1},{1,0},{2,3},{3,2},{4,5},{5,4},{6,7},{7,6},{8,9},{9,8},{10,11... | collective-permute-start | bytes 811016 | tf_op jit(solution)/shard_map/ppermute | solution.py:571
  13.8 5.7 %collective-permute-start.4 = (bf16[1056,128]{1,0:T(8,128)(2,1)S(1)}, bf16[1056,128]{1,0:T(8,128)(2,1)S(1)}, u32[]{:S(2)}, u32[]{:S(2)}) collective-permute-start(bf16[1056,128]{1,0:T(8,128)(2,1)S(1)} %collective-permute-done.2.left_ref.refs_4_), channel_id=1, source_target_pairs={{0,1},{1,0},{2,3},{3,2},{4,5},{5,4},{6,7},{7,6},{8,9},{9,8},{10,11... | collective-permute-start | bytes 811016 | tf_op jit(solution)/shard_map/ppermute | solution.py:589
  13.8 11.4 %collective-permute-start.5 = (bf16[1056,128]{1,0:T(8,128)(2,1)S(1)}, bf16[1056,128]{1,0:T(8,128)(2,1)S(1)}, u32[]{:S(2)}, u32[]{:S(2)}) collective-permute-start(bf16[1056,128]{1,0:T(8,128)(2,1)S(1)} %collective-permute-done.2.left_ref.refs_4_), channel_id=1, source_target_pairs={{0,6},{1,7},{2,0},{3,1},{4,2},{5,3},{6,4},{7,5},{8,14},{9,15},{10,... | collective-permute-start | bytes 811016 | tf_op jit(solution)/shard_map/ppermute | solution.py:566
  19.5 2.7 %collective-permute-start.3 = (bf16[1056,128]{1,0:T(8,128)(2,1)S(1)}, bf16[1056,128]{1,0:T(8,128)(2,1)S(1)}, u32[]{:S(2)}, u32[]{:S(2)}) collective-permute-start(bf16[1056,128]{1,0:T(8,128)(2,1)S(1)} %collective-permute-done.1.left_ref.refs_2_), channel_id=1, source_target_pairs={{0,1},{1,0},{2,3},{3,2},{4,5},{5,4},{6,7},{7,6},{8,9},{9,8},{10,11... | collective-permute-start | bytes 811016 | tf_op jit(solution)/shard_map/ppermute | solution.py:587
  22.1 4.6 %copy-start.5 = (s32[1,8,1]{1,2,0:T(1,128)S(1)}, s32[1,8,1]{1,2,0:T(1,128)}, u32[]{:S(2)}) copy-start(s32[1,8,1]{1,2,0:T(1,128)} %param.14) | copy-start | bytes 100
  22.1 4.5 %copy-start.7 = (f32[1,128]{1,0:T(1,128)S(1)}, f32[1,128]{1,0:T(1,128)}, u32[]{:S(2)}) copy-start(f32[1,128]{1,0:T(1,128)} %out_gain_ref.1) | copy-start | bytes 1540
  22.2 25.3 %slice-start = ((s8[8388608]{0:T(1024)(128)(4,1)}), s8[4194304]{0:T(1024)(128)(4,1)S(1)}, s32[]{:S(2)}) async-start(s8[8388608]{0:T(1024)(128)(4,1)} %bitcast.14), calls=%async_computation | async-start | bytes 8388608
  22.2 25.3 %slice-start.2 = ((s8[8388608]{0:T(1024)(128)(4,1)}), s8[4194304]{0:T(1024)(128)(4,1)S(1)}, s32[]{:S(2)}) async-start(s8[8388608]{0:T(1024)(128)(4,1)} %bitcast.16), calls=%async_computation.2 | async-start | bytes 8388608
  22.2 25.3 %slice-start.4 = ((s8[8388608]{0:T(1024)(128)(4,1)}), s8[4194304]{0:T(1024)(128)(4,1)S(1)}, s32[]{:S(2)}) async-start(s8[8388608]{0:T(1024)(128)(4,1)} %bitcast.18), calls=%async_computation.4 | async-start | bytes 8388608
  25.1 1.5 %collective-permute-start.6 = (bf16[1056,128]{1,0:T(8,128)(2,1)S(1)}, bf16[1056,128]{1,0:T(8,128)(2,1)S(1)}, u32[]{:S(2)}, u32[]{:S(2)}) collective-permute-start(bf16[1056,128]{1,0:T(8,128)(2,1)S(1)} %collective-permute-done.5.refs_14_.refs_6_), channel_id=1, source_target_pairs={{0,1},{1,0},{2,3},{3,2},{4,5},{5,4},{6,7},{7,6},{8,9},{9,8},{10,11... | collective-permute-start | bytes 811016 | tf_op jit(solution)/shard_map/ppermute | solution.py:592
  26.7 19.2 %copy-start.1 = (bf16[1,1024,1024]{2,1,0:T(8,128)(2,1)S(1)}, bf16[1,1024,1024]{2,1,0:T(8,128)(2,1)}, u32[]{:S(2)}) copy-start(bf16[1,1024,1024]{2,1,0:T(8,128)(2,1)} %param.19) | copy-start | bytes 6291460
  26.7 20.8 %slice-start.1 = ((s8[8388608]{0:T(1024)(128)(4,1)}), s8[4194304]{0:T(1024)(128)(4,1)S(1)}, s32[]{:S(2)}) async-start(s8[8388608]{0:T(1024)(128)(4,1)} %bitcast.14), calls=%async_computation.1 | async-start | bytes 8388608
  26.7 20.8 %slice-start.3 = ((s8[8388608]{0:T(1024)(128)(4,1)}), s8[4194304]{0:T(1024)(128)(4,1)S(1)}, s32[]{:S(2)}) async-start(s8[8388608]{0:T(1024)(128)(4,1)} %bitcast.16), calls=%async_computation.3 | async-start | bytes 8388608
  26.7 20.8 %slice-start.5 = ((s8[8388608]{0:T(1024)(128)(4,1)}), s8[4194304]{0:T(1024)(128)(4,1)S(1)}, s32[]{:S(2)}) async-start(s8[8388608]{0:T(1024)(128)(4,1)} %bitcast.18), calls=%async_computation.5 | async-start | bytes 8388608
  31.0 7.9 %collective-permute-start.8 = (bf16[2,2,128,128]{3,2,1,0:T(8,128)(2,1)S(1)}, bf16[2,2,128,128]{3,2,1,0:T(8,128)(2,1)S(1)}, u32[]{:S(2)}, u32[]{:S(2)}) collective-permute-start(bf16[2,2,128,128]{3,2,1,0:T(8,128)(2,1)S(1)} %get-tuple-element.44), channel_id=1, source_target_pairs={{0,2},{1,3},{2,0},{3,1},{4,6},{5,7},{6,4},{7,5},{8,10},{9,11},{10,... | collective-permute-start | bytes 393224 | tf_op jit(solution)/shard_map/ppermute | solution.py:599
  32.5 12.9 %collective-permute-start.10 = (bf16[2,2,128,128]{3,2,1,0:T(8,128)(2,1)S(1)}, bf16[2,2,128,128]{3,2,1,0:T(8,128)(2,1)S(1)}, u32[]{:S(2)}, u32[]{:S(2)}) collective-permute-start(bf16[2,2,128,128]{3,2,1,0:T(8,128)(2,1)S(1)} %get-tuple-element.45), channel_id=1, source_target_pairs={{0,4},{1,5},{2,6},{3,7},{4,0},{5,1},{6,2},{7,3},{8,12},{9,13},{10,... | collective-permute-start | bytes 393224 | tf_op jit(solution)/shard_map/ppermute | solution.py:599
  35.2 10.2 %collective-permute-start.12 = (bf16[2,2,128,128]{3,2,1,0:T(8,128)(2,1)S(1)}, bf16[2,2,128,128]{3,2,1,0:T(8,128)(2,1)S(1)}, u32[]{:S(2)}, u32[]{:S(2)}) collective-permute-start(bf16[2,2,128,128]{3,2,1,0:T(8,128)(2,1)S(1)} %get-tuple-element.46), channel_id=1, source_target_pairs={{0,6},{1,7},{2,4},{3,5},{4,2},{5,3},{6,0},{7,1},{8,14},{9,15},{10,... | collective-permute-start | bytes 393224 | tf_op jit(solution)/shard_map/ppermute | solution.py:599
  35.5 10.5 %collective-permute-start.7 = (bf16[2,2,128,128]{3,2,1,0:T(8,128)(2,1)S(1)}, bf16[2,2,128,128]{3,2,1,0:T(8,128)(2,1)S(1)}, u32[]{:S(2)}, u32[]{:S(2)}) collective-permute-start(bf16[2,2,128,128]{3,2,1,0:T(8,128)(2,1)S(1)} %get-tuple-element.43.refs_8_), channel_id=1, source_target_pairs={{0,1},{1,0},{2,3},{3,2},{4,5},{5,4},{6,7},{7,6},{8,9},{9,8},{10,11... | collective-permute-start | bytes 393224 | tf_op jit(solution)/shard_map/ppermute | solution.py:601
  38.9 7.0 %collective-permute-start.9 = (bf16[2,2,128,128]{3,2,1,0:T(8,128)(2,1)S(1)}, bf16[2,2,128,128]{3,2,1,0:T(8,128)(2,1)S(1)}, u32[]{:S(2)}, u32[]{:S(2)}) collective-permute-start(bf16[2,2,128,128]{3,2,1,0:T(8,128)(2,1)S(1)} %collective-permute-done.8.refs_10_), channel_id=1, source_target_pairs={{0,1},{1,0},{2,3},{3,2},{4,5},{5,4},{6,7},{7,6},{8,9},{9,8},{10,11... | collective-permute-start | bytes 393224 | tf_op jit(solution)/shard_map/ppermute | solution.py:601
  45.4 2.0 %collective-permute-start.11 = (bf16[2,2,128,128]{3,2,1,0:T(8,128)(2,1)S(1)}, bf16[2,2,128,128]{3,2,1,0:T(8,128)(2,1)S(1)}, u32[]{:S(2)}, u32[]{:S(2)}) collective-permute-start(bf16[2,2,128,128]{3,2,1,0:T(8,128)(2,1)S(1)} %collective-permute-done.10.refs_0_), channel_id=1, source_target_pairs={{0,1},{1,0},{2,3},{3,2},{4,5},{5,4},{6,7},{7,6},{8,9},{9,8},{10,11... | collective-permute-start | bytes 393224 | tf_op jit(solution)/shard_map/ppermute | solution.py:603
  45.4 2.0 %collective-permute-start.13 = (bf16[2,2,128,128]{3,2,1,0:T(8,128)(2,1)S(1)}, bf16[2,2,128,128]{3,2,1,0:T(8,128)(2,1)S(1)}, u32[]{:S(2)}, u32[]{:S(2)}) collective-permute-start(bf16[2,2,128,128]{3,2,1,0:T(8,128)(2,1)S(1)} %collective-permute-done.12.refs_2_), channel_id=1, source_target_pairs={{0,1},{1,0},{2,3},{3,2},{4,5},{5,4},{6,7},{7,6},{8,9},{9,8},{10,11... | collective-permute-start | bytes 393224 | tf_op jit(solution)/shard_map/ppermute | solution.py:603
  45.9 1.6 %copy-start.4 = (f32[1,1024]{1,0:T(1,128)S(1)}, f32[1,1024]{1,0:T(1,128)}, u32[]{:S(2)}) copy-start(f32[1,1024]{1,0:T(1,128)} %gain_ref.7) | copy-start | bytes 12292
  54.9 2.0 %collective-permute-start.14 = (bf16[256,1024]{1,0:T(8,128)(2,1)S(1)}, bf16[256,1024]{1,0:T(8,128)(2,1)S(1)}, u32[]{:S(2)}, u32[]{:S(2)}) collective-permute-start(bf16[256,1024]{1,0:T(8,128)(2,1)S(1)} %expert.1.own_ref), channel_id=1, source_target_pairs={{0,1},{1,0},{2,3},{3,2},{4,5},{5,4},{6,7},{7,6},{8,9},{9,8},{10,11... | collective-permute-start | bytes 1572872 | tf_op jit(solution)/shard_map/ppermute | solution.py:625
  57.7 11.0 %collective-permute-start.15 = (bf16[128,1024]{1,0:T(8,128)(2,1)S(1)}, bf16[128,1024]{1,0:T(8,128)(2,1)S(1)}, u32[]{:S(2)}, u32[]{:S(2)}) collective-permute-start(bf16[128,1024]{1,0:T(8,128)(2,1)S(1)} %get-tuple-element.47), channel_id=1, source_target_pairs={{0,2},{1,3},{2,4},{3,5},{4,6},{5,7},{6,0},{7,1},{8,10},{9,11},{10,... | collective-permute-start | bytes 786440 | tf_op jit(solution)/shard_map/ppermute | solution.py:566
  59.9 16.3 %collective-permute-start.17 = (bf16[128,1024]{1,0:T(8,128)(2,1)S(1)}, bf16[128,1024]{1,0:T(8,128)(2,1)S(1)}, u32[]{:S(2)}, u32[]{:S(2)}) collective-permute-start(bf16[128,1024]{1,0:T(8,128)(2,1)S(1)} %get-tuple-element.49), channel_id=1, source_target_pairs={{0,14},{1,15},{2,8},{3,9},{4,10},{5,11},{6,12},{7,13},{8,22},{9,23... | collective-permute-start | bytes 786440 | tf_op jit(solution)/shard_map/ppermute | solution.py:623
  62.5 19.8 %collective-permute-start.18 = (bf16[128,1024]{1,0:T(8,128)(2,1)S(1)}, bf16[128,1024]{1,0:T(8,128)(2,1)S(1)}, u32[]{:S(2)}, u32[]{:S(2)}) collective-permute-start(bf16[128,1024]{1,0:T(8,128)(2,1)S(1)} %get-tuple-element.50), channel_id=1, source_target_pairs={{0,8},{1,9},{2,10},{3,11},{4,12},{5,13},{6,14},{7,15},{8,16},{9,17... | collective-permute-start | bytes 786440 | tf_op jit(solution)/shard_map/ppermute | solution.py:623
  68.8 13.5 %collective-permute-start.16 = (bf16[128,1024]{1,0:T(8,128)(2,1)S(1)}, bf16[128,1024]{1,0:T(8,128)(2,1)S(1)}, u32[]{:S(2)}, u32[]{:S(2)}) collective-permute-start(bf16[128,1024]{1,0:T(8,128)(2,1)S(1)} %add.34), channel_id=1, source_target_pairs={{0,10},{1,11},{2,12},{3,13},{4,14},{5,15},{6,8},{7,9},{8,18},{9,19... | collective-permute-start | bytes 786440 | tf_op jit(solution)/shard_map/ppermute | solution.py:623
  (1 other events, 0.7 us)

commit v5 on v4

--- a/solution.py
+++ b/solution.py
@@ -623,10 +623,10 @@
         return lax.ppermute(block, ("segment", "seq"), home_route(sections, count, by))
 
     here, right_home, far_home, left_home = homeward(kinds, finished, pair(finished))
-    passed = hop(far_home, 1)
-    from_right = send_home(left_home, -1)
+    passed = hop(far_home, -1)
+    from_right = send_home(right_home, 1)
     from_here = send_home(here, 0)
-    from_left = send_home(passed + right_home, 1)
+    from_left = send_home(passed + left_home, -1)
     return (from_left + from_right + from_here)[None]
 
 

time: 83.3 us -> 82.7 us (level)
  waiting for transfers between devices: 34.5 us -> 31.6 us
  starting transfers between devices: 22.3 us -> 24.7 us
    ppermute x3, waiting for transfers between devices: 12.3 us -> 9.74 us  [send_home(): lax.ppermute(block, ('segment', 'seq'), home_route(sections, count, by))]
    ppermute x3, starting transfers between devices: 5.34 us -> 7.57 us  [send_home(): lax.ppermute(block, ('segment', 'seq'), home_route(sections, count, by))]
  transfers between devices with their start and end apart: 19 -> 19, of which waited for: 10 -> 11; matrix products, arithmetic and copies ran while one was open for 2% -> 2% of each run, Pallas kernels for 11% -> 11%
where the time goes in v5:
time: 82.7 us; the launch traced here: 82.6 us
  waiting for transfers between devices  31.6 us (38%)
  starting transfers between devices  24.7 us (30%)
  Pallas kernels  21.9 us (26%)
  local copies, waits for them, and re-layouts  3.14 us (4%)
  other arithmetic  0.93 us (1%)
    ppermute x4, starting transfers between devices, hop(): return lax.ppermute(block, 'seq', lane_route(count, by))  11.8 us
    ppermute x3, waiting for transfers between devices, per_device(): lax.ppermute(sends[k], 'seq', chip_route(count, k))  9.93 us
    ppermute x3, waiting for transfers between devices, send_home(): lax.ppermute(block, ('segment', 'seq'), home_route(sections, count, by))  9.74 us
    ppermute x4, waiting for transfers between devices, hop(): return lax.ppermute(block, 'seq', lane_route(count, by))  8.78 us
    pallas_call x3, Pallas kernels, terms(): pl.pallas_call(terms_kernel, out_shape=tuple((jax.ShapeDtypeStruct(*s) fo...  7.9 us
    ppermute x3, starting transfers between devices, send_home(): lax.ppermute(block, ('segment', 'seq'), home_route(sections, count, by))  7.57 us
    pallas_call x1, Pallas kernels, expert(): pl.pallas_call(partial(expert_kernel, min(512, gate.shape[3])), out_shape...  7.37 us
    ppermute x3, starting transfers between devices, per_device(): lax.ppermute(sends[k], 'seq', chip_route(count, k))  4.45 us
  transfers between devices with their start and end apart: 19, of which 11 were waited for; matrix products, arithmetic and copies ran while one was open for 2% of the time, Pallas kernels for 11%

profile of v5, /device:TPU:0, one launch (start us, length us, event | category | flops | bytes accessed | tf_op | source)
XLA Modules:
  0.0 82.6 jit_solution(17980592365302394418)
XLA Ops:
  0.0 1.0 %copy-done.2 = bf16[1,128,1024]{2,1,0:T(8,128)(2,1)S(1)} copy-done((bf16[1,128,1024]{2,1,0:T(8,128)(2,1)S(1)}, bf16[1,128,1024]{2,1,0:T(8,128)(2,1)}, u32[]{:S(2)}) %copy-start.2) | copy-done | bytes 262168
  1.0 0.7 copy-done.3
  1.8 5.1 %collective-permute-start.2 = (bf16[1056,128]{1,0:T(8,128)(2,1)S(1)}, bf16[1056,128]{1,0:T(8,128)(2,1)S(1)}, u32[]{:S(2)}, u32[]{:S(2)}) collective-permute-start(bf16[1056,128]{1,0:T(8,128)(2,1)S(1)} %attach_decay.1.left_ref.refs_0_), channel_id=1, source_target_pairs={{0,6},{1,7},{2,0},{3,1},{4,2},{5,3},{6,4},{7,5},{8,14},{9,15},{10,... | collective-permute-start | bytes 811016 | tf_op jit(solution)/shard_map/ppermute | solution.py:566
  6.9 1.2 %dynamic-slice_bitcast_fusion.2 = (bf16[1024,128]{1,0:T(8,128)(2,1)S(1)}, bf16[1024,128]{1,0:T(8,128)(2,1)S(1)}, bf16[1024,128]{1,0:T(8,128)(2,1)S(1)}) fusion(bf16[1,1024,3072]{2,1,0:T(8,128)(2,1)} %param.16, s32[]{:T(128)S(6)} %select_n.20, s32[]{:T(128)S(6)} %select_n.22, s32[]{:T(128)S(6)} %select_n.21), kind=kLoop, calls=%fused_computation.4 | loop fusion | bytes 1572876 | tf_op jit(solution)/shard_map/dynamic_slice | solution.py:574
  8.4 2.6 %chunk_terms.3 = (bf16[2,128,128]{2,1,0:T(8,128)(2,1)S(1)}, f32[2,128,128]{2,1,0:T(8,128)S(1)}, f32[2,256,128]{2,1,0:T(8,128)S(1)}, f32[2,8,128]{2,1,0:T(8,128)S(1)}) custom-call(f32[1,1024]{1,0:T(1,128)S(1)} %copy-done.6, bf16[1024,512]{1,0:T(8,128)(2,1)S(1)} %pad_maximum_fusion.weight_ref.refs_13_, bf16[1056,128]{1,0:T(8,128)(2,1)S(1)} %attach_decay.1.left_ref.refs_0_, ...), custom_call_target="tpu_custom_call" | custom-call | flops 4000000000 | bytes 3000000 | tf_op jit(solution)/shard_map/chunk_terms/pallas_call | solution.py:274
  11.1 2.7 %collective-permute-done.2.left_ref.refs_4_ = bf16[1056,128]{1,0:T(8,128)(2,1)S(1)} collective-permute-done((bf16[1056,128]{1,0:T(8,128)(2,1)S(1)}, bf16[1056,128]{1,0:T(8,128)(2,1)S(1)}, u32[]{:S(2)}, u32[]{:S(2)}) %collective-permute-start.2) | collective-permute-done | bytes 270368 | tf_op jit(solution)/shard_map/ppermute | solution.py:566
  13.8 4.3 %collective-permute-start.5 = (bf16[1056,128]{1,0:T(8,128)(2,1)S(1)}, bf16[1056,128]{1,0:T(8,128)(2,1)S(1)}, u32[]{:S(2)}, u32[]{:S(2)}) collective-permute-start(bf16[1056,128]{1,0:T(8,128)(2,1)S(1)} %collective-permute-done.2.left_ref.refs_4_), channel_id=1, source_target_pairs={{0,6},{1,7},{2,0},{3,1},{4,2},{5,3},{6,4},{7,5},{8,14},{9,15},{10,... | collective-permute-start | bytes 811016 | tf_op jit(solution)/shard_map/ppermute | solution.py:566
  18.0 1.4 %collective-permute-done.1.left_ref.refs_2_ = bf16[1056,128]{1,0:T(8,128)(2,1)S(1)} collective-permute-done((bf16[1056,128]{1,0:T(8,128)(2,1)S(1)}, bf16[1056,128]{1,0:T(8,128)(2,1)S(1)}, u32[]{:S(2)}, u32[]{:S(2)}) %collective-permute-start.1) | collective-permute-done | bytes 270368 | tf_op jit(solution)/shard_map/ppermute | solution.py:566
  19.5 2.6 %chunk_terms.5 = (bf16[2,128,128]{2,1,0:T(8,128)(2,1)S(1)}, f32[2,128,128]{2,1,0:T(8,128)S(1)}, f32[2,256,128]{2,1,0:T(8,128)S(1)}, f32[2,8,128]{2,1,0:T(8,128)S(1)}) custom-call(f32[1,1024]{1,0:T(1,128)S(1)} %copy-done.6, bf16[1024,512]{1,0:T(8,128)(2,1)S(1)} %pad_maximum_fusion.weight_ref.refs_13_, ...), custom_call_target="tpu_custom_call" | custom-call | flops 4000000000 | bytes 3000000 | tf_op jit(solution)/shard_map/chunk_terms/pallas_call | solution.py:274
  22.2 2.6 %chunk_terms.4 = (bf16[2,128,128]{2,1,0:T(8,128)(2,1)S(1)}, f32[2,128,128]{2,1,0:T(8,128)S(1)}, f32[2,256,128]{2,1,0:T(8,128)S(1)}, f32[2,8,128]{2,1,0:T(8,128)S(1)}) custom-call(f32[1,1024]{1,0:T(1,128)S(1)} %copy-done.6, bf16[1024,512]{1,0:T(8,128)(2,1)S(1)} %pad_maximum_fusion.weight_ref.refs_13_, ...), custom_call_target="tpu_custom_call" | custom-call | flops 4000000000 | bytes 3000000 | tf_op jit(solution)/shard_map/chunk_terms/pallas_call | solution.py:274
  24.8 0.3 collective-permute-done.5.refs_14_.refs_6_
  25.1 0.3 collective-permute-start.6
  25.4 1.3 %collective-permute-done.6.refs_15_.refs_7_ = bf16[1056,128]{1,0:T(8,128)(2,1)S(1)} collective-permute-done((bf16[1056,128]{1,0:T(8,128)(2,1)S(1)}, bf16[1056,128]{1,0:T(8,128)(2,1)S(1)}, u32[]{:S(2)}, u32[]{:S(2)}) %collective-permute-start.6) | collective-permute-done | bytes 270368 | tf_op jit(solution)/shard_map/ppermute | solution.py:592
  26.7 4.3 %state_walk.1 = (bf16[2,2,128,128]{3,2,1,0:T(8,128)(2,1)S(1)}, bf16[2,2,128,128]{3,2,1,0:T(8,128)(2,1)S(1)}, bf16[2,2,128,128]{3,2,1,0:T(8,128)(2,1)S(1)}, bf16[2,2,128,128]{3,2,1,0:T(8,128)(2,1)S(1)}) custom-call(s32[8]{0:T(128)S(1)} %bitcast.24, f32[1,128]{1,0:T(1,128)S(1)} %copy-done.7, bf16[2,128,128]{2,1,0:T(8,128)(2,1)S(1)} %get-tuple-element.28.refs_0_, ...), custom_call_target="tpu_custom_call" | custom-call | flops 30000001024 | bytes 4000000 | tf_op jit(solution)/shard_map/state_walk/pallas_call | solution.py:343
  31.0 1.5 %collective-permute-start.8 = (bf16[2,2,128,128]{3,2,1,0:T(8,128)(2,1)S(1)}, bf16[2,2,128,128]{3,2,1,0:T(8,128)(2,1)S(1)}, u32[]{:S(2)}, u32[]{:S(2)}) collective-permute-start(bf16[2,2,128,128]{3,2,1,0:T(8,128)(2,1)S(1)} %get-tuple-element.44), channel_id=1, source_target_pairs={{0,2},{1,3},{2,0},{3,1},{4,6},{5,7},{6,4},{7,5},{8,10},{9,11},{10,... | collective-permute-start | bytes 393224 | tf_op jit(solution)/shard_map/ppermute | solution.py:599
  32.5 2.8 %collective-permute-start.10 = (bf16[2,2,128,128]{3,2,1,0:T(8,128)(2,1)S(1)}, bf16[2,2,128,128]{3,2,1,0:T(8,128)(2,1)S(1)}, u32[]{:S(2)}, u32[]{:S(2)}) collective-permute-start(bf16[2,2,128,128]{3,2,1,0:T(8,128)(2,1)S(1)} %get-tuple-element.45), channel_id=1, source_target_pairs={{0,4},{1,5},{2,6},{3,7},{4,0},{5,1},{6,2},{7,3},{8,12},{9,13},{10,... | collective-permute-start | bytes 393224 | tf_op jit(solution)/shard_map/ppermute | solution.py:599
  35.5 3.4 %collective-permute-done.8.refs_10_ = bf16[2,2,128,128]{3,2,1,0:T(8,128)(2,1)S(1)} collective-permute-done((bf16[2,2,128,128]{3,2,1,0:T(8,128)(2,1)S(1)}, bf16[2,2,128,128]{3,2,1,0:T(8,128)(2,1)S(1)}, u32[]{:S(2)}, u32[]{:S(2)}) %collective-permute-start.8) | collective-permute-done | bytes 131104 | tf_op jit(solution)/shard_map/ppermute | solution.py:599
  38.9 6.5 %collective-permute-done.10.refs_0_ = bf16[2,2,128,128]{3,2,1,0:T(8,128)(2,1)S(1)} collective-permute-done((bf16[2,2,128,128]{3,2,1,0:T(8,128)(2,1)S(1)}, bf16[2,2,128,128]{3,2,1,0:T(8,128)(2,1)S(1)}, u32[]{:S(2)}, u32[]{:S(2)}) %collective-permute-start.10) | collective-permute-done | bytes 131104 | tf_op jit(solution)/shard_map/ppermute | solution.py:599
  45.4 0.5 collective-permute-start.13
  45.9 1.5 %early_project.1.early_ref = f32[256,1024]{1,0:T(8,128)S(1)} custom-call(s32[8]{0:T(128)S(1)} %bitcast.25, bf16[1024,1024]{1,0:T(8,128)(2,1)S(1)} %bitcast.20, bf16[1056,128]{1,0:T(8,128)(2,1)S(1)} %attach_decay.1.left_ref.refs_0_, bf16[1056,128]{1,0:T(8,128)(2,1)S(1)} %collective-permute-done.right_ref.refs_1_, ...), custom_call_target="tpu_custom_call" | custom-call | tf_op jit(solution)/shard_map/early_project/pallas_call | solution.py:436
  47.5 7.4 %expert.1.own_ref = bf16[256,1024]{1,0:T(8,128)(2,1)S(1)} custom-call(f32[1,1024]{1,0:T(1,128)S(1)} %copy-done.4, bf16[1024,1024]{1,0:T(8,128)(2,1)S(1)} %bitcast.21, f32[256,1024]{1,0:T(8,128)S(1)} %early_project.1.early_ref, bf16[2,2,128,128]{3,2,1,0:T(8,128)(2,1)S(1)} %collective-permute-done.10.refs_0_, ...), custom_call_target="tpu_custom_call" | custom-call | tf_op jit(solution)/shard_map/expert/pallas_call | solution.py:486
  55.0 1.9 %collective-permute-done.14.other_ref = bf16[256,1024]{1,0:T(8,128)(2,1)S(1)} collective-permute-done((bf16[256,1024]{1,0:T(8,128)(2,1)S(1)}, bf16[256,1024]{1,0:T(8,128)(2,1)S(1)}, u32[]{:S(2)}, u32[]{:S(2)}) %collective-permute-start.14) | collective-permute-done | bytes 524320 | tf_op jit(solution)/shard_map/ppermute | solution.py:625
  56.9 0.8 homeward.1
  57.7 2.4 %collective-permute-start.15 = (bf16[128,1024]{1,0:T(8,128)(2,1)S(1)}, bf16[128,1024]{1,0:T(8,128)(2,1)S(1)}, u32[]{:S(2)}, u32[]{:S(2)}) collective-permute-start(bf16[128,1024]{1,0:T(8,128)(2,1)S(1)} %get-tuple-element.47), channel_id=1, source_target_pairs={{0,6},{1,7},{2,0},{3,1},{4,2},{5,3},{6,4},{7,5},{8,14},{9,15},{10,... | collective-permute-start | bytes 786440 | tf_op jit(solution)/shard_map/ppermute | solution.py:566
  60.1 0.8 %collective-permute-start.17 = (bf16[128,1024]{1,0:T(8,128)(2,1)S(1)}, bf16[128,1024]{1,0:T(8,128)(2,1)S(1)}, u32[]{:S(2)}, u32[]{:S(2)}) collective-permute-start(bf16[128,1024]{1,0:T(8,128)(2,1)S(1)} %get-tuple-element.49), channel_id=1, source_target_pairs={{0,10},{1,11},{2,12},{3,13},{4,14},{5,15},{6,8},{7,9},{8,18},{9,19... | collective-permute-start | bytes 786440 | tf_op jit(solution)/shard_map/ppermute | solution.py:623
  60.9 1.5 %collective-permute-start.18 = (bf16[128,1024]{1,0:T(8,128)(2,1)S(1)}, bf16[128,1024]{1,0:T(8,128)(2,1)S(1)}, u32[]{:S(2)}, u32[]{:S(2)}) collective-permute-start(bf16[128,1024]{1,0:T(8,128)(2,1)S(1)} %get-tuple-element.50), channel_id=1, source_target_pairs={{0,8},{1,9},{2,10},{3,11},{4,12},{5,13},{6,14},{7,15},{8,16},{9,17... | collective-permute-start | bytes 786440 | tf_op jit(solution)/shard_map/ppermute | solution.py:623
  62.4 4.4 %collective-permute-done.15 = bf16[128,1024]{1,0:T(8,128)(2,1)S(1)} collective-permute-done((bf16[128,1024]{1,0:T(8,128)(2,1)S(1)}, bf16[128,1024]{1,0:T(8,128)(2,1)S(1)}, u32[]{:S(2)}, u32[]{:S(2)}) %collective-permute-start.15) | collective-permute-done | bytes 262176 | tf_op jit(solution)/shard_map/ppermute | solution.py:566
  66.8 5.2 %collective-permute-start.16 = (bf16[128,1024]{1,0:T(8,128)(2,1)S(1)}, bf16[128,1024]{1,0:T(8,128)(2,1)S(1)}, u32[]{:S(2)}, u32[]{:S(2)}) collective-permute-start(bf16[128,1024]{1,0:T(8,128)(2,1)S(1)} %add.34), channel_id=1, source_target_pairs={{0,14},{1,15},{2,8},{3,9},{4,10},{5,11},{6,12},{7,13},{8,22},{9,23... | collective-permute-start | bytes 786440 | tf_op jit(solution)/shard_map/ppermute | solution.py:623
  72.1 4.8 %collective-permute-done.17 = bf16[128,1024]{1,0:T(8,128)(2,1)S(1)} collective-permute-done((bf16[128,1024]{1,0:T(8,128)(2,1)S(1)}, bf16[128,1024]{1,0:T(8,128)(2,1)S(1)}, u32[]{:S(2)}, u32[]{:S(2)}) %collective-permute-start.17) | collective-permute-done | bytes 262176 | tf_op jit(solution)/shard_map/ppermute | solution.py:623
  76.9 2.5 %collective-permute-done.18 = bf16[128,1024]{1,0:T(8,128)(2,1)S(1)} collective-permute-done((bf16[128,1024]{1,0:T(8,128)(2,1)S(1)}, bf16[128,1024]{1,0:T(8,128)(2,1)S(1)}, u32[]{:S(2)}, u32[]{:S(2)}) %collective-permute-start.18) | collective-permute-done | bytes 262176 | tf_op jit(solution)/shard_map/ppermute | solution.py:623
  79.5 2.4 %collective-permute-done.16 = bf16[128,1024]{1,0:T(8,128)(2,1)S(1)} collective-permute-done((bf16[128,1024]{1,0:T(8,128)(2,1)S(1)}, bf16[128,1024]{1,0:T(8,128)(2,1)S(1)}, u32[]{:S(2)}, u32[]{:S(2)}) %collective-permute-start.16) | collective-permute-done | bytes 262176 | tf_op jit(solution)/shard_map/ppermute | solution.py:623
  81.8 0.7 add_bitcast_fusion
  (51 shorter events, 0.9 us)
Async XLA Ops:
  0.0 6.9 %copy-start = (bf16[1,1024,8]{1,2,0:T(8,128)(2,1)S(1)}, bf16[1,1024,8]{1,2,0:T(8,128)(2,1)}, u32[]{:S(2)}) copy-start(bf16[1,1024,8]{1,2,0:T(8,128)(2,1)} %param.17) | copy-start | bytes 49156
  0.0 1.0 %copy-start.2 = (bf16[1,128,1024]{2,1,0:T(8,128)(2,1)S(1)}, bf16[1,128,1024]{2,1,0:T(8,128)(2,1)}, u32[]{:S(2)}) copy-start(bf16[1,128,1024]{2,1,0:T(8,128)(2,1)} %param.12) | copy-start | bytes 786436
  1.8 6.7 %copy-start.6 = (f32[1,1024]{1,0:T(1,128)S(1)}, f32[1,1024]{1,0:T(1,128)}, u32[]{:S(2)}) copy-start(f32[1,1024]{1,0:T(1,128)} %refs_12_.1) | copy-start | bytes 12292
  1.8 12.0 %collective-permute-start.2 = (bf16[1056,128]{1,0:T(8,128)(2,1)S(1)}, bf16[1056,128]{1,0:T(8,128)(2,1)S(1)}, u32[]{:S(2)}, u32[]{:S(2)}) collective-permute-start(bf16[1056,128]{1,0:T(8,128)(2,1)S(1)} %attach_decay.1.left_ref.refs_0_), channel_id=1, source_target_pairs={{0,6},{1,7},{2,0},{3,1},{4,2},{5,3},{6,4},{7,5},{8,14},{9,15},{10,... | collective-permute-start | bytes 811016 | tf_op jit(solution)/shard_map/ppermute | solution.py:566
  6.9 12.6 %collective-permute-start.1 = (bf16[1056,128]{1,0:T(8,128)(2,1)S(1)}, bf16[1056,128]{1,0:T(8,128)(2,1)S(1)}, u32[]{:S(2)}, u32[]{:S(2)}) collective-permute-start(bf16[1056,128]{1,0:T(8,128)(2,1)S(1)} %attach_decay.1.left_ref.refs_0_), channel_id=1, source_target_pairs={{0,2},{1,3},{2,4},{3,5},{4,6},{5,7},{6,0},{7,1},{8,10},{9,11},{10,... | collective-permute-start | bytes 811016 | tf_op jit(solution)/shard_map/ppermute | solution.py:566
  6.9 1.6 %collective-permute-start = (bf16[1056,128]{1,0:T(8,128)(2,1)S(1)}, bf16[1056,128]{1,0:T(8,128)(2,1)S(1)}, u32[]{:S(2)}, u32[]{:S(2)}) collective-permute-start(bf16[1056,128]{1,0:T(8,128)(2,1)S(1)} %attach_decay.1.left_ref.refs_0_), channel_id=1, source_target_pairs={{0,1},{1,0},{2,3},{3,2},{4,5},{5,4},{6,7},{7,6},{8,9},{9,8},{10,11... | collective-permute-start | bytes 811016 | tf_op jit(solution)/shard_map/ppermute | solution.py:571
  13.8 5.7 %collective-permute-start.4 = (bf16[1056,128]{1,0:T(8,128)(2,1)S(1)}, bf16[1056,128]{1,0:T(8,128)(2,1)S(1)}, u32[]{:S(2)}, u32[]{:S(2)}) collective-permute-start(bf16[1056,128]{1,0:T(8,128)(2,1)S(1)} %collective-permute-done.2.left_ref.refs_4_), channel_id=1, source_target_pairs={{0,1},{1,0},{2,3},{3,2},{4,5},{5,4},{6,7},{7,6},{8,9},{9,8},{10,11... | collective-permute-start | bytes 811016 | tf_op jit(solution)/shard_map/ppermute | solution.py:589
  13.8 11.4 %collective-permute-start.5 = (bf16[1056,128]{1,0:T(8,128)(2,1)S(1)}, bf16[1056,128]{1,0:T(8,128)(2,1)S(1)}, u32[]{:S(2)}, u32[]{:S(2)}) collective-permute-start(bf16[1056,128]{1,0:T(8,128)(2,1)S(1)} %collective-permute-done.2.left_ref.refs_4_), channel_id=1, source_target_pairs={{0,6},{1,7},{2,0},{3,1},{4,2},{5,3},{6,4},{7,5},{8,14},{9,15},{10,... | collective-permute-start | bytes 811016 | tf_op jit(solution)/shard_map/ppermute | solution.py:566
  19.5 2.7 %collective-permute-start.3 = (bf16[1056,128]{1,0:T(8,128)(2,1)S(1)}, bf16[1056,128]{1,0:T(8,128)(2,1)S(1)}, u32[]{:S(2)}, u32[]{:S(2)}) collective-permute-start(bf16[1056,128]{1,0:T(8,128)(2,1)S(1)} %collective-permute-done.1.left_ref.refs_2_), channel_id=1, source_target_pairs={{0,1},{1,0},{2,3},{3,2},{4,5},{5,4},{6,7},{7,6},{8,9},{9,8},{10,11... | collective-permute-start | bytes 811016 | tf_op jit(solution)/shard_map/ppermute | solution.py:587
  22.1 4.6 %copy-start.5 = (s32[1,8,1]{1,2,0:T(1,128)S(1)}, s32[1,8,1]{1,2,0:T(1,128)}, u32[]{:S(2)}) copy-start(s32[1,8,1]{1,2,0:T(1,128)} %param.14) | copy-start | bytes 100
  22.1 4.5 %copy-start.7 = (f32[1,128]{1,0:T(1,128)S(1)}, f32[1,128]{1,0:T(1,128)}, u32[]{:S(2)}) copy-start(f32[1,128]{1,0:T(1,128)} %out_gain_ref.1) | copy-start | bytes 1540
  22.2 25.3 %slice-start = ((s8[8388608]{0:T(1024)(128)(4,1)}), s8[4194304]{0:T(1024)(128)(4,1)S(1)}, s32[]{:S(2)}) async-start(s8[8388608]{0:T(1024)(128)(4,1)} %bitcast.14), calls=%async_computation | async-start | bytes 8388608
  22.2 25.3 %slice-start.2 = ((s8[8388608]{0:T(1024)(128)(4,1)}), s8[4194304]{0:T(1024)(128)(4,1)S(1)}, s32[]{:S(2)}) async-start(s8[8388608]{0:T(1024)(128)(4,1)} %bitcast.16), calls=%async_computation.2 | async-start | bytes 8388608
  22.2 25.3 %slice-start.4 = ((s8[8388608]{0:T(1024)(128)(4,1)}), s8[4194304]{0:T(1024)(128)(4,1)S(1)}, s32[]{:S(2)}) async-start(s8[8388608]{0:T(1024)(128)(4,1)} %bitcast.18), calls=%async_computation.4 | async-start | bytes 8388608
  25.1 1.5 %collective-permute-start.6 = (bf16[1056,128]{1,0:T(8,128)(2,1)S(1)}, bf16[1056,128]{1,0:T(8,128)(2,1)S(1)}, u32[]{:S(2)}, u32[]{:S(2)}) collective-permute-start(bf16[1056,128]{1,0:T(8,128)(2,1)S(1)} %collective-permute-done.5.refs_14_.refs_6_), channel_id=1, source_target_pairs={{0,1},{1,0},{2,3},{3,2},{4,5},{5,4},{6,7},{7,6},{8,9},{9,8},{10,11... | collective-permute-start | bytes 811016 | tf_op jit(solution)/shard_map/ppermute | solution.py:592
  26.7 19.2 %copy-start.1 = (bf16[1,1024,1024]{2,1,0:T(8,128)(2,1)S(1)}, bf16[1,1024,1024]{2,1,0:T(8,128)(2,1)}, u32[]{:S(2)}) copy-start(bf16[1,1024,1024]{2,1,0:T(8,128)(2,1)} %param.19) | copy-start | bytes 6291460
  26.7 20.8 %slice-start.1 = ((s8[8388608]{0:T(1024)(128)(4,1)}), s8[4194304]{0:T(1024)(128)(4,1)S(1)}, s32[]{:S(2)}) async-start(s8[8388608]{0:T(1024)(128)(4,1)} %bitcast.14), calls=%async_computation.1 | async-start | bytes 8388608
  26.7 20.8 %slice-start.3 = ((s8[8388608]{0:T(1024)(128)(4,1)}), s8[4194304]{0:T(1024)(128)(4,1)S(1)}, s32[]{:S(2)}) async-start(s8[8388608]{0:T(1024)(128)(4,1)} %bitcast.16), calls=%async_computation.3 | async-start | bytes 8388608
  26.7 20.8 %slice-start.5 = ((s8[8388608]{0:T(1024)(128)(4,1)}), s8[4194304]{0:T(1024)(128)(4,1)S(1)}, s32[]{:S(2)}) async-start(s8[8388608]{0:T(1024)(128)(4,1)} %bitcast.18), calls=%async_computation.5 | async-start | bytes 8388608
  31.0 7.9 %collective-permute-start.8 = (bf16[2,2,128,128]{3,2,1,0:T(8,128)(2,1)S(1)}, bf16[2,2,128,128]{3,2,1,0:T(8,128)(2,1)S(1)}, u32[]{:S(2)}, u32[]{:S(2)}) collective-permute-start(bf16[2,2,128,128]{3,2,1,0:T(8,128)(2,1)S(1)} %get-tuple-element.44), channel_id=1, source_target_pairs={{0,2},{1,3},{2,0},{3,1},{4,6},{5,7},{6,4},{7,5},{8,10},{9,11},{10,... | collective-permute-start | bytes 393224 | tf_op jit(solution)/shard_map/ppermute | solution.py:599
  32.5 12.9 %collective-permute-start.10 = (bf16[2,2,128,128]{3,2,1,0:T(8,128)(2,1)S(1)}, bf16[2,2,128,128]{3,2,1,0:T(8,128)(2,1)S(1)}, u32[]{:S(2)}, u32[]{:S(2)}) collective-permute-start(bf16[2,2,128,128]{3,2,1,0:T(8,128)(2,1)S(1)} %get-tuple-element.45), channel_id=1, source_target_pairs={{0,4},{1,5},{2,6},{3,7},{4,0},{5,1},{6,2},{7,3},{8,12},{9,13},{10,... | collective-permute-start | bytes 393224 | tf_op jit(solution)/shard_map/ppermute | solution.py:599
  35.2 10.2 %collective-permute-start.12 = (bf16[2,2,128,128]{3,2,1,0:T(8,128)(2,1)S(1)}, bf16[2,2,128,128]{3,2,1,0:T(8,128)(2,1)S(1)}, u32[]{:S(2)}, u32[]{:S(2)}) collective-permute-start(bf16[2,2,128,128]{3,2,1,0:T(8,128)(2,1)S(1)} %get-tuple-element.46), channel_id=1, source_target_pairs={{0,6},{1,7},{2,4},{3,5},{4,2},{5,3},{6,0},{7,1},{8,14},{9,15},{10,... | collective-permute-start | bytes 393224 | tf_op jit(solution)/shard_map/ppermute | solution.py:599
  35.5 10.5 %collective-permute-start.7 = (bf16[2,2,128,128]{3,2,1,0:T(8,128)(2,1)S(1)}, bf16[2,2,128,128]{3,2,1,0:T(8,128)(2,1)S(1)}, u32[]{:S(2)}, u32[]{:S(2)}) collective-permute-start(bf16[2,2,128,128]{3,2,1,0:T(8,128)(2,1)S(1)} %get-tuple-element.43.refs_8_), channel_id=1, source_target_pairs={{0,1},{1,0},{2,3},{3,2},{4,5},{5,4},{6,7},{7,6},{8,9},{9,8},{10,11... | collective-permute-start | bytes 393224 | tf_op jit(solution)/shard_map/ppermute | solution.py:601
  38.9 7.0 %collective-permute-start.9 = (bf16[2,2,128,128]{3,2,1,0:T(8,128)(2,1)S(1)}, bf16[2,2,128,128]{3,2,1,0:T(8,128)(2,1)S(1)}, u32[]{:S(2)}, u32[]{:S(2)}) collective-permute-start(bf16[2,2,128,128]{3,2,1,0:T(8,128)(2,1)S(1)} %collective-permute-done.8.refs_10_), channel_id=1, source_target_pairs={{0,1},{1,0},{2,3},{3,2},{4,5},{5,4},{6,7},{7,6},{8,9},{9,8},{10,11... | collective-permute-start | bytes 393224 | tf_op jit(solution)/shard_map/ppermute | solution.py:601
  45.4 2.0 %collective-permute-start.11 = (bf16[2,2,128,128]{3,2,1,0:T(8,128)(2,1)S(1)}, bf16[2,2,128,128]{3,2,1,0:T(8,128)(2,1)S(1)}, u32[]{:S(2)}, u32[]{:S(2)}) collective-permute-start(bf16[2,2,128,128]{3,2,1,0:T(8,128)(2,1)S(1)} %collective-permute-done.10.refs_0_), channel_id=1, source_target_pairs={{0,1},{1,0},{2,3},{3,2},{4,5},{5,4},{6,7},{7,6},{8,9},{9,8},{10,11... | collective-permute-start | bytes 393224 | tf_op jit(solution)/shard_map/ppermute | solution.py:603
  45.4 2.0 %collective-permute-start.13 = (bf16[2,2,128,128]{3,2,1,0:T(8,128)(2,1)S(1)}, bf16[2,2,128,128]{3,2,1,0:T(8,128)(2,1)S(1)}, u32[]{:S(2)}, u32[]{:S(2)}) collective-permute-start(bf16[2,2,128,128]{3,2,1,0:T(8,128)(2,1)S(1)} %collective-permute-done.12.refs_2_), channel_id=1, source_target_pairs={{0,1},{1,0},{2,3},{3,2},{4,5},{5,4},{6,7},{7,6},{8,9},{9,8},{10,11... | collective-permute-start | bytes 393224 | tf_op jit(solution)/shard_map/ppermute | solution.py:603
  45.9 1.6 %copy-start.4 = (f32[1,1024]{1,0:T(1,128)S(1)}, f32[1,1024]{1,0:T(1,128)}, u32[]{:S(2)}) copy-start(f32[1,1024]{1,0:T(1,128)} %gain_ref.7) | copy-start | bytes 12292
  54.9 2.0 %collective-permute-start.14 = (bf16[256,1024]{1,0:T(8,128)(2,1)S(1)}, bf16[256,1024]{1,0:T(8,128)(2,1)S(1)}, u32[]{:S(2)}, u32[]{:S(2)}) collective-permute-start(bf16[256,1024]{1,0:T(8,128)(2,1)S(1)} %expert.1.own_ref), channel_id=1, source_target_pairs={{0,1},{1,0},{2,3},{3,2},{4,5},{5,4},{6,7},{7,6},{8,9},{9,8},{10,11... | collective-permute-start | bytes 1572872 | tf_op jit(solution)/shard_map/ppermute | solution.py:625
  57.7 9.1 %collective-permute-start.15 = (bf16[128,1024]{1,0:T(8,128)(2,1)S(1)}, bf16[128,1024]{1,0:T(8,128)(2,1)S(1)}, u32[]{:S(2)}, u32[]{:S(2)}) collective-permute-start(bf16[128,1024]{1,0:T(8,128)(2,1)S(1)} %get-tuple-element.47), channel_id=1, source_target_pairs={{0,6},{1,7},{2,0},{3,1},{4,2},{5,3},{6,4},{7,5},{8,14},{9,15},{10,... | collective-permute-start | bytes 786440 | tf_op jit(solution)/shard_map/ppermute | solution.py:566
  60.1 16.9 %collective-permute-start.17 = (bf16[128,1024]{1,0:T(8,128)(2,1)S(1)}, bf16[128,1024]{1,0:T(8,128)(2,1)S(1)}, u32[]{:S(2)}, u32[]{:S(2)}) collective-permute-start(bf16[128,1024]{1,0:T(8,128)(2,1)S(1)} %get-tuple-element.49), channel_id=1, source_target_pairs={{0,10},{1,11},{2,12},{3,13},{4,14},{5,15},{6,8},{7,9},{8,18},{9,19... | collective-permute-start | bytes 786440 | tf_op jit(solution)/shard_map/ppermute | solution.py:623
  60.9 18.6 %collective-permute-start.18 = (bf16[128,1024]{1,0:T(8,128)(2,1)S(1)}, bf16[128,1024]{1,0:T(8,128)(2,1)S(1)}, u32[]{:S(2)}, u32[]{:S(2)}) collective-permute-start(bf16[128,1024]{1,0:T(8,128)(2,1)S(1)} %get-tuple-element.50), channel_id=1, source_target_pairs={{0,8},{1,9},{2,10},{3,11},{4,12},{5,13},{6,14},{7,15},{8,16},{9,17... | collective-permute-start | bytes 786440 | tf_op jit(solution)/shard_map/ppermute | solution.py:623
  66.8 15.0 %collective-permute-start.16 = (bf16[128,1024]{1,0:T(8,128)(2,1)S(1)}, bf16[128,1024]{1,0:T(8,128)(2,1)S(1)}, u32[]{:S(2)}, u32[]{:S(2)}) collective-permute-start(bf16[128,1024]{1,0:T(8,128)(2,1)S(1)} %add.34), channel_id=1, source_target_pairs={{0,14},{1,15},{2,8},{3,9},{4,10},{5,11},{6,12},{7,13},{8,22},{9,23... | collective-permute-start | bytes 786440 | tf_op jit(solution)/shard_map/ppermute | solution.py:623
  (1 other events, 0.7 us)

commit v6 on v5

--- a/solution.py
+++ b/solution.py
@@ -596,7 +596,9 @@
     else:
         sends = mix(kinds, out_gain, known, late=(norm_gain, weight, *last))
 
-    got = [sends[0]] + [lax.ppermute(sends[k], "seq", chip_route(count, k)) for k in range(1, CHIPS)]
+    got = [sends[0], None, None, None]
+    for k in (3, 2, 1):
+        got[k] = lax.ppermute(sends[k], "seq", chip_route(count, k))
     blocks = [block for two in near + [last] for block in two]
     near_heads = [got[0], pair(got[0]), got[1], pair(got[1])]
     early = early_project(kinds, out_weight[0], blocks, near_heads)

time: 82.7 us -> 82.8 us (level)
  no operation moved by 1% of the time
where the time goes in v6:
time: 82.8 us; the launch traced here: 82.6 us
  waiting for transfers between devices  31.6 us (38%)
  starting transfers between devices  24.7 us (30%)
  Pallas kernels  21.9 us (26%)
  local copies, waits for them, and re-layouts  3.14 us (4%)
  other arithmetic  0.93 us (1%)
    ppermute x4, starting transfers between devices, hop(): return lax.ppermute(block, 'seq', lane_route(count, by))  11.7 us
    ppermute x3, waiting for transfers between devices, per_device(): got[k] = lax.ppermute(sends[k], 'seq', chip_route(count, k))  9.93 us
    ppermute x3, waiting for transfers between devices, send_home(): lax.ppermute(block, ('segment', 'seq'), home_route(sections, count, by))  9.79 us
    ppermute x4, waiting for transfers between devices, hop(): return lax.ppermute(block, 'seq', lane_route(count, by))  8.75 us
    pallas_call x3, Pallas kernels, terms(): pl.pallas_call(terms_kernel, out_shape=tuple((jax.ShapeDtypeStruct(*s) fo...  7.9 us
    ppermute x3, starting transfers between devices, send_home(): lax.ppermute(block, ('segment', 'seq'), home_route(sections, count, by))  7.63 us
    pallas_call x1, Pallas kernels, expert(): pl.pallas_call(partial(expert_kernel, min(512, gate.shape[3])), out_shape...  7.37 us
    ppermute x3, starting transfers between devices, per_device(): got[k] = lax.ppermute(sends[k], 'seq', chip_route(count, k))  4.45 us
  transfers between devices with their start and end apart: 19, of which 11 were waited for; matrix products, arithmetic and copies ran while one was open for 2% of the time, Pallas kernels for 11%

profile of v6, /device:TPU:0, one launch (start us, length us, event | category | flops | bytes accessed | tf_op | source)
XLA Modules:
  0.0 82.6 jit_solution(17980592365302394418)
XLA Ops:
  0.0 1.0 %copy-done.2 = bf16[1,128,1024]{2,1,0:T(8,128)(2,1)S(1)} copy-done((bf16[1,128,1024]{2,1,0:T(8,128)(2,1)S(1)}, bf16[1,128,1024]{2,1,0:T(8,128)(2,1)}, u32[]{:S(2)}) %copy-start.2) | copy-done | bytes 262168
  1.0 0.7 copy-done.3
  1.8 5.1 %collective-permute-start.2 = (bf16[1056,128]{1,0:T(8,128)(2,1)S(1)}, bf16[1056,128]{1,0:T(8,128)(2,1)S(1)}, u32[]{:S(2)}, u32[]{:S(2)}) collective-permute-start(bf16[1056,128]{1,0:T(8,128)(2,1)S(1)} %attach_decay.1.left_ref.refs_0_), channel_id=1, source_target_pairs={{0,6},{1,7},{2,0},{3,1},{4,2},{5,3},{6,4},{7,5},{8,14},{9,15},{10,... | collective-permute-start | bytes 811016 | tf_op jit(solution)/shard_map/ppermute | solution.py:566
  6.9 1.2 %dynamic-slice_bitcast_fusion.2 = (bf16[1024,128]{1,0:T(8,128)(2,1)S(1)}, bf16[1024,128]{1,0:T(8,128)(2,1)S(1)}, bf16[1024,128]{1,0:T(8,128)(2,1)S(1)}) fusion(bf16[1,1024,3072]{2,1,0:T(8,128)(2,1)} %param.16, s32[]{:T(128)S(6)} %select_n.20, s32[]{:T(128)S(6)} %select_n.22, s32[]{:T(128)S(6)} %select_n.21), kind=kLoop, calls=%fused_computation.4 | loop fusion | bytes 1572876 | tf_op jit(solution)/shard_map/dynamic_slice | solution.py:574
  8.4 2.6 %chunk_terms.3 = (bf16[2,128,128]{2,1,0:T(8,128)(2,1)S(1)}, f32[2,128,128]{2,1,0:T(8,128)S(1)}, f32[2,256,128]{2,1,0:T(8,128)S(1)}, f32[2,8,128]{2,1,0:T(8,128)S(1)}) custom-call(f32[1,1024]{1,0:T(1,128)S(1)} %copy-done.6, bf16[1024,512]{1,0:T(8,128)(2,1)S(1)} %pad_maximum_fusion.weight_ref.refs_13_, bf16[1056,128]{1,0:T(8,128)(2,1)S(1)} %attach_decay.1.left_ref.refs_0_, ...), custom_call_target="tpu_custom_call" | custom-call | flops 4000000000 | bytes 3000000 | tf_op jit(solution)/shard_map/chunk_terms/pallas_call | solution.py:274
  11.1 2.7 %collective-permute-done.2.left_ref.refs_4_ = bf16[1056,128]{1,0:T(8,128)(2,1)S(1)} collective-permute-done((bf16[1056,128]{1,0:T(8,128)(2,1)S(1)}, bf16[1056,128]{1,0:T(8,128)(2,1)S(1)}, u32[]{:S(2)}, u32[]{:S(2)}) %collective-permute-start.2) | collective-permute-done | bytes 270368 | tf_op jit(solution)/shard_map/ppermute | solution.py:566
  13.8 4.3 %collective-permute-start.5 = (bf16[1056,128]{1,0:T(8,128)(2,1)S(1)}, bf16[1056,128]{1,0:T(8,128)(2,1)S(1)}, u32[]{:S(2)}, u32[]{:S(2)}) collective-permute-start(bf16[1056,128]{1,0:T(8,128)(2,1)S(1)} %collective-permute-done.2.left_ref.refs_4_), channel_id=1, source_target_pairs={{0,6},{1,7},{2,0},{3,1},{4,2},{5,3},{6,4},{7,5},{8,14},{9,15},{10,... | collective-permute-start | bytes 811016 | tf_op jit(solution)/shard_map/ppermute | solution.py:566
  18.0 1.4 %collective-permute-done.1.left_ref.refs_2_ = bf16[1056,128]{1,0:T(8,128)(2,1)S(1)} collective-permute-done((bf16[1056,128]{1,0:T(8,128)(2,1)S(1)}, bf16[1056,128]{1,0:T(8,128)(2,1)S(1)}, u32[]{:S(2)}, u32[]{:S(2)}) %collective-permute-start.1) | collective-permute-done | bytes 270368 | tf_op jit(solution)/shard_map/ppermute | solution.py:566
  19.5 2.6 %chunk_terms.5 = (bf16[2,128,128]{2,1,0:T(8,128)(2,1)S(1)}, f32[2,128,128]{2,1,0:T(8,128)S(1)}, f32[2,256,128]{2,1,0:T(8,128)S(1)}, f32[2,8,128]{2,1,0:T(8,128)S(1)}) custom-call(f32[1,1024]{1,0:T(1,128)S(1)} %copy-done.6, bf16[1024,512]{1,0:T(8,128)(2,1)S(1)} %pad_maximum_fusion.weight_ref.refs_13_, ...), custom_call_target="tpu_custom_call" | custom-call | flops 4000000000 | bytes 3000000 | tf_op jit(solution)/shard_map/chunk_terms/pallas_call | solution.py:274
  22.2 2.6 %chunk_terms.4 = (bf16[2,128,128]{2,1,0:T(8,128)(2,1)S(1)}, f32[2,128,128]{2,1,0:T(8,128)S(1)}, f32[2,256,128]{2,1,0:T(8,128)S(1)}, f32[2,8,128]{2,1,0:T(8,128)S(1)}) custom-call(f32[1,1024]{1,0:T(1,128)S(1)} %copy-done.6, bf16[1024,512]{1,0:T(8,128)(2,1)S(1)} %pad_maximum_fusion.weight_ref.refs_13_, ...), custom_call_target="tpu_custom_call" | custom-call | flops 4000000000 | bytes 3000000 | tf_op jit(solution)/shard_map/chunk_terms/pallas_call | solution.py:274
  24.8 0.3 collective-permute-done.5.refs_14_.refs_6_
  25.1 0.3 collective-permute-start.6
  25.4 1.3 %collective-permute-done.6.refs_15_.refs_7_ = bf16[1056,128]{1,0:T(8,128)(2,1)S(1)} collective-permute-done((bf16[1056,128]{1,0:T(8,128)(2,1)S(1)}, bf16[1056,128]{1,0:T(8,128)(2,1)S(1)}, u32[]{:S(2)}, u32[]{:S(2)}) %collective-permute-start.6) | collective-permute-done | bytes 270368 | tf_op jit(solution)/shard_map/ppermute | solution.py:592
  26.7 4.3 %state_walk.1 = (bf16[2,2,128,128]{3,2,1,0:T(8,128)(2,1)S(1)}, bf16[2,2,128,128]{3,2,1,0:T(8,128)(2,1)S(1)}, bf16[2,2,128,128]{3,2,1,0:T(8,128)(2,1)S(1)}, bf16[2,2,128,128]{3,2,1,0:T(8,128)(2,1)S(1)}) custom-call(s32[8]{0:T(128)S(1)} %bitcast.24, f32[1,128]{1,0:T(1,128)S(1)} %copy-done.7, bf16[2,128,128]{2,1,0:T(8,128)(2,1)S(1)} %get-tuple-element.28.refs_0_, ...), custom_call_target="tpu_custom_call" | custom-call | flops 30000001024 | bytes 4000000 | tf_op jit(solution)/shard_map/state_walk/pallas_call | solution.py:343
  31.0 1.5 %collective-permute-start.8 = (bf16[2,2,128,128]{3,2,1,0:T(8,128)(2,1)S(1)}, bf16[2,2,128,128]{3,2,1,0:T(8,128)(2,1)S(1)}, u32[]{:S(2)}, u32[]{:S(2)}) collective-permute-start(bf16[2,2,128,128]{3,2,1,0:T(8,128)(2,1)S(1)} %get-tuple-element.44), channel_id=1, source_target_pairs={{0,2},{1,3},{2,0},{3,1},{4,6},{5,7},{6,4},{7,5},{8,10},{9,11},{10,... | collective-permute-start | bytes 393224 | tf_op jit(solution)/shard_map/ppermute | solution.py:601
  32.5 2.8 %collective-permute-start.10 = (bf16[2,2,128,128]{3,2,1,0:T(8,128)(2,1)S(1)}, bf16[2,2,128,128]{3,2,1,0:T(8,128)(2,1)S(1)}, u32[]{:S(2)}, u32[]{:S(2)}) collective-permute-start(bf16[2,2,128,128]{3,2,1,0:T(8,128)(2,1)S(1)} %get-tuple-element.45), channel_id=1, source_target_pairs={{0,4},{1,5},{2,6},{3,7},{4,0},{5,1},{6,2},{7,3},{8,12},{9,13},{10,... | collective-permute-start | bytes 393224 | tf_op jit(solution)/shard_map/ppermute | solution.py:601
  35.5 3.4 %collective-permute-done.8.refs_10_ = bf16[2,2,128,128]{3,2,1,0:T(8,128)(2,1)S(1)} collective-permute-done((bf16[2,2,128,128]{3,2,1,0:T(8,128)(2,1)S(1)}, bf16[2,2,128,128]{3,2,1,0:T(8,128)(2,1)S(1)}, u32[]{:S(2)}, u32[]{:S(2)}) %collective-permute-start.8) | collective-permute-done | bytes 131104 | tf_op jit(solution)/shard_map/ppermute | solution.py:601
  38.9 6.5 %collective-permute-done.10.refs_0_ = bf16[2,2,128,128]{3,2,1,0:T(8,128)(2,1)S(1)} collective-permute-done((bf16[2,2,128,128]{3,2,1,0:T(8,128)(2,1)S(1)}, bf16[2,2,128,128]{3,2,1,0:T(8,128)(2,1)S(1)}, u32[]{:S(2)}, u32[]{:S(2)}) %collective-permute-start.10) | collective-permute-done | bytes 131104 | tf_op jit(solution)/shard_map/ppermute | solution.py:601
  45.4 0.5 collective-permute-start.13
  45.9 1.5 %early_project.1.early_ref = f32[256,1024]{1,0:T(8,128)S(1)} custom-call(s32[8]{0:T(128)S(1)} %bitcast.25, bf16[1024,1024]{1,0:T(8,128)(2,1)S(1)} %bitcast.20, bf16[1056,128]{1,0:T(8,128)(2,1)S(1)} %attach_decay.1.left_ref.refs_0_, bf16[1056,128]{1,0:T(8,128)(2,1)S(1)} %collective-permute-done.right_ref.refs_1_, ...), custom_call_target="tpu_custom_call" | custom-call | tf_op jit(solution)/shard_map/early_project/pallas_call | solution.py:436
  47.5 7.4 %expert.1.own_ref = bf16[256,1024]{1,0:T(8,128)(2,1)S(1)} custom-call(f32[1,1024]{1,0:T(1,128)S(1)} %copy-done.4, bf16[1024,1024]{1,0:T(8,128)(2,1)S(1)} %bitcast.21, f32[256,1024]{1,0:T(8,128)S(1)} %early_project.1.early_ref, bf16[2,2,128,128]{3,2,1,0:T(8,128)(2,1)S(1)} %collective-permute-done.10.refs_0_, ...), custom_call_target="tpu_custom_call" | custom-call | tf_op jit(solution)/shard_map/expert/pallas_call | solution.py:486
  55.0 1.9 %collective-permute-done.14.other_ref = bf16[256,1024]{1,0:T(8,128)(2,1)S(1)} collective-permute-done((bf16[256,1024]{1,0:T(8,128)(2,1)S(1)}, bf16[256,1024]{1,0:T(8,128)(2,1)S(1)}, u32[]{:S(2)}, u32[]{:S(2)}) %collective-permute-start.14) | collective-permute-done | bytes 524320 | tf_op jit(solution)/shard_map/ppermute | solution.py:627
  56.9 0.8 homeward.1
  57.7 2.3 %collective-permute-start.15 = (bf16[128,1024]{1,0:T(8,128)(2,1)S(1)}, bf16[128,1024]{1,0:T(8,128)(2,1)S(1)}, u32[]{:S(2)}, u32[]{:S(2)}) collective-permute-start(bf16[128,1024]{1,0:T(8,128)(2,1)S(1)} %get-tuple-element.47), channel_id=1, source_target_pairs={{0,6},{1,7},{2,0},{3,1},{4,2},{5,3},{6,4},{7,5},{8,14},{9,15},{10,... | collective-permute-start | bytes 786440 | tf_op jit(solution)/shard_map/ppermute | solution.py:566
  60.0 0.8 collective-permute-start.17
  60.9 1.5 %collective-permute-start.18 = (bf16[128,1024]{1,0:T(8,128)(2,1)S(1)}, bf16[128,1024]{1,0:T(8,128)(2,1)S(1)}, u32[]{:S(2)}, u32[]{:S(2)}) collective-permute-start(bf16[128,1024]{1,0:T(8,128)(2,1)S(1)} %get-tuple-element.50), channel_id=1, source_target_pairs={{0,8},{1,9},{2,10},{3,11},{4,12},{5,13},{6,14},{7,15},{8,16},{9,17... | collective-permute-start | bytes 786440 | tf_op jit(solution)/shard_map/ppermute | solution.py:625
  62.4 4.4 %collective-permute-done.15 = bf16[128,1024]{1,0:T(8,128)(2,1)S(1)} collective-permute-done((bf16[128,1024]{1,0:T(8,128)(2,1)S(1)}, bf16[128,1024]{1,0:T(8,128)(2,1)S(1)}, u32[]{:S(2)}, u32[]{:S(2)}) %collective-permute-start.15) | collective-permute-done | bytes 262176 | tf_op jit(solution)/shard_map/ppermute | solution.py:566
  66.8 5.3 %collective-permute-start.16 = (bf16[128,1024]{1,0:T(8,128)(2,1)S(1)}, bf16[128,1024]{1,0:T(8,128)(2,1)S(1)}, u32[]{:S(2)}, u32[]{:S(2)}) collective-permute-start(bf16[128,1024]{1,0:T(8,128)(2,1)S(1)} %add.34), channel_id=1, source_target_pairs={{0,14},{1,15},{2,8},{3,9},{4,10},{5,11},{6,12},{7,13},{8,22},{9,23... | collective-permute-start | bytes 786440 | tf_op jit(solution)/shard_map/ppermute | solution.py:625
  72.1 4.7 %collective-permute-done.17 = bf16[128,1024]{1,0:T(8,128)(2,1)S(1)} collective-permute-done((bf16[128,1024]{1,0:T(8,128)(2,1)S(1)}, bf16[128,1024]{1,0:T(8,128)(2,1)S(1)}, u32[]{:S(2)}, u32[]{:S(2)}) %collective-permute-start.17) | collective-permute-done | bytes 262176 | tf_op jit(solution)/shard_map/ppermute | solution.py:625
  76.9 2.6 %collective-permute-done.18 = bf16[128,1024]{1,0:T(8,128)(2,1)S(1)} collective-permute-done((bf16[128,1024]{1,0:T(8,128)(2,1)S(1)}, bf16[128,1024]{1,0:T(8,128)(2,1)S(1)}, u32[]{:S(2)}, u32[]{:S(2)}) %collective-permute-start.18) | collective-permute-done | bytes 262176 | tf_op jit(solution)/shard_map/ppermute | solution.py:625
  79.5 2.4 %collective-permute-done.16 = bf16[128,1024]{1,0:T(8,128)(2,1)S(1)} collective-permute-done((bf16[128,1024]{1,0:T(8,128)(2,1)S(1)}, bf16[128,1024]{1,0:T(8,128)(2,1)S(1)}, u32[]{:S(2)}, u32[]{:S(2)}) %collective-permute-start.16) | collective-permute-done | bytes 262176 | tf_op jit(solution)/shard_map/ppermute | solution.py:625
  81.9 0.7 add_bitcast_fusion
  (51 shorter events, 0.9 us)
Async XLA Ops:
  0.0 6.9 %copy-start = (bf16[1,1024,8]{1,2,0:T(8,128)(2,1)S(1)}, bf16[1,1024,8]{1,2,0:T(8,128)(2,1)}, u32[]{:S(2)}) copy-start(bf16[1,1024,8]{1,2,0:T(8,128)(2,1)} %param.17) | copy-start | bytes 49156
  0.0 1.0 %copy-start.2 = (bf16[1,128,1024]{2,1,0:T(8,128)(2,1)S(1)}, bf16[1,128,1024]{2,1,0:T(8,128)(2,1)}, u32[]{:S(2)}) copy-start(bf16[1,128,1024]{2,1,0:T(8,128)(2,1)} %param.12) | copy-start | bytes 786436
  1.8 6.7 %copy-start.6 = (f32[1,1024]{1,0:T(1,128)S(1)}, f32[1,1024]{1,0:T(1,128)}, u32[]{:S(2)}) copy-start(f32[1,1024]{1,0:T(1,128)} %refs_12_.1) | copy-start | bytes 12292
  1.8 12.0 %collective-permute-start.2 = (bf16[1056,128]{1,0:T(8,128)(2,1)S(1)}, bf16[1056,128]{1,0:T(8,128)(2,1)S(1)}, u32[]{:S(2)}, u32[]{:S(2)}) collective-permute-start(bf16[1056,128]{1,0:T(8,128)(2,1)S(1)} %attach_decay.1.left_ref.refs_0_), channel_id=1, source_target_pairs={{0,6},{1,7},{2,0},{3,1},{4,2},{5,3},{6,4},{7,5},{8,14},{9,15},{10,... | collective-permute-start | bytes 811016 | tf_op jit(solution)/shard_map/ppermute | solution.py:566
  6.9 12.6 %collective-permute-start.1 = (bf16[1056,128]{1,0:T(8,128)(2,1)S(1)}, bf16[1056,128]{1,0:T(8,128)(2,1)S(1)}, u32[]{:S(2)}, u32[]{:S(2)}) collective-permute-start(bf16[1056,128]{1,0:T(8,128)(2,1)S(1)} %attach_decay.1.left_ref.refs_0_), channel_id=1, source_target_pairs={{0,2},{1,3},{2,4},{3,5},{4,6},{5,7},{6,0},{7,1},{8,10},{9,11},{10,... | collective-permute-start | bytes 811016 | tf_op jit(solution)/shard_map/ppermute | solution.py:566
  6.9 1.6 %collective-permute-start = (bf16[1056,128]{1,0:T(8,128)(2,1)S(1)}, bf16[1056,128]{1,0:T(8,128)(2,1)S(1)}, u32[]{:S(2)}, u32[]{:S(2)}) collective-permute-start(bf16[1056,128]{1,0:T(8,128)(2,1)S(1)} %attach_decay.1.left_ref.refs_0_), channel_id=1, source_target_pairs={{0,1},{1,0},{2,3},{3,2},{4,5},{5,4},{6,7},{7,6},{8,9},{9,8},{10,11... | collective-permute-start | bytes 811016 | tf_op jit(solution)/shard_map/ppermute | solution.py:571
  13.8 5.7 %collective-permute-start.4 = (bf16[1056,128]{1,0:T(8,128)(2,1)S(1)}, bf16[1056,128]{1,0:T(8,128)(2,1)S(1)}, u32[]{:S(2)}, u32[]{:S(2)}) collective-permute-start(bf16[1056,128]{1,0:T(8,128)(2,1)S(1)} %collective-permute-done.2.left_ref.refs_4_), channel_id=1, source_target_pairs={{0,1},{1,0},{2,3},{3,2},{4,5},{5,4},{6,7},{7,6},{8,9},{9,8},{10,11... | collective-permute-start | bytes 811016 | tf_op jit(solution)/shard_map/ppermute | solution.py:589
  13.8 11.4 %collective-permute-start.5 = (bf16[1056,128]{1,0:T(8,128)(2,1)S(1)}, bf16[1056,128]{1,0:T(8,128)(2,1)S(1)}, u32[]{:S(2)}, u32[]{:S(2)}) collective-permute-start(bf16[1056,128]{1,0:T(8,128)(2,1)S(1)} %collective-permute-done.2.left_ref.refs_4_), channel_id=1, source_target_pairs={{0,6},{1,7},{2,0},{3,1},{4,2},{5,3},{6,4},{7,5},{8,14},{9,15},{10,... | collective-permute-start | bytes 811016 | tf_op jit(solution)/shard_map/ppermute | solution.py:566
  19.5 2.7 %collective-permute-start.3 = (bf16[1056,128]{1,0:T(8,128)(2,1)S(1)}, bf16[1056,128]{1,0:T(8,128)(2,1)S(1)}, u32[]{:S(2)}, u32[]{:S(2)}) collective-permute-start(bf16[1056,128]{1,0:T(8,128)(2,1)S(1)} %collective-permute-done.1.left_ref.refs_2_), channel_id=1, source_target_pairs={{0,1},{1,0},{2,3},{3,2},{4,5},{5,4},{6,7},{7,6},{8,9},{9,8},{10,11... | collective-permute-start | bytes 811016 | tf_op jit(solution)/shard_map/ppermute | solution.py:587
  22.1 4.6 %copy-start.5 = (s32[1,8,1]{1,2,0:T(1,128)S(1)}, s32[1,8,1]{1,2,0:T(1,128)}, u32[]{:S(2)}) copy-start(s32[1,8,1]{1,2,0:T(1,128)} %param.14) | copy-start | bytes 100
  22.1 4.5 %copy-start.7 = (f32[1,128]{1,0:T(1,128)S(1)}, f32[1,128]{1,0:T(1,128)}, u32[]{:S(2)}) copy-start(f32[1,128]{1,0:T(1,128)} %out_gain_ref.1) | copy-start | bytes 1540
  22.2 25.3 %slice-start = ((s8[8388608]{0:T(1024)(128)(4,1)}), s8[4194304]{0:T(1024)(128)(4,1)S(1)}, s32[]{:S(2)}) async-start(s8[8388608]{0:T(1024)(128)(4,1)} %bitcast.14), calls=%async_computation | async-start | bytes 8388608
  22.2 25.3 %slice-start.2 = ((s8[8388608]{0:T(1024)(128)(4,1)}), s8[4194304]{0:T(1024)(128)(4,1)S(1)}, s32[]{:S(2)}) async-start(s8[8388608]{0:T(1024)(128)(4,1)} %bitcast.16), calls=%async_computation.2 | async-start | bytes 8388608
  22.2 25.3 %slice-start.4 = ((s8[8388608]{0:T(1024)(128)(4,1)}), s8[4194304]{0:T(1024)(128)(4,1)S(1)}, s32[]{:S(2)}) async-start(s8[8388608]{0:T(1024)(128)(4,1)} %bitcast.18), calls=%async_computation.4 | async-start | bytes 8388608
  25.1 1.5 %collective-permute-start.6 = (bf16[1056,128]{1,0:T(8,128)(2,1)S(1)}, bf16[1056,128]{1,0:T(8,128)(2,1)S(1)}, u32[]{:S(2)}, u32[]{:S(2)}) collective-permute-start(bf16[1056,128]{1,0:T(8,128)(2,1)S(1)} %collective-permute-done.5.refs_14_.refs_6_), channel_id=1, source_target_pairs={{0,1},{1,0},{2,3},{3,2},{4,5},{5,4},{6,7},{7,6},{8,9},{9,8},{10,11... | collective-permute-start | bytes 811016 | tf_op jit(solution)/shard_map/ppermute | solution.py:592
  26.7 19.2 %copy-start.1 = (bf16[1,1024,1024]{2,1,0:T(8,128)(2,1)S(1)}, bf16[1,1024,1024]{2,1,0:T(8,128)(2,1)}, u32[]{:S(2)}) copy-start(bf16[1,1024,1024]{2,1,0:T(8,128)(2,1)} %param.19) | copy-start | bytes 6291460
  26.7 20.8 %slice-start.1 = ((s8[8388608]{0:T(1024)(128)(4,1)}), s8[4194304]{0:T(1024)(128)(4,1)S(1)}, s32[]{:S(2)}) async-start(s8[8388608]{0:T(1024)(128)(4,1)} %bitcast.14), calls=%async_computation.1 | async-start | bytes 8388608
  26.7 20.8 %slice-start.3 = ((s8[8388608]{0:T(1024)(128)(4,1)}), s8[4194304]{0:T(1024)(128)(4,1)S(1)}, s32[]{:S(2)}) async-start(s8[8388608]{0:T(1024)(128)(4,1)} %bitcast.16), calls=%async_computation.3 | async-start | bytes 8388608
  26.7 20.8 %slice-start.5 = ((s8[8388608]{0:T(1024)(128)(4,1)}), s8[4194304]{0:T(1024)(128)(4,1)S(1)}, s32[]{:S(2)}) async-start(s8[8388608]{0:T(1024)(128)(4,1)} %bitcast.18), calls=%async_computation.5 | async-start | bytes 8388608
  31.0 7.9 %collective-permute-start.8 = (bf16[2,2,128,128]{3,2,1,0:T(8,128)(2,1)S(1)}, bf16[2,2,128,128]{3,2,1,0:T(8,128)(2,1)S(1)}, u32[]{:S(2)}, u32[]{:S(2)}) collective-permute-start(bf16[2,2,128,128]{3,2,1,0:T(8,128)(2,1)S(1)} %get-tuple-element.44), channel_id=1, source_target_pairs={{0,2},{1,3},{2,0},{3,1},{4,6},{5,7},{6,4},{7,5},{8,10},{9,11},{10,... | collective-permute-start | bytes 393224 | tf_op jit(solution)/shard_map/ppermute | solution.py:601
  32.5 12.9 %collective-permute-start.10 = (bf16[2,2,128,128]{3,2,1,0:T(8,128)(2,1)S(1)}, bf16[2,2,128,128]{3,2,1,0:T(8,128)(2,1)S(1)}, u32[]{:S(2)}, u32[]{:S(2)}) collective-permute-start(bf16[2,2,128,128]{3,2,1,0:T(8,128)(2,1)S(1)} %get-tuple-element.45), channel_id=1, source_target_pairs={{0,4},{1,5},{2,6},{3,7},{4,0},{5,1},{6,2},{7,3},{8,12},{9,13},{10,... | collective-permute-start | bytes 393224 | tf_op jit(solution)/shard_map/ppermute | solution.py:601
  35.2 10.2 %collective-permute-start.12 = (bf16[2,2,128,128]{3,2,1,0:T(8,128)(2,1)S(1)}, bf16[2,2,128,128]{3,2,1,0:T(8,128)(2,1)S(1)}, u32[]{:S(2)}, u32[]{:S(2)}) collective-permute-start(bf16[2,2,128,128]{3,2,1,0:T(8,128)(2,1)S(1)} %get-tuple-element.46), channel_id=1, source_target_pairs={{0,6},{1,7},{2,4},{3,5},{4,2},{5,3},{6,0},{7,1},{8,14},{9,15},{10,... | collective-permute-start | bytes 393224 | tf_op jit(solution)/shard_map/ppermute | solution.py:601
  35.5 10.5 %collective-permute-start.7 = (bf16[2,2,128,128]{3,2,1,0:T(8,128)(2,1)S(1)}, bf16[2,2,128,128]{3,2,1,0:T(8,128)(2,1)S(1)}, u32[]{:S(2)}, u32[]{:S(2)}) collective-permute-start(bf16[2,2,128,128]{3,2,1,0:T(8,128)(2,1)S(1)} %get-tuple-element.43.refs_8_), channel_id=1, source_target_pairs={{0,1},{1,0},{2,3},{3,2},{4,5},{5,4},{6,7},{7,6},{8,9},{9,8},{10,11... | collective-permute-start | bytes 393224 | tf_op jit(solution)/shard_map/ppermute | solution.py:603
  38.9 7.0 %collective-permute-start.9 = (bf16[2,2,128,128]{3,2,1,0:T(8,128)(2,1)S(1)}, bf16[2,2,128,128]{3,2,1,0:T(8,128)(2,1)S(1)}, u32[]{:S(2)}, u32[]{:S(2)}) collective-permute-start(bf16[2,2,128,128]{3,2,1,0:T(8,128)(2,1)S(1)} %collective-permute-done.8.refs_10_), channel_id=1, source_target_pairs={{0,1},{1,0},{2,3},{3,2},{4,5},{5,4},{6,7},{7,6},{8,9},{9,8},{10,11... | collective-permute-start | bytes 393224 | tf_op jit(solution)/shard_map/ppermute | solution.py:603
  45.4 2.0 %collective-permute-start.11 = (bf16[2,2,128,128]{3,2,1,0:T(8,128)(2,1)S(1)}, bf16[2,2,128,128]{3,2,1,0:T(8,128)(2,1)S(1)}, u32[]{:S(2)}, u32[]{:S(2)}) collective-permute-start(bf16[2,2,128,128]{3,2,1,0:T(8,128)(2,1)S(1)} %collective-permute-done.10.refs_0_), channel_id=1, source_target_pairs={{0,1},{1,0},{2,3},{3,2},{4,5},{5,4},{6,7},{7,6},{8,9},{9,8},{10,11... | collective-permute-start | bytes 393224 | tf_op jit(solution)/shard_map/ppermute | solution.py:605
  45.4 2.0 %collective-permute-start.13 = (bf16[2,2,128,128]{3,2,1,0:T(8,128)(2,1)S(1)}, bf16[2,2,128,128]{3,2,1,0:T(8,128)(2,1)S(1)}, u32[]{:S(2)}, u32[]{:S(2)}) collective-permute-start(bf16[2,2,128,128]{3,2,1,0:T(8,128)(2,1)S(1)} %collective-permute-done.12.refs_2_), channel_id=1, source_target_pairs={{0,1},{1,0},{2,3},{3,2},{4,5},{5,4},{6,7},{7,6},{8,9},{9,8},{10,11... | collective-permute-start | bytes 393224 | tf_op jit(solution)/shard_map/ppermute | solution.py:605
  45.9 1.6 %copy-start.4 = (f32[1,1024]{1,0:T(1,128)S(1)}, f32[1,1024]{1,0:T(1,128)}, u32[]{:S(2)}) copy-start(f32[1,1024]{1,0:T(1,128)} %gain_ref.7) | copy-start | bytes 12292
  54.9 2.0 %collective-permute-start.14 = (bf16[256,1024]{1,0:T(8,128)(2,1)S(1)}, bf16[256,1024]{1,0:T(8,128)(2,1)S(1)}, u32[]{:S(2)}, u32[]{:S(2)}) collective-permute-start(bf16[256,1024]{1,0:T(8,128)(2,1)S(1)} %expert.1.own_ref), channel_id=1, source_target_pairs={{0,1},{1,0},{2,3},{3,2},{4,5},{5,4},{6,7},{7,6},{8,9},{9,8},{10,11... | collective-permute-start | bytes 1572872 | tf_op jit(solution)/shard_map/ppermute | solution.py:627
  57.7 9.1 %collective-permute-start.15 = (bf16[128,1024]{1,0:T(8,128)(2,1)S(1)}, bf16[128,1024]{1,0:T(8,128)(2,1)S(1)}, u32[]{:S(2)}, u32[]{:S(2)}) collective-permute-start(bf16[128,1024]{1,0:T(8,128)(2,1)S(1)} %get-tuple-element.47), channel_id=1, source_target_pairs={{0,6},{1,7},{2,0},{3,1},{4,2},{5,3},{6,4},{7,5},{8,14},{9,15},{10,... | collective-permute-start | bytes 786440 | tf_op jit(solution)/shard_map/ppermute | solution.py:566
  60.0 16.8 %collective-permute-start.17 = (bf16[128,1024]{1,0:T(8,128)(2,1)S(1)}, bf16[128,1024]{1,0:T(8,128)(2,1)S(1)}, u32[]{:S(2)}, u32[]{:S(2)}) collective-permute-start(bf16[128,1024]{1,0:T(8,128)(2,1)S(1)} %get-tuple-element.49), channel_id=1, source_target_pairs={{0,10},{1,11},{2,12},{3,13},{4,14},{5,15},{6,8},{7,9},{8,18},{9,19... | collective-permute-start | bytes 786440 | tf_op jit(solution)/shard_map/ppermute | solution.py:625
  60.9 18.6 %collective-permute-start.18 = (bf16[128,1024]{1,0:T(8,128)(2,1)S(1)}, bf16[128,1024]{1,0:T(8,128)(2,1)S(1)}, u32[]{:S(2)}, u32[]{:S(2)}) collective-permute-start(bf16[128,1024]{1,0:T(8,128)(2,1)S(1)} %get-tuple-element.50), channel_id=1, source_target_pairs={{0,8},{1,9},{2,10},{3,11},{4,12},{5,13},{6,14},{7,15},{8,16},{9,17... | collective-permute-start | bytes 786440 | tf_op jit(solution)/shard_map/ppermute | solution.py:625
  66.8 15.1 %collective-permute-start.16 = (bf16[128,1024]{1,0:T(8,128)(2,1)S(1)}, bf16[128,1024]{1,0:T(8,128)(2,1)S(1)}, u32[]{:S(2)}, u32[]{:S(2)}) collective-permute-start(bf16[128,1024]{1,0:T(8,128)(2,1)S(1)} %add.34), channel_id=1, source_target_pairs={{0,14},{1,15},{2,8},{3,9},{4,10},{5,11},{6,12},{7,13},{8,22},{9,23... | collective-permute-start | bytes 786440 | tf_op jit(solution)/shard_map/ppermute | solution.py:625
  (1 other events, 0.7 us)
